TPU v7x, 32 devices: a whole 2x2x4 slice. The times are simulated.
32 devices in a mesh: nodes: 8 (over y, x, core), tp: 4 (over z).
Axes of the slice: x: 2, y: 2, z: 4, core: 2. Of those that a mesh axis runs over, the one named last changes fastest.
Arguments:
- tokens: bfloat16 [32768, 512], P(('nodes', 'tp')), may hold values from -6 to 6
- hop_mask: int32 [32768], P(('nodes', 'tp')), may hold values from 0 to 1, as said below
- graph_ids: int32 [4096], P(('nodes', 'tp')), may hold values from 0 to 63
- norm1_gain: bfloat16 [512], replicated, may hold values from 0.5 to 1.5
- norm1_shift: bfloat16 [512], replicated, may hold values from -2 to 2
- w_query: bfloat16 [512, 512], P(None, 'tp'), may hold values from -0.25 to 0.25
- w_key: bfloat16 [512, 512], P(None, 'tp'), may hold values from -0.25 to 0.25
- w_value: bfloat16 [512, 512], P(None, 'tp'), may hold values from -0.25 to 0.25
- w_out: bfloat16 [512, 512], P('tp'), may hold values from -0.5 to 0.5
- norm2_gain: bfloat16 [512], replicated, may hold values from 0.5 to 1.5
- norm2_shift: bfloat16 [512], replicated, may hold values from -2 to 2
- w_up: bfloat16 [512, 1024], P(None, 'tp'), may hold values from -0.25 to 0.25
- w_down: bfloat16 [1024, 512], P('tp'), may hold values from -0.375 to 0.375
- hop_weight: bfloat16 [512], replicated, may hold values from -0.25 to 0.25
- cotangent: bfloat16 [4096, 512], P(('nodes', 'tp')), may hold values from -6 to 6
Outputs:
- readout: bfloat16 [4096, 512], P(('nodes', 'tp'))
- grad_tokens: bfloat16 [32768, 512], P(('nodes', 'tp'))
- grad_norm1_gain: float32 [512], replicated
- grad_norm1_shift: float32 [512], replicated
- grad_query: float32 [512, 512], P(None, 'tp')
- grad_key: float32 [512, 512], P(None, 'tp')
- grad_value: float32 [512, 512], P(None, 'tp')
- grad_out: float32 [512, 512], P('tp')
- grad_norm2_gain: float32 [512], replicated
- grad_norm2_shift: float32 [512], replicated
- grad_up: float32 [512, 1024], P(None, 'tp')
- grad_down: float32 [1024, 512], P('tp')
- grad_hop_weight: float32 [512], replicated
Inputs may be any that keep to these rules, and one draw needn't show every extreme that they name: `hop_mask`: hops 0 and 1 of every node are real tokens.
All inputs are finite; a program needn't handle non-finite values.
Results may differ from a plain program's by a relative error of at most 0.038.
Values may be sent and summed in bfloat16 or wider, within the bound.
A program may use at most 128 MiB of HBM per device.

v0:
```python
import jax
import jax.numpy as jnp
from jax import lax
from jax.sharding import PartitionSpec as P

HOPS = 8
HEAD = 64
GRAPHS = 64


EPSILON = 1e-05
NEGATIVE = -1000000000.0
HIGHEST = lax.Precision.HIGHEST


def norm_rows(values, gains, shifts):
    centre = values - jnp.mean(values, axis=-1, keepdims=True)
    spread = jnp.mean(centre * centre, axis=-1, keepdims=True)
    return centre * lax.rsqrt(spread + EPSILON) * gains + shifts


def masked_scores(query_four, key_four, allowed, scale):
    scores = (
        jnp.einsum("nqhe,nkhe->hqkn", query_four, key_four, preferred_element_type=jnp.float32)
        * scale
    )
    return jnp.where(allowed, scores, NEGATIVE)


def exact_gelu(values):
    return jax.nn.gelu(values, approximate=False)


def shards(
    tokens,
    hop_mask,
    graph_ids,
    norm1_gain,
    norm1_shift,
    w_query,
    w_key,
    w_value,
    w_out,
    norm2_gain,
    norm2_shift,
    w_up,
    w_down,
    hop_weight,
    cotangent,
):
    rows_here = tokens.shape[0]
    width = tokens.shape[1]
    nodes_here = rows_here // HOPS
    scale = HEAD ** (-0.5)
    query_w, key_w, value_w, up_w = (w_query, w_key, w_value, w_up)
    out_w, down_w = (w_out, w_down)
    group_rows = rows_here * lax.axis_size("tp")
    node_group = group_rows // HOPS
    heads_here = query_w.shape[1] // HEAD
    shape_four = (node_group, HOPS, heads_here, HEAD)
    tokens_f = tokens.astype(jnp.float32)
    gain_one = norm1_gain.astype(jnp.float32)
    shift_one = norm1_shift.astype(jnp.float32)
    gain_two = norm2_gain.astype(jnp.float32)
    shift_two = norm2_shift.astype(jnp.float32)
    hop_vector = hop_weight.astype(jnp.float32)
    normed_one = norm_rows(tokens_f, gain_one, shift_one).astype(jnp.bfloat16)
    gathered_one, group_mask = (
        lax.all_gather(normed_one, "tp", axis=0, tiled=True),
        lax.all_gather(hop_mask.astype(jnp.bfloat16), "tp", axis=0, tiled=True),
    )
    allowed = (group_mask.reshape(node_group, HOPS).T > 0.5)[None, None]
    queries = jnp.dot(gathered_one, query_w, preferred_element_type=jnp.float32).astype(
        jnp.bfloat16
    )
    keys_all = jnp.dot(gathered_one, key_w, preferred_element_type=jnp.float32).astype(jnp.bfloat16)
    values_all = jnp.dot(gathered_one, value_w, preferred_element_type=jnp.float32).astype(
        jnp.bfloat16
    )
    query_four = queries.reshape(shape_four)
    key_four = keys_all.reshape(shape_four)
    value_four = values_all.reshape(shape_four)
    scores = masked_scores(query_four, key_four, allowed, scale)
    peak = jnp.max(scores, axis=2, keepdims=True)
    log_total = peak + jnp.log(jnp.sum(jnp.exp(scores - peak), axis=2, keepdims=True))
    probs = jnp.exp(scores - log_total)
    context = jnp.einsum(
        "hqkn,nkhe->nqhe",
        probs.astype(jnp.bfloat16),
        value_four,
        preferred_element_type=jnp.float32,
    )
    context = context.astype(jnp.bfloat16).reshape(group_rows, heads_here * HEAD)
    piece = context
    attended = lax.psum_scatter(
        jnp.dot(piece, out_w, preferred_element_type=jnp.float32).astype(jnp.bfloat16),
        "tp",
        scatter_dimension=0,
        tiled=True,
    ).astype(jnp.float32)
    residual_one = tokens_f + attended
    normed_two = norm_rows(residual_one, gain_two, shift_two).astype(jnp.bfloat16)
    gathered_two = lax.all_gather(normed_two, "tp", axis=0, tiled=True)
    before = jnp.dot(gathered_two, up_w, preferred_element_type=jnp.float32)
    activated = exact_gelu(before).astype(jnp.bfloat16)
    piece = activated
    branch = lax.psum_scatter(
        jnp.dot(piece, down_w, preferred_element_type=jnp.float32).astype(jnp.bfloat16),
        "tp",
        scatter_dimension=0,
        tiled=True,
    ).astype(jnp.float32)
    layer_out = residual_one + branch
    per_node = layer_out.reshape(nodes_here, HOPS, width)
    first = per_node[:, 0]
    rest = per_node[:, 1:]
    valid = hop_mask.reshape(nodes_here, HOPS)[:, 1:].astype(jnp.float32)
    logits = jnp.einsum("nkd,d->nk", rest, hop_vector, precision=HIGHEST)
    logits = jnp.where(valid > 0.5, logits, NEGATIVE)
    weights = jax.nn.softmax(logits, axis=1)
    member = (graph_ids[:, None] == jnp.arange(GRAPHS, dtype=jnp.int32)[None, :]).astype(
        jnp.float32
    )
    sums, counts = lax.psum(
        (jnp.dot(member.T, weights, precision=HIGHEST), jnp.sum(member, axis=0)), ("nodes", "tp")
    )
    denom = (counts + 1.0)[:, None]
    means = sums / denom
    coef = valid * (weights - jnp.dot(member, means, precision=HIGHEST))
    readout = (first + jnp.einsum("nk,nkd->nd", coef, rest, precision=HIGHEST)).astype(jnp.bfloat16)
    grad_read = cotangent.astype(jnp.float32)
    grad_coef = jnp.einsum("nd,nkd->nk", grad_read, rest, precision=HIGHEST)
    grad_rest = coef[:, :, None] * grad_read[:, None, :]
    direct = valid * grad_coef
    grad_means = lax.psum(-jnp.dot(member.T, direct, precision=HIGHEST), ("nodes", "tp"))
    grad_weights = direct + jnp.dot(member, grad_means / denom, precision=HIGHEST)
    grad_logits = weights * (grad_weights - jnp.sum(weights * grad_weights, axis=1, keepdims=True))
    grad_rest = grad_rest + grad_logits[:, :, None] * hop_vector[None, None, :]
    grad_hop = jnp.einsum("nk,nkd->d", grad_logits, rest, precision=HIGHEST)
    grad_layer = jnp.concatenate([grad_read[:, None, :], grad_rest], axis=1).reshape(
        rows_here, width
    )
    grad_branch = lax.all_gather(grad_layer.astype(jnp.bfloat16), "tp", axis=0, tiled=True)
    grad_activated = jnp.einsum(
        "rd,fd->rf", grad_branch, down_w, preferred_element_type=jnp.float32
    )
    grad_down = jnp.einsum("rf,rd->fd", activated, grad_branch, preferred_element_type=jnp.float32)
    gelu_pull = jax.vjp(exact_gelu, before)[1]
    grad_before = gelu_pull(grad_activated)[0].astype(jnp.bfloat16)
    grad_up = jnp.einsum("rd,rf->df", gathered_two, grad_before, preferred_element_type=jnp.float32)
    piece = grad_before
    grad_normed_two = lax.psum_scatter(
        jnp.einsum("rf,df->rd", piece, up_w, preferred_element_type=jnp.float32).astype(
            jnp.bfloat16
        ),
        "tp",
        scatter_dimension=0,
        tiled=True,
    ).astype(jnp.float32)
    norm_two_pull = jax.vjp(norm_rows, residual_one, gain_two, shift_two)[1]
    back_two, grad_gain_two, grad_shift_two = norm_two_pull(grad_normed_two)
    grad_residual = grad_layer + back_two
    grad_attended = lax.all_gather(grad_residual.astype(jnp.bfloat16), "tp", axis=0, tiled=True)
    grad_context = jnp.einsum(
        "rd,cd->rc", grad_attended, out_w, preferred_element_type=jnp.float32
    ).astype(jnp.bfloat16)
    grad_outw = jnp.einsum("rc,rd->cd", context, grad_attended, preferred_element_type=jnp.float32)
    context_four = grad_context.reshape(shape_four)
    again_scores = masked_scores(query_four, key_four, allowed, scale)
    probs_again = jnp.exp(again_scores - log_total)
    grad_values = jnp.einsum(
        "hqkn,nqhe->nkhe",
        probs_again.astype(jnp.bfloat16),
        context_four,
        preferred_element_type=jnp.float32,
    ).astype(jnp.bfloat16)
    grad_probs = jnp.einsum(
        "nqhe,nkhe->hqkn", context_four, value_four, preferred_element_type=jnp.float32
    )
    grad_scores = probs_again * (
        grad_probs - jnp.sum(probs_again * grad_probs, axis=2, keepdims=True)
    )
    grad_scores = grad_scores.astype(jnp.bfloat16)
    grad_queries = (
        jnp.einsum("hqkn,nkhe->nqhe", grad_scores, key_four, preferred_element_type=jnp.float32)
        * scale
    ).astype(jnp.bfloat16)
    grad_keys = (
        jnp.einsum("hqkn,nqhe->nkhe", grad_scores, query_four, preferred_element_type=jnp.float32)
        * scale
    ).astype(jnp.bfloat16)
    flat_queries = grad_queries.reshape(group_rows, heads_here * HEAD)
    flat_keys = grad_keys.reshape(group_rows, heads_here * HEAD)
    flat_values = grad_values.reshape(group_rows, heads_here * HEAD)
    grad_qw = jnp.einsum(
        "rd,rc->dc", gathered_one, flat_queries, preferred_element_type=jnp.float32
    )
    grad_kw = jnp.einsum("rd,rc->dc", gathered_one, flat_keys, preferred_element_type=jnp.float32)
    grad_vw = jnp.einsum("rd,rc->dc", gathered_one, flat_values, preferred_element_type=jnp.float32)
    total = jnp.einsum("rc,dc->rd", flat_queries, query_w, preferred_element_type=jnp.float32)
    total = total + jnp.einsum("rc,dc->rd", flat_keys, key_w, preferred_element_type=jnp.float32)
    grad_normed_one = lax.psum_scatter(
        (
            total
            + jnp.einsum("rc,dc->rd", flat_values, value_w, preferred_element_type=jnp.float32)
        ).astype(jnp.bfloat16),
        "tp",
        scatter_dimension=0,
        tiled=True,
    ).astype(jnp.float32)
    norm_one_pull = jax.vjp(norm_rows, tokens_f, gain_one, shift_one)[1]
    back_one, grad_gain_one, grad_shift_one = norm_one_pull(grad_normed_one)
    grad_tokens = (grad_residual + back_one).astype(jnp.bfloat16)
    sum_q, sum_k, sum_v, sum_o, sum_up, sum_down = lax.psum(
        (grad_qw, grad_kw, grad_vw, grad_outw, grad_up, grad_down), "nodes"
    )
    sum_g1, sum_s1, sum_g2, sum_s2, sum_hop = lax.psum(
        (grad_gain_one, grad_shift_one, grad_gain_two, grad_shift_two, grad_hop), ("nodes", "tp")
    )
    return (
        readout,
        grad_tokens,
        sum_g1,
        sum_s1,
        sum_q,
        sum_k,
        sum_v,
        sum_o,
        sum_g2,
        sum_s2,
        sum_up,
        sum_down,
        sum_hop,
    )


def solution(mesh):
    return jax.shard_map(
        shards,
        mesh=mesh,
        in_specs=(
            P(("nodes", "tp"), None),
            P(("nodes", "tp")),
            P(("nodes", "tp")),
            P(),
            P(),
            P(None, "tp"),
            P(None, "tp"),
            P(None, "tp"),
            P("tp", None),
            P(),
            P(),
            P(None, "tp"),
            P("tp", None),
            P(),
            P(("nodes", "tp"), None),
        ),
        out_specs=(
            P(("nodes", "tp"), None),
            P(("nodes", "tp"), None),
            P(),
            P(),
            P(None, "tp"),
            P(None, "tp"),
            P(None, "tp"),
            P("tp", None),
            P(),
            P(),
            P(None, "tp"),
            P("tp", None),
            P(),
        ),
        check_vma=False,
    )
```

profile of v0, /device:TPU:0, one launch (start us, length us, event | category | flops | bytes accessed | tf_op | source)
XLA Modules:
  0.0 924.0 jit_solution(6074492153965677261)
XLA Ops:
  13.5 13.5 %all_gather.16 = bf16[4096]{0:T(1024)(128)(2,1)S(1)} all-gather(bf16[1024]{0:T(1024)(128)(2,1)S(1)} %convert_element_type.126), channel_id=1, replica_groups=mesh['nodes'=8,'tp'=4] {'tp'}, dimensions={0}, use_global_device_ids=true | all-gather | bytes 10240 | tf_op jit(solution)/shard_map/all_gather | solution.py:70
  27.3 69.7 %all-gather.5.cloned.1.call-done = bf16[4096,512]{1,0:T(8,128)(2,1)} async-done(((bf16[1024,512]{1,0:T(8,128)(2,1)}), bf16[4096,512]{1,0:T(8,128)(2,1)}) %all-gather.5.cloned.1.call-update) | async-done | bytes 4194320 | tf_op jit(solution)/shard_map/all_gather | solution.py:69
  113.2 5.5 fusion.31
  131.5 3.9 reshape.149
  139.4 74.8 %reduce-scatter.5.cloned.1.call-done = bf16[1024,512]{1,0:T(8,128)(2,1)} async-done(((bf16[4096,512]{1,0:T(8,128)(2,1)}), bf16[1024,512]{1,0:T(8,128)(2,1)}) %reduce-scatter.5.cloned.1.call-update) | async-done | bytes 1048592 | tf_op jit(solution)/shard_map/reduce_scatter | solution.py:95
  218.6 81.4 %all-gather.7.cloned.1.call-done = bf16[4096,512]{1,0:T(8,128)(2,1)} async-done(((bf16[1024,512]{1,0:T(8,128)(2,1)}), bf16[4096,512]{1,0:T(8,128)(2,1)}) %all-gather.7.cloned.1.call-update) | async-done | bytes 4194320 | tf_op jit(solution)/shard_map/all_gather | solution.py:103
  300.0 12.5 %multiply_convert_fusion.2 = (bf16[4096,256]{1,0:T(8,128)(2,1)S(1)}, f32[4096,256]{1,0:T(8,128)}, f32[4096,256]{1,0:T(8,128)}) fusion(bf16[4096,512]{1,0:T(8,128)(2,1)} %all-gather.7.cloned.1.call-done, bf16[512,256]{1,0:T(8,128)(2,1)S(1)} %copy-done), kind=kOutput, calls=%fused_computation.14 | convolution fusion | flops 1141899264 | bytes 14942208 | tf_op jit(solution)/shard_map/dot_general | solution.py:104
  319.1 73.5 %reduce-scatter.7.cloned.1.call-done = bf16[1024,512]{1,0:T(8,128)(2,1)} async-done(((bf16[4096,512]{1,0:T(8,128)(2,1)}), bf16[1024,512]{1,0:T(8,128)(2,1)}) %reduce-scatter.7.cloned.1.call-update) | async-done | bytes 1048592 | tf_op jit(solution)/shard_map/reduce_scatter | solution.py:107
  402.5 41.5 %all-reduce.1 = (f32[64,7]{0,1:T(8,128)S(1)}, f32[64]{0:T(128)S(1)}, f32[64,7]{0,1:T(8,128)S(1)}) all-reduce(f32[64,7]{0,1:T(8,128)S(1)} %fusion.67, f32[64]{0:T(128)S(1)} %convert_reduce_fusion.3, f32[64,7]{0,1:T(8,128)S(1)} %convolution_negate_fusion), channel_id=1, replica_groups=mesh['nodes'=8,'tp'=4] {'nodes','tp'}, use_global_device_ids=true, to_apply=%region_10.11 | all-reduce | flops 960 | bytes 7680 | tf_op jit(solution)/shard_map/psum | solution.py:124
  449.1 80.7 %all-gather.9.cloned.1.call-done = bf16[4096,512]{1,0:T(8,128)(2,1)} async-done(((bf16[1024,512]{1,0:T(8,128)(2,1)}), bf16[4096,512]{1,0:T(8,128)(2,1)}) %all-gather.9.cloned.1.call-update) | async-done | bytes 4194320 | tf_op jit(solution)/shard_map/all_gather | solution.py:143
  529.8 6.7 add_convert_fusion.1
  541.1 75.4 %reduce-scatter.9.cloned.1.call-done = bf16[1024,512]{1,0:T(8,128)(2,1)} async-done(((bf16[4096,512]{1,0:T(8,128)(2,1)}), bf16[1024,512]{1,0:T(8,128)(2,1)}) %reduce-scatter.9.cloned.1.call-update) | async-done | bytes 1048592 | tf_op jit(solution)/shard_map/reduce_scatter | solution.py:152
  624.0 81.2 %all-gather.11.cloned.1.call-done = bf16[4096,512]{1,0:T(8,128)(2,1)} async-done(((bf16[1024,512]{1,0:T(8,128)(2,1)}), bf16[4096,512]{1,0:T(8,128)(2,1)}) %all-gather.11.cloned.1.call-update) | async-done | bytes 4194320 | tf_op jit(solution)/shard_map/all_gather | solution.py:163
  710.4 5.0 convert_bitcast_fusion
  724.5 4.4 fusion.40
  735.0 4.9 reshape.156
  739.9 5.1 copy.127
  749.0 5.5 copy.124
  754.4 4.8 reshape.154
  772.2 4.4 fusion.97
  787.9 52.5 %reduce-scatter.11.cloned.1.call-done = bf16[1024,512]{1,0:T(8,128)(2,1)} async-done(((bf16[4096,512]{1,0:T(8,128)(2,1)}), bf16[1024,512]{1,0:T(8,128)(2,1)}) %reduce-scatter.11.cloned.1.call-update) | async-done | bytes 1048592 | tf_op jit(solution)/shard_map/reduce_scatter | solution.py:202
  844.3 41.0 %all-reduce = (f32[512]{0:T(512)}, f32[512]{0:T(512)}, f32[512]{0:T(512)}, f32[512]{0:T(512)}, f32[512]{0:T(512)}) all-reduce(f32[512]{0:T(512)S(1)} %get-tuple-element.15, f32[512]{0:T(512)S(1)} %get-tuple-element.19, f32[512]{0:T(512)S(1)} %copy-done.66, f32[512]{0:T(512)S(1)} %copy-done.65, ...), channel_id=1, replica_groups=mesh['nodes'=8,'tp'=4] {'nodes','tp'}, use_global_device_ids=true, to_apply=%region_23.24 | all-reduce | flops 2560 | bytes 20480 | tf_op jit(solution)/shard_map/psum | solution.py:217
  885.3 4.7 add_convert_fusion.2
  890.0 18.9 %all-reduce.5.cloned.1.call-done = (f32[512,128]{1,0:T(8,128)}, f32[512,128]{1,0:T(8,128)}, f32[512,128]{1,0:T(8,128)}, f32[128,512]{1,0:T(8,128)}, f32[512,256]{1,0:T(8,128)}, /*index=5*/f32[256,512]{1,0:T(8,128)}) async-done(((f32[512,128]{1,0:T(8,128)}, f32[512,128]{1,0:T(8,128)}, f32[512,128]{1,0:T(8,128)}, f32[128,512]{1,0:T(8,128)}, f32[512,256]{1,0:T(8,128)}, /*index=5*/f32[256,512]{1,0:T(8,128)}), ...) | async-done | bytes 2097168 | tf_op jit(solution)/shard_map/psum | solution.py:214
  (262 shorter events, 137.8 us)
Async XLA Ops:
  7.2 292.8 %copy-start = (bf16[512,256]{1,0:T(8,128)(2,1)S(1)}, bf16[512,256]{1,0:T(8,128)(2,1)}, u32[]{:S(2)}) copy-start(bf16[512,256]{1,0:T(8,128)(2,1)} %param.26) | copy-start | bytes 786436
  7.2 89.8 %all-gather.5.cloned.1.call-start = ((), (), s32[]{:S(2)}) async-start(), calls=%async_computation.4 | async-start | bytes 5242880 | tf_op jit(solution)/shard_map/all_gather | solution.py:69
  10.2 86.8 %copy-start.35 = (bf16[512,128]{1,0:T(8,128)(2,1)S(1)}, bf16[512,128]{1,0:T(8,128)(2,1)}, u32[]{:S(2)}) copy-start(bf16[512,128]{1,0:T(8,128)(2,1)} %param.20) | copy-start | bytes 393220
  13.4 200.8 %reduce-scatter.5.cloned.1.call-start = ((), (), s32[]{:S(2)}) async-start(), calls=%async_computation.5 | async-start | bytes 5242880 | tf_op jit(solution)/shard_map/reduce_scatter | solution.py:95
  27.3 94.5 %copy-start.50 = (pred[8,512]{1,0:T(8,128)(4,1)}, pred[8,512]{1,0:T(8,128)(4,1)S(1)}, u32[]{:S(2)}) copy-start(pred[8,512]{1,0:T(8,128)(4,1)S(1)} %copy.107) | copy-start | bytes 12292
  138.7 161.3 %all-gather.7.cloned.1.call-start = ((), (), s32[]{:S(2)}) async-start(), calls=%async_computation.6 | async-start | bytes 5242880 | tf_op jit(solution)/shard_map/all_gather | solution.py:103
  218.6 95.3 %copy-start.41 = (bf16[256,512]{1,0:T(8,128)(2,1)S(1)}, bf16[256,512]{1,0:T(8,128)(2,1)}, u32[]{:S(2)}) copy-start(bf16[256,512]{1,0:T(8,128)(2,1)} %param.27) | copy-start | bytes 786436
  218.6 174.1 %reduce-scatter.7.cloned.1.call-start = ((), (), s32[]{:S(2)}) async-start(), calls=%async_computation.7 | async-start | bytes 5242880 | tf_op jit(solution)/shard_map/reduce_scatter | solution.py:107
  317.2 212.6 %all-gather.9.cloned.1.call-start = ((), (), s32[]{:S(2)}) async-start(), calls=%async_computation.8 | async-start | bytes 5242880 | tf_op jit(solution)/shard_map/all_gather | solution.py:143
  319.0 302.5 %copy-start.31 = (f32[128,1,512]{2,1,0:T(1,128)}, f32[128,1,512]{2,1,0:T(1,128)S(1)}, u32[]{:S(2)}) copy-start(f32[128,1,512]{2,1,0:T(1,128)S(1)} %copy.118) | copy-start | bytes 786436
  447.5 82.2 %copy-start.42 = (bf16[256,512]{1,0:T(8,128)(2,1)S(1)}, bf16[256,512]{1,0:T(8,128)(2,1)}, u32[]{:S(2)}) copy-start(bf16[256,512]{1,0:T(8,128)(2,1)} %param.27) | copy-start | bytes 786436
  449.0 167.4 %reduce-scatter.9.cloned.1.call-start = ((), (), s32[]{:S(2)}) async-start(), calls=%async_computation.9 | async-start | bytes 5242880 | tf_op jit(solution)/shard_map/reduce_scatter | solution.py:152
  541.0 78.3 %copy-start.59 = (f32[1024]{0:T(1024)S(1)}, f32[1024]{0:T(1024)}, u32[]{:S(2)}) copy-start(f32[1024]{0:T(1024)} %copy-done.58) | copy-start | bytes 12292
  541.0 164.2 %all-gather.11.cloned.1.call-start = ((), (), s32[]{:S(2)}) async-start(), calls=%async_computation.10 | async-start | bytes 5242880 | tf_op jit(solution)/shard_map/all_gather | solution.py:163
  623.8 216.7 %reduce-scatter.11.cloned.1.call-start = ((), (), s32[]{:S(2)}) async-start(), calls=%async_computation.11 | async-start | bytes 5242880 | tf_op jit(solution)/shard_map/reduce_scatter | solution.py:202
  765.1 143.9 %all-reduce.5.cloned.1.call-start = ((), (), s32[]{:S(2)}) async-start(), calls=%async_computation.12 | async-start | bytes 4194304 | tf_op jit(solution)/shard_map/psum | solution.py:214
  787.8 52.6 %copy-start.53 = (f32[512]{0:T(512)S(1)}, f32[512]{0:T(512)}, u32[]{:S(2)}) copy-start(f32[512]{0:T(512)} %copy-done.52) | copy-start | bytes 6148
  787.8 54.8 %copy-start.57 = (f32[1024]{0:T(1024)S(1)}, f32[1024]{0:T(1024)}, u32[]{:S(2)}) copy-start(f32[1024]{0:T(1024)} %copy-done.56) | copy-start | bytes 12292
  787.8 54.8 %copy-start.49 = (f32[1024]{0:T(1024)S(1)}, f32[1024]{0:T(1024)}, u32[]{:S(2)}) copy-start(f32[1024]{0:T(1024)} %copy-done.48) | copy-start | bytes 12292
  787.9 56.4 %copy-start.65 = (f32[512]{0:T(512)S(1)}, f32[512]{0:T(512)}, u32[]{:S(2)}) copy-start(f32[512]{0:T(512)} %get-tuple-element.17) | copy-start | bytes 6148
  787.9 56.4 %copy-start.66 = (f32[512]{0:T(512)S(1)}, f32[512]{0:T(512)}, u32[]{:S(2)}) copy-start(f32[512]{0:T(512)} %get-tuple-element.13) | copy-start | bytes 6148
  787.9 97.4 %copy-start.13 = (bf16[1024,512]{1,0:T(8,128)(2,1)S(1)}, bf16[1024,512]{1,0:T(8,128)(2,1)}, u32[]{:S(2)}) copy-start(bf16[1024,512]{1,0:T(8,128)(2,1)} %reduce-scatter.9.cloned.1.call-done) | copy-start | bytes 3145732
  787.9 97.4 %copy-start.47 = (f32[1024]{0:T(1024)S(1)}, f32[1024]{0:T(1024)}, u32[]{:S(2)}) copy-start(f32[1024]{0:T(1024)} %copy-done.46) | copy-start | bytes 12292
  787.9 97.4 %copy-start.55 = (f32[1024]{0:T(1024)S(1)}, f32[1024]{0:T(1024)}, u32[]{:S(2)}) copy-start(f32[1024]{0:T(1024)} %copy-done.54) | copy-start | bytes 12292
  (58 other events, 204.6 us)
Sparse Core Ops, SparseCore 0:
  13.5 83.4 all-gather.4
  138.8 75.2 reduce-scatter.4
  218.7 81.2 all-gather.6
  317.3 75.2 reduce-scatter.6
  449.2 80.5 all-gather.8
  541.1 75.2 reduce-scatter.8
  623.9 81.2 all-gather.10
  765.2 75.2 reduce-scatter.10
  845.5 63.4 all-reduce.4
where the time goes:
time: 928 us; the launch traced here: 924 us
  waiting for transfers between devices  608 us (66%)
  matrix products  97.8 us (11%)
  blocking collectives  96 us (10%)
  local copies, waits for them, and re-layouts  74.2 us (8%)
  other arithmetic  31.6 us (3%)
  between operations  14.8 us (2%)
    all_gather x1, waiting for transfers between devices, shards(): gathered_two = lax.all_gather(normed_two, 'tp', axis=0, tiled=True)  81.4 us
    all_gather x1, waiting for transfers between devices, shards(): lax.all_gather(grad_residual.astype(jnp.bfloat16), 'tp', axis=0, tiled=True)  81.2 us
    all_gather x1, waiting for transfers between devices, shards(): lax.all_gather(grad_layer.astype(jnp.bfloat16), 'tp', axis=0, tiled=True)  80.7 us
    reduce_scatter x1, waiting for transfers between devices, shards(): lax.psum_scatter(jnp.einsum('rf,df->rd', piece, up_w, preferred_element_t...  75.4 us
    reduce_scatter x1, waiting for transfers between devices, shards(): lax.psum_scatter(jnp.dot(piece, out_w, preferred_element_type=jnp.float32...  74.8 us
    reduce_scatter x1, waiting for transfers between devices, shards(): lax.psum_scatter(jnp.dot(piece, down_w, preferred_element_type=jnp.float3...  73.5 us
    all_gather x1, waiting for transfers between devices, shards(): lax.all_gather(normed_one, 'tp', axis=0, tiled=True)  69.7 us
    reduce_scatter x1, waiting for transfers between devices, shards(): lax.psum_scatter((total + jnp.einsum('rc,dc->rd', flat_values, value_w, p...  52.5 us
  transfers between devices with their start and end apart: 9, of which 9 were waited for; matrix products, arithmetic and copies ran while one was open for 3% of the time, Pallas kernels for 0%

commit v1 on v0

--- a/solution.py
+++ b/solution.py
@@ -54,7 +54,20 @@
     scale = HEAD ** (-0.5)
     query_w, key_w, value_w, up_w = (w_query, w_key, w_value, w_up)
     out_w, down_w = (w_out, w_down)
-    group_rows = rows_here * lax.axis_size("tp")
+    tp = lax.axis_size("tp")
+    cols = w_query.shape[1]
+    ff_cols = w_up.shape[1]
+    qkv = lax.all_gather(jnp.concatenate([w_query, w_key, w_value, w_up], axis=1), "tp", axis=0)
+    outd = lax.all_gather(jnp.concatenate([w_out, w_down], axis=0), "tp", axis=0)
+
+    def wide(lo, n):
+        return jnp.transpose(qkv[:, :, lo : lo + n], (1, 0, 2)).reshape(width, tp * n)
+
+    query_w, key_w, value_w = (wide(0, cols), wide(cols, cols), wide(2 * cols, cols))
+    up_w = wide(3 * cols, ff_cols)
+    out_w = outd[:, :cols].reshape(tp * cols, width)
+    down_w = outd[:, cols:].reshape(tp * ff_cols, width)
+    group_rows = rows_here
     node_group = group_rows // HOPS
     heads_here = query_w.shape[1] // HEAD
     shape_four = (node_group, HOPS, heads_here, HEAD)
@@ -65,10 +78,7 @@
     shift_two = norm2_shift.astype(jnp.float32)
     hop_vector = hop_weight.astype(jnp.float32)
     normed_one = norm_rows(tokens_f, gain_one, shift_one).astype(jnp.bfloat16)
-    gathered_one, group_mask = (
-        lax.all_gather(normed_one, "tp", axis=0, tiled=True),
-        lax.all_gather(hop_mask.astype(jnp.bfloat16), "tp", axis=0, tiled=True),
-    )
+    gathered_one, group_mask = normed_one, hop_mask.astype(jnp.bfloat16)
     allowed = (group_mask.reshape(node_group, HOPS).T > 0.5)[None, None]
     queries = jnp.dot(gathered_one, query_w, preferred_element_type=jnp.float32).astype(
         jnp.bfloat16
@@ -92,24 +102,14 @@
     )
     context = context.astype(jnp.bfloat16).reshape(group_rows, heads_here * HEAD)
     piece = context
-    attended = lax.psum_scatter(
-        jnp.dot(piece, out_w, preferred_element_type=jnp.float32).astype(jnp.bfloat16),
-        "tp",
-        scatter_dimension=0,
-        tiled=True,
-    ).astype(jnp.float32)
+    attended = jnp.dot(piece, out_w, preferred_element_type=jnp.float32)
     residual_one = tokens_f + attended
     normed_two = norm_rows(residual_one, gain_two, shift_two).astype(jnp.bfloat16)
-    gathered_two = lax.all_gather(normed_two, "tp", axis=0, tiled=True)
+    gathered_two = normed_two
     before = jnp.dot(gathered_two, up_w, preferred_element_type=jnp.float32)
     activated = exact_gelu(before).astype(jnp.bfloat16)
     piece = activated
-    branch = lax.psum_scatter(
-        jnp.dot(piece, down_w, preferred_element_type=jnp.float32).astype(jnp.bfloat16),
-        "tp",
-        scatter_dimension=0,
-        tiled=True,
-    ).astype(jnp.float32)
+    branch = jnp.dot(piece, down_w, preferred_element_type=jnp.float32)
     layer_out = residual_one + branch
     per_node = layer_out.reshape(nodes_here, HOPS, width)
     first = per_node[:, 0]
@@ -121,18 +121,22 @@
     member = (graph_ids[:, None] == jnp.arange(GRAPHS, dtype=jnp.int32)[None, :]).astype(
         jnp.float32
     )
-    sums, counts = lax.psum(
-        (jnp.dot(member.T, weights, precision=HIGHEST), jnp.sum(member, axis=0)), ("nodes", "tp")
+    grad_read = cotangent.astype(jnp.float32)
+    grad_coef = jnp.einsum("nd,nkd->nk", grad_read, rest, precision=HIGHEST)
+    direct = valid * grad_coef
+    sums, counts, grad_means = lax.psum(
+        (
+            jnp.dot(member.T, weights, precision=HIGHEST),
+            jnp.sum(member, axis=0),
+            -jnp.dot(member.T, direct, precision=HIGHEST),
+        ),
+        ("nodes", "tp"),
     )
     denom = (counts + 1.0)[:, None]
     means = sums / denom
     coef = valid * (weights - jnp.dot(member, means, precision=HIGHEST))
     readout = (first + jnp.einsum("nk,nkd->nd", coef, rest, precision=HIGHEST)).astype(jnp.bfloat16)
-    grad_read = cotangent.astype(jnp.float32)
-    grad_coef = jnp.einsum("nd,nkd->nk", grad_read, rest, precision=HIGHEST)
     grad_rest = coef[:, :, None] * grad_read[:, None, :]
-    direct = valid * grad_coef
-    grad_means = lax.psum(-jnp.dot(member.T, direct, precision=HIGHEST), ("nodes", "tp"))
     grad_weights = direct + jnp.dot(member, grad_means / denom, precision=HIGHEST)
     grad_logits = weights * (grad_weights - jnp.sum(weights * grad_weights, axis=1, keepdims=True))
     grad_rest = grad_rest + grad_logits[:, :, None] * hop_vector[None, None, :]
@@ -140,7 +144,7 @@
     grad_layer = jnp.concatenate([grad_read[:, None, :], grad_rest], axis=1).reshape(
         rows_here, width
     )
-    grad_branch = lax.all_gather(grad_layer.astype(jnp.bfloat16), "tp", axis=0, tiled=True)
+    grad_branch = grad_layer.astype(jnp.bfloat16)
     grad_activated = jnp.einsum(
         "rd,fd->rf", grad_branch, down_w, preferred_element_type=jnp.float32
     )
@@ -149,18 +153,11 @@
     grad_before = gelu_pull(grad_activated)[0].astype(jnp.bfloat16)
     grad_up = jnp.einsum("rd,rf->df", gathered_two, grad_before, preferred_element_type=jnp.float32)
     piece = grad_before
-    grad_normed_two = lax.psum_scatter(
-        jnp.einsum("rf,df->rd", piece, up_w, preferred_element_type=jnp.float32).astype(
-            jnp.bfloat16
-        ),
-        "tp",
-        scatter_dimension=0,
-        tiled=True,
-    ).astype(jnp.float32)
+    grad_normed_two = jnp.einsum("rf,df->rd", piece, up_w, preferred_element_type=jnp.float32)
     norm_two_pull = jax.vjp(norm_rows, residual_one, gain_two, shift_two)[1]
     back_two, grad_gain_two, grad_shift_two = norm_two_pull(grad_normed_two)
     grad_residual = grad_layer + back_two
-    grad_attended = lax.all_gather(grad_residual.astype(jnp.bfloat16), "tp", axis=0, tiled=True)
+    grad_attended = grad_residual.astype(jnp.bfloat16)
     grad_context = jnp.einsum(
         "rd,cd->rc", grad_attended, out_w, preferred_element_type=jnp.float32
     ).astype(jnp.bfloat16)
@@ -199,21 +196,36 @@
     grad_vw = jnp.einsum("rd,rc->dc", gathered_one, flat_values, preferred_element_type=jnp.float32)
     total = jnp.einsum("rc,dc->rd", flat_queries, query_w, preferred_element_type=jnp.float32)
     total = total + jnp.einsum("rc,dc->rd", flat_keys, key_w, preferred_element_type=jnp.float32)
-    grad_normed_one = lax.psum_scatter(
-        (
-            total
-            + jnp.einsum("rc,dc->rd", flat_values, value_w, preferred_element_type=jnp.float32)
-        ).astype(jnp.bfloat16),
-        "tp",
-        scatter_dimension=0,
-        tiled=True,
-    ).astype(jnp.float32)
+    grad_normed_one = total + jnp.einsum(
+        "rc,dc->rd", flat_values, value_w, preferred_element_type=jnp.float32
+    )
     norm_one_pull = jax.vjp(norm_rows, tokens_f, gain_one, shift_one)[1]
     back_one, grad_gain_one, grad_shift_one = norm_one_pull(grad_normed_one)
     grad_tokens = (grad_residual + back_one).astype(jnp.bfloat16)
-    sum_q, sum_k, sum_v, sum_o, sum_up, sum_down = lax.psum(
-        (grad_qw, grad_kw, grad_vw, grad_outw, grad_up, grad_down), "nodes"
-    )
+    def lead(grad, n):
+        return jnp.transpose(grad.reshape(width, tp, n), (1, 0, 2)).astype(jnp.bfloat16)
+
+    left = jnp.concatenate(
+        [lead(grad_qw, cols), lead(grad_kw, cols), lead(grad_vw, cols), lead(grad_up, ff_cols)], axis=2
+    )
+    right = jnp.concatenate(
+        [
+            grad_outw.reshape(tp, cols, width).astype(jnp.bfloat16),
+            grad_down.reshape(tp, ff_cols, width).astype(jnp.bfloat16),
+        ],
+        axis=1,
+    )
+    left, right = lax.psum(
+        (
+            lax.psum_scatter(left, "tp", scatter_dimension=0, tiled=True)[0],
+            lax.psum_scatter(right, "tp", scatter_dimension=0, tiled=True)[0],
+        ),
+        "nodes",
+    )
+    left, right = left.astype(jnp.float32), right.astype(jnp.float32)
+    sum_q, sum_k, sum_v = (left[:, :cols], left[:, cols : 2 * cols], left[:, 2 * cols : 3 * cols])
+    sum_up = left[:, 3 * cols :]
+    sum_o, sum_down = right[:cols], right[cols:]
     sum_g1, sum_s1, sum_g2, sum_s2, sum_hop = lax.psum(
         (grad_gain_one, grad_shift_one, grad_gain_two, grad_shift_two, grad_hop), ("nodes", "tp")
     )

time: 928 us -> 502 us (0.54)
  waiting for transfers between devices: 608 us -> 138 us
  local copies, waits for them, and re-layouts: 74.2 us -> 125 us
  other arithmetic: 31.6 us -> 57 us
  matrix products: 97.8 us -> 78.9 us
  blocking collectives: 96 us -> 82.5 us
    reduce_scatter x4 -> x2, waiting for transfers between devices: 276 us -> 0.01 us  [the longest x1 0.01 us: shards(): lax.psum_scatter(right, 'tp', scatter_dimension=0, tiled=True)[0]]
    all_gather x4 -> x2, waiting for transfers between devices: 313 us -> 84.5 us  [the longest x1 51.7 us: shards(): lax.all_gather(jnp.concatenate([w_query, w_key, w_value, w_up], axis=1),...]
    psum x1, waiting for transfers between devices: 18.9 us -> 53.7 us  [shards(): lax.psum((lax.psum_scatter(left, 'tp', scatter_dimension=0, tiled=True)[0...]
    another operation x0 -> x4, local copies, waits for them, and re-layouts: none -> 20 us  [exact_gelu(): return jax.nn.gelu(values, approximate=False)]
    another operation x0 -> x2, other arithmetic: none -> 14.4 us  [exact_gelu(): return jax.nn.gelu(values, approximate=False)]
    all_gather x1 -> x0, blocking collectives: 13.5 us -> none  [shards(): lax.all_gather(hop_mask.astype(jnp.bfloat16), 'tp', axis=0, tiled=True)]
    dot_general x1, matrix products: 12.5 us -> 1.44 us  [shards(): before = jnp.dot(gathered_two, up_w, preferred_element_type=jnp.float32)]
    slice x0 -> x6, local copies, waits for them, and re-layouts: none -> 10.3 us  [the longest x2 3.5 us: shards(): sum_o, sum_down = (right[:cols], right[cols:])]
  transfers between devices with their start and end apart: 9 -> 5, of which waited for: 9 -> 3; matrix products, arithmetic and copies ran while one was open for 3% -> 20% of each run, Pallas kernels for 0% -> 0%
where the time goes in v1:
time: 502 us; the launch traced here: 497 us
  waiting for transfers between devices  138 us (27%)
  local copies, waits for them, and re-layouts  125 us (25%)
  blocking collectives  82.5 us (16%)
  matrix products  78.9 us (16%)
  other arithmetic  57 us (11%)
  between operations  14.8 us (3%)
    psum x1, waiting for transfers between devices, shards(): lax.psum((lax.psum_scatter(left, 'tp', scatter_dimension=0, tiled=True)[0...  53.7 us
    all_gather x1, waiting for transfers between devices, shards(): lax.all_gather(jnp.concatenate([w_query, w_key, w_value, w_up], axis=1),...  51.7 us
    psum x1, blocking collectives, shards(): lax.psum((grad_gain_one, grad_shift_one, grad_gain_two, grad_shift_two, g...  42.9 us
    psum x1, blocking collectives, shards(): lax.psum((jnp.dot(member.T, weights, precision=HIGHEST), jnp.sum(member,...  39.6 us
    all_gather x1, waiting for transfers between devices, shards(): lax.all_gather(jnp.concatenate([w_out, w_down], axis=0), 'tp', axis=0)  32.7 us
    another operation x4, local copies, waits for them, and re-layouts, exact_gelu(): return jax.nn.gelu(values, approximate=False)  20 us
    another operation x2, other arithmetic, exact_gelu(): return jax.nn.gelu(values, approximate=False)  14.4 us
  transfers between devices with their start and end apart: 5, of which 3 were waited for; matrix products, arithmetic and copies ran while one was open for 20% of the time, Pallas kernels for 0%

profile of v1, /device:TPU:0, one launch (start us, length us, event | category | flops | bytes accessed | tf_op | source)
XLA Modules:
  0.0 497.2 jit_solution(13761124633650814749)
XLA Ops:
  17.3 32.7 %all-gather.7.cloned.1.call-done = bf16[1536,512]{1,0:T(8,128)(2,1)} async-done(((bf16[384,512]{1,0:T(8,128)(2,1)}), bf16[1536,512]{1,0:T(8,128)(2,1)}) %all-gather.7.cloned.1.call-update) | async-done | bytes 1572880 | tf_op jit(solution)/shard_map/all_gather | solution.py:61
  54.2 51.7 %all-gather.5.cloned.1.call-done = bf16[2048,640]{1,0:T(8,128)(2,1)} async-done(((bf16[512,640]{1,0:T(8,128)(2,1)}), bf16[2048,640]{1,0:T(8,128)(2,1)}) %all-gather.5.cloned.1.call-update) | async-done | bytes 2621456 | tf_op jit(solution)/shard_map/all_gather | solution.py:60
  122.8 3.9 reshape.192
  133.4 4.8 fusion.35
  150.9 4.2 reshape.193
  160.0 9.7 %fusion.13 = (f32[1024,1024]{1,0:T(8,128)}, f32[1024,1024]{0,1:T(8,128)S(1)}) fusion(f32[1024,1024]{0,1:T(8,128)S(1)} %fusion.106), kind=kLoop, calls=%fused_computation.35 | loop fusion | flops 65011712 | bytes 12582912 | tf_op jit(solution)/shard_map/mul | solution.py:31
  175.8 4.3 fusion.51
  181.7 39.6 %all-reduce.1 = (f32[64,7]{0,1:T(8,128)S(1)}, f32[64]{0:T(128)S(1)}, f32[64,7]{0,1:T(8,128)S(1)}) all-reduce(f32[64,7]{0,1:T(8,128)S(1)} %fusion.80, f32[64]{0:T(128)S(1)} %copy-done.60, f32[64,7]{0,1:T(8,128)S(1)} %convolution_negate_fusion), channel_id=1, replica_groups=mesh['nodes'=8,'tp'=4] {'nodes','tp'}, use_global_device_ids=true, to_apply=%region_8.9 | all-reduce | flops 960 | bytes 7680 | tf_op jit(solution)/shard_map/psum | solution.py:127
  225.2 5.7 %add_convert_fusion = bf16[1024,1024]{0,1:T(8,128)(2,1)S(1)} fusion(f32[1024,1024]{0,1:T(8,128)} %copy-done.7, f32[1024,1024]{0,1:T(8,128)} %copy-done, bf16[1024,512]{1,0:T(8,128)(2,1)S(1)} %bitcast.174, f32[128,7,512]{2,1,0:T(8,128)S(1)} %multiply_add_fusion, f32[128,1,512]{2,1,0:T(1,128)S(1)} %copy-done.22), kind=kOutput, calls=%fused_computation.19 | convolution fusion | flops 1090519040 | bytes 13631488 | tf_op jit(solution)/shard_map/rd,fd->rf/dot_general | solution.py:148
  237.1 5.4 %copy.225 = f32[1024,1024]{0,1:T(8,128)} copy(f32[1024,1024]{1,0:T(8,128)} %get-tuple-element.35) | data formatting | bytes 8388608 | tf_op jit(solution)/shard_map/mul | solution.py:31
  242.5 4.0 abs_compare_fusion
  246.5 10.4 %broadcast_subtract_fusion = (f32[1024,1024]{0,1:T(8,128)}, f32[1024,1024]{0,1:T(8,128)}, f32[1024,1024]{0,1:T(8,128)}) fusion(f32[1024,1024]{0,1:T(8,128)S(1)} %copy-done.2), kind=kLoop, calls=%fused_computation.75 | loop fusion | flops 58720256 | bytes 16777216 | tf_op jit(solution)/shard_map/erfc | solution.py:31
  267.8 5.4 %copy.230 = f32[1024,1024]{1,0:T(8,128)} copy(f32[1024,1024]{0,1:T(8,128)} %get-tuple-element.30) | data formatting | bytes 8388608 | tf_op jit(solution)/shard_map/erfc | solution.py:31
  273.1 5.3 %copy.231 = f32[1024,1024]{1,0:T(8,128)} copy(f32[1024,1024]{0,1:T(8,128)} %get-tuple-element.31) | data formatting | bytes 8388608 | tf_op jit(solution)/shard_map/erfc | solution.py:31
  278.5 5.6 %copy.233 = f32[1024,1024]{1,0:T(8,128)} copy(f32[1024,1024]{0,1:T(8,128)} %get-tuple-element.34) | data formatting | bytes 8388608 | tf_op jit(solution)/shard_map/erfc | solution.py:31
  284.1 8.3 %fusion.2 = bf16[1024,1024]{1,0:T(8,128)(2,1)S(1)} fusion(pred[1024,1024]{1,0:T(8,128)(4,1)S(1)} %copy-done.15, f32[1024,1024]{1,0:T(8,128)} %copy.233, f32[1024,1024]{1,0:T(8,128)} %copy.230, f32[1024,1024]{1,0:T(8,128)} %copy.231, f32[1024,1024]{0,1:T(8,128)} %copy-done), kind=kLoop, calls=%fused_computation.4 | loop fusion | flops 8388608 | bytes 19922944 | tf_op jit(solution)/shard_map/convert_element_type | solution.py:110
  300.1 3.9 reshape.200
  303.9 5.4 %fusion.30 = f32[8,128,8,8]{3,2,1,0:T(8,128)} fusion(bf16[128,8,8,64]{3,2,1,0:T(8,128)(2,1)} %reshape.200, bf16[128,8,8,64]{3,2,1,0:T(8,128)(2,1)} %reshape.188), kind=kOutput, calls=%fused_computation.60 | convolution fusion | flops 8388608 | bytes 2359296 | tf_op jit(solution)/shard_map/nqhe,nkhe->hqkn/dot_general | solution.py:174
  318.3 4.1 reshape.203
  330.8 4.2 copy.212
  340.4 4.0 reshape.202
  349.6 4.2 reshape.201
  380.3 42.9 %all-reduce = (f32[512]{0:T(512)}, f32[512]{0:T(512)}, f32[512]{0:T(512)}, f32[512]{0:T(512)}, f32[512]{0:T(512)}) all-reduce(f32[512]{0:T(512)S(1)} %get-tuple-element.15, f32[512]{0:T(512)S(1)} %get-tuple-element.18, f32[512]{0:T(512)S(1)} %copy-done.47, f32[512]{0:T(512)S(1)} %copy-done.48, ...), channel_id=1, replica_groups=mesh['nodes'=8,'tp'=4] {'nodes','tp'}, use_global_device_ids=true, to_apply=%region_19.20 | all-reduce | flops 2560 | bytes 20480 | tf_op jit(solution)/shard_map/psum | solution.py:229
  430.5 53.7 %all-reduce.5.cloned.1.call-done = (bf16[512,640]{1,0:T(8,128)(2,1)}, bf16[384,512]{1,0:T(8,128)(2,1)}) async-done(((bf16[512,640]{1,0:T(8,128)(2,1)}, bf16[384,512]{1,0:T(8,128)(2,1)}), (bf16[512,640]{1,0:T(8,128)(2,1)}, bf16[384,512]{1,0:T(8,128)(2,1)})) %all-reduce.5.cloned.1.call-update) | async-done | bytes 1048592 | tf_op jit(solution)/shard_map/psum | solution.py:218
  (246 shorter events, 158.8 us)
Async XLA Ops:
  7.2 5.9 %copy-start.59 = (bf16[512]{0:T(512)(128)(2,1)S(1)}, bf16[512]{0:T(512)(128)(2,1)}, u32[]{:S(2)}) copy-start(bf16[512]{0:T(512)(128)(2,1)} %param.25) | copy-start | bytes 3076
  7.2 6.5 %copy-start.40 = (s32[1024]{0:T(1024)S(1)}, s32[1024]{0:T(1024)}, u32[]{:S(2)}) copy-start(s32[1024]{0:T(1024)} %param.16) | copy-start | bytes 12292
  7.2 6.9 %copy-start.27 = (bf16[128,512]{1,0:T(8,128)(2,1)S(1)}, bf16[128,512]{1,0:T(8,128)(2,1)}, u32[]{:S(2)}) copy-start(bf16[128,512]{1,0:T(8,128)(2,1)} %param.29) | copy-start | bytes 393220
  7.3 42.8 %all-gather.7.cloned.1.call-start = ((), (), s32[]{:S(2)}) async-start(), calls=%async_computation.5 | async-start | bytes 1966080 | tf_op jit(solution)/shard_map/all_gather | solution.py:61
  9.1 6.8 %copy-start.49 = (s32[128]{0:T(128)S(1)}, s32[128]{0:T(128)}, u32[]{:S(2)}) copy-start(s32[128]{0:T(128)} %param.17) | copy-start | bytes 1540
  9.1 7.5 %copy-start.1 = (bf16[1024,512]{1,0:T(8,128)(2,1)S(1)}, bf16[1024,512]{1,0:T(8,128)(2,1)}, u32[]{:S(2)}) copy-start(bf16[1024,512]{1,0:T(8,128)(2,1)} %param.15) | copy-start | bytes 3145732
  9.1 96.8 %all-gather.5.cloned.1.call-start = ((), (), s32[]{:S(2)}) async-start(), calls=%async_computation.4 | async-start | bytes 3276800 | tf_op jit(solution)/shard_map/all_gather | solution.py:60
  11.3 416.1 %reduce-scatter.5.cloned.1.call-start = ((), (), s32[]{:S(2)}) async-start(), calls=%async_computation.3 | async-start | bytes 1966080 | tf_op jit(solution)/shard_map/reduce_scatter | solution.py:221
  12.5 114.1 %copy-start.36 = (f32[512]{0:T(512)}, f32[512]{0:T(512)S(1)}, u32[]{:S(2)}) copy-start(f32[512]{0:T(512)S(1)} %convert_element_type.153) | copy-start | bytes 6148
  12.6 114.1 %copy-start.51 = (f32[512]{0:T(512)}, f32[512]{0:T(512)S(1)}, u32[]{:S(2)}) copy-start(f32[512]{0:T(512)S(1)} %convert_element_type.154) | copy-start | bytes 6148
  14.0 127.2 %copy-start.38 = (pred[8,128]{1,0:T(8,128)(4,1)}, pred[8,128]{1,0:T(8,128)(4,1)S(1)}, u32[]{:S(2)}) copy-start(pred[8,128]{1,0:T(8,128)(4,1)S(1)} %copy.188) | copy-start | bytes 3076
  17.3 109.4 %copy-start.30 = (f32[1024]{0:T(1024)}, f32[1024]{0:T(1024)S(1)}, u32[]{:S(2)}) copy-start(f32[1024]{0:T(1024)S(1)} %fusion.89) | copy-start | bytes 12292
  119.6 13.8 %copy-start.6 = (bf16[128,8,8,64]{3,2,1,0:T(8,128)(2,1)}, bf16[128,8,8,64]{3,2,1,0:T(8,128)(2,1)S(1)}, u32[]{:S(2)}) copy-start(bf16[128,8,8,64]{3,2,1,0:T(8,128)(2,1)S(1)} %reshape.190) | copy-start | bytes 3145732
  160.0 9.7 %copy-start = (f32[1024,1024]{0,1:T(8,128)}, f32[1024,1024]{0,1:T(8,128)S(1)}, u32[]{:S(2)}) copy-start(f32[1024,1024]{0,1:T(8,128)S(1)} %fusion.106) | copy-start | bytes 12582916
  160.0 9.7 %copy-start.16 = (bf16[4,256,512]{2,1,0:T(8,128)(2,1)S(1)}, bf16[4,256,512]{2,1,0:T(8,128)(2,1)}, u32[]{:S(2)}) copy-start(bf16[4,256,512]{2,1,0:T(8,128)(2,1)} %slice.65) | copy-start | bytes 3145732
  284.1 8.3 %copy-start.12 = (f32[128,7,512]{2,1,0:T(8,128)S(1)}, f32[128,7,512]{2,1,0:T(8,128)}, u32[]{:S(2)}) copy-start(f32[128,7,512]{2,1,0:T(8,128)} %copy-done.11) | copy-start | bytes 5505028
  284.1 8.3 %copy-start.23 = (f32[128,1,512]{2,1,0:T(1,128)S(1)}, f32[128,1,512]{2,1,0:T(1,128)}, u32[]{:S(2)}) copy-start(f32[128,1,512]{2,1,0:T(1,128)} %copy.202) | copy-start | bytes 786436
  297.2 130.2 %reduce-scatter.3.cloned.1.call-start = ((), (), s32[]{:S(2)}) async-start(), calls=%async_computation.2 | async-start | bytes 3276800 | tf_op jit(solution)/shard_map/reduce_scatter | solution.py:220
  318.3 6.3 %copy-start.31 = (f32[1024]{0:T(1024)S(1)}, f32[1024]{0:T(1024)}, u32[]{:S(2)}) copy-start(f32[1024]{0:T(1024)} %copy-done.30) | copy-start | bytes 12292
  318.3 6.3 %copy-start.37 = (f32[512]{0:T(512)S(1)}, f32[512]{0:T(512)}, u32[]{:S(2)}) copy-start(f32[512]{0:T(512)} %copy-done.36) | copy-start | bytes 6148
  318.3 6.3 %copy-start.52 = (f32[512]{0:T(512)S(1)}, f32[512]{0:T(512)}, u32[]{:S(2)}) copy-start(f32[512]{0:T(512)} %copy-done.51) | copy-start | bytes 6148
  349.6 6.5 %copy-start.53 = (f32[512]{0:T(512)S(1)}, f32[512]{0:T(512)}, u32[]{:S(2)}) copy-start(f32[512]{0:T(512)} %copy-done.51) | copy-start | bytes 6148
  371.1 113.1 %all-reduce.5.cloned.1.call-start = ((), (), s32[]{:S(2)}) async-start(), calls=%async_computation.6 | async-start | bytes 2097152 | tf_op jit(solution)/shard_map/psum | solution.py:218
  379.0 47.7 %slice-start = ((f32[128,8,512]{2,1,0:T(8,128)}), f32[128,1,512]{2,1,0:T(1,128)S(1)}, s32[]{:S(2)}) async-start(f32[128,8,512]{2,1,0:T(8,128)} %copy-done.3), calls=%async_computation.7 | async-start | bytes 524288 | tf_op jit(solution)/shard_map/slice | solution.py:115
  (43 other events, 131.2 us)
Sparse Core Ops, SparseCore 0:
  10.2 39.7 all-gather.6
  52.2 53.6 all-gather.4
  297.4 35.0 reduce-scatter.4
  371.2 53.0 reduce-scatter.2
  427.6 56.5 all-reduce.4

commit v2 on v0

v2 whole, which is shorter than its diff:
```python
import functools

import jax
import jax.numpy as jnp
from jax import lax
from jax.experimental import pallas as pl
from jax.experimental.pallas import tpu as pltpu
from jax.sharding import PartitionSpec as P

HOPS = 8
HEAD = 64
GRAPHS = 64
EPSILON = 1e-05
NEGATIVE = -1000000000.0
MESH = pl.DeviceIdType.MESH
F32 = jnp.float32
BF16 = jnp.bfloat16
CHUNK = 256
TILE = 128


def mm(a, b):
    return lax.dot_general(a, b, (((1,), (0,)), ((), ())), preferred_element_type=F32)


def mm_rt(a, b):
    return lax.dot_general(a, b, (((1,), (1,)), ((), ())), preferred_element_type=F32)


def mm_lt(a, b):
    return lax.dot_general(a, b, (((0,), (0,)), ((), ())), preferred_element_type=F32)


def iota(shape, axis):
    return lax.broadcasted_iota(jnp.int32, shape, axis)


def centred(values):
    centre = values - jnp.mean(values, axis=-1, keepdims=True)
    spread = jnp.mean(centre * centre, axis=-1, keepdims=True)
    return centre * lax.rsqrt(spread + EPSILON), lax.rsqrt(spread + EPSILON)


def gelu_both(x):
    size = jnp.abs(x)
    t = 1.0 / (1.0 + (0.3275911 * 0.7071067811865476) * size)
    bell = jnp.exp(-0.5 * (x * x))
    poly = 1.061405429 * t - 1.453152027
    poly = poly * t + 1.421413741
    poly = poly * t - 0.284496736
    poly = poly * t + 0.254829592
    tail = (0.5 * t) * poly * bell
    phi = jnp.where(x >= 0, 1.0 - tail, tail)
    return x * phi, phi + x * (bell * 0.3989422804014327)


def seg8(x, op, lane):
    for bit in (1, 2, 4):
        up = pltpu.roll(x, bit, x.ndim - 1)
        down = pltpu.roll(x, 128 - bit, x.ndim - 1)
        x = op(x, jnp.where((lane & bit) != 0, up, down))
    return x


class Group:
    def __init__(self, array, wide, recv_core, recv_z, part, recv_plane, final, send, recv):
        self.array, self.wide = array, wide
        self.recv_core, self.recv_z, self.part = recv_core, recv_z, part
        self.recv_plane, self.final = recv_plane, final
        self.send, self.recv = send, recv
        self.half_rows = part.shape[0]
        self.piece_rows = part.shape[0] // 4
        self.width = part.shape[1]

    def half(self, c):
        rows = pl.ds(pl.multiple_of(c * self.half_rows, self.half_rows), self.half_rows)
        return self.array.at[rows] if self.wide else self.array.at[:, rows]

    def slot(self, c, d):
        rows = pl.ds(pl.multiple_of(c * self.half_rows, self.half_rows), self.half_rows)
        if self.wide:
            return self.array.at[rows, d * self.width : (d + 1) * self.width]
        return self.array.at[d, rows]

    def piece(self, ref, p, base=0):
        start = pl.multiple_of(base + p * self.piece_rows, 16)
        return ref.at[pl.ds(start, self.piece_rows)]


def kernel(
    nn,
    tok_hbm,
    mask_ref,
    gid_ref,
    g1_ref,
    s1_ref,
    wq_hbm,
    wk_hbm,
    wv_hbm,
    wo_hbm,
    g2_ref,
    s2_ref,
    wu_hbm,
    wd_hbm,
    hw_ref,
    cot_hbm,
    readout_ref,
    gtok_ref,
    small_ref,
    fin_in_ref,
    fin_out_ref,
    fin_up_ref,
    fin_dn_ref,
    w_in,
    w_up,
    w_od,
    tok,
    cot,
    n1,
    qkv,
    pn,
    ctx,
    res,
    n2,
    act,
    gp,
    lay,
    vcol,
    mt,
    gexp,
    wcol,
    dcol,
    ab,
    zed,
    gbef,
    gl,
    datt,
    dctx,
    dqkv,
    g_up,
    g_dn,
    g_out,
    g_in,
    rc_up,
    rc_dn,
    rc_out,
    rc_in,
    rz_up,
    rz_dn,
    rz_out,
    rz_in,
    sm_up,
    sm_dn,
    sm_out,
    sm_in,
    rp_up,
    rp_dn,
    rp_out,
    rp_in,
    ar_one,
    ar_nodes,
    ar_tp,
    sv_one,
    sv_nodes,
    sv_tp,
    lsem,
    wsend,
    wrecv,
    gsend,
    grecv,
    asend,
    arecv,
    bsend,
    brecv,
):
    n, t = lax.axis_index("nodes"), lax.axis_index("tp")
    rows_here, width = tok.shape
    chunks = rows_here // CHUNK
    tiles = rows_here // TILE
    c = n % 2
    plane = (n // 2) % 4
    half = (plane % 2 + plane // 2) % 2
    quarter = 2 * half + c
    other = 2 * (1 - half) + c
    extra = [b for b in range(3, 12) if (1 << b) < nn]

    def node_peer(k):
        out = n
        for b in range(12):
            if (k >> b) & 1:
                bit = (n // (1 << b)) % 2
                out = out + (1 << b) * (1 - 2 * bit)
        return (out, t)

    def tp_peer(k):
        out = t
        for b in range(2):
            if (k >> b) & 1:
                bit = (t // (1 << b)) % 2
                out = out + (1 << b) * (1 - 2 * bit)
        return (n, out)

    def remote(src, dst, ssem, rsem, peer):
        return pltpu.make_async_remote_copy(
            src_ref=src, dst_ref=dst, send_sem=ssem, recv_sem=rsem, device_id=peer, device_id_type=MESH
        )

    qw = wq_hbm.shape[1]
    local = [
        pltpu.make_async_copy(wq_hbm, w_in.at[:, 0:qw], lsem.at[0]),
        pltpu.make_async_copy(wk_hbm, w_in.at[:, qw : 2 * qw], lsem.at[1]),
        pltpu.make_async_copy(wv_hbm, w_in.at[:, 2 * qw : 3 * qw], lsem.at[2]),
        pltpu.make_async_copy(tok_hbm, tok, lsem.at[3]),
        pltpu.make_async_copy(wo_hbm, w_od.at[0, 0:qw], lsem.at[4]),
        pltpu.make_async_copy(wd_hbm, w_od.at[0, qw:], lsem.at[5]),
        pltpu.make_async_copy(wu_hbm, w_up.at[:, 0 : wu_hbm.shape[1]], lsem.at[6]),
        pltpu.make_async_copy(cot_hbm, cot, lsem.at[7]),
    ]
    for copy in local:
        copy.start()

    barrier = pltpu.get_barrier_semaphore()
    greet = [node_peer(k) for k in range(1, 8)] + [node_peer(1 << b) for b in extra]
    greet += [tp_peer(k) for k in range(1, 4)]
    for peer in greet:
        pl.semaphore_signal(barrier, inc=1, device_id=peer, device_id_type=MESH)
    pl.semaphore_wait(barrier, len(greet))

    def block_of(ref, group, rows, d0, d1):
        if group == 1:
            return ref.at[d0:d1, rows]
        w = ref.shape[1] // 4
        return ref.at[rows, d0 * w : d1 * w]

    weights = [(w_in, 0), (w_od, 1), (w_up, 2)]

    def weight_copies(which):
        ref, group = weights[which]
        total = ref.shape[1] if group == 1 else ref.shape[0]
        quart = total // 4

        def rows(q, off, size):
            return pl.ds(pl.multiple_of(q * quart + off, 16), size)

        base = which * 7
        out = []
        for d in range(1, 4):
            out.append(
                remote(
                    block_of(ref, group, rows(quarter, 0, quart), 0, 1),
                    block_of(ref, group, rows(quarter, 0, quart), d, d + 1),
                    wsend.at[base + d - 1],
                    wrecv.at[base + d - 1],
                    tp_peer(d),
                )
            )
        for e, peer in enumerate((2, 4)):
            piece = block_of(ref, group, rows(quarter, e * (quart // 2), quart // 2), 1, 4)
            out.append(remote(piece, piece, wsend.at[base + 3 + e], wrecv.at[base + 3 + e], node_peer(peer)))
        for e, q in enumerate((quarter, other)):
            piece = block_of(ref, group, rows(q, 0, quart), 1, 4)
            out.append(remote(piece, piece, wsend.at[base + 5 + e], wrecv.at[base + 5 + e], node_peer(1)))
        return out

    copies_in, copies_od, copies_up = weight_copies(0), weight_copies(1), weight_copies(2)

    def step_z(copies):
        for cp in copies[0:3]:
            cp.start()

    def step_plane(copies):
        for cp in copies[0:3]:
            cp.wait()
        for cp in copies[3:6]:
            cp.start()

    def step_core(copies):
        for cp in copies[3:5]:
            cp.wait()
        copies[6].start()

    def step_end(copies):
        for cp in copies[5:7]:
            cp.wait()

    for i in (0, 1, 2):
        local[i].wait()
    step_z(copies_in)

    gain1 = g1_ref[...].astype(F32)
    shift1 = s1_ref[...].astype(F32)
    gain2 = g2_ref[...].astype(F32)
    shift2 = s2_ref[...].astype(F32)
    hopw = hw_ref[...].astype(F32)

    eye = iota((TILE, TILE), 0) == iota((TILE, TILE), 1)
    ones = jnp.ones((TILE, TILE), BF16)
    lane8 = iota((HOPS, TILE), 1)
    block8 = lane8 // HOPS
    left = iota((TILE, TILE), 1) < HEAD
    nodes_chunk = CHUNK // HOPS
    spread_c = (iota((CHUNK, nodes_chunk), 0) // HOPS == iota((CHUNK, nodes_chunk), 1)).astype(F32).astype(BF16)

    def rows_of(i, size):
        return pl.ds(pl.multiple_of(i * size, size), size)

    mask_f = mask_ref[...].astype(F32)
    for i in range(tiles):
        col = mm(jnp.where(eye, mask_f[i : i + 1, :], 0.0).astype(BF16), ones)
        vcol[i * TILE : (i + 1) * TILE, :] = col
        acc = jnp.zeros((HOPS, TILE), F32)
        col3 = col.reshape(TILE // HOPS, HOPS, TILE)
        for r in range(TILE // HOPS):
            acc = jnp.where(block8 == r, col3[r], acc)
        mt[i] = acc
    gcol = mm(jnp.where(eye, gid_ref[...].astype(F32), 0.0).astype(BF16), ones).astype(BF16)
    for i in range(chunks):
        gexp[i * CHUNK : (i + 1) * CHUNK, :] = mm(spread_c, gcol[i * nodes_chunk : (i + 1) * nodes_chunk])

    local[3].wait()

    def norm_one(i, carry):
        x = tok[rows_of(i, CHUNK), :].astype(F32)
        hat, _ = centred(x)
        n1[rows_of(i, CHUNK), :] = (hat * gain1 + shift1).astype(BF16)
        return carry

    lax.fori_loop(0, chunks, norm_one, 0)

    for i in (4, 5, 6, 7):
        local[i].wait()
    step_plane(copies_in)
    step_z(copies_od)
    step_z(copies_up)
    step_core(copies_in)
    step_end(copies_in)

    def project(i, carry):
        r = rows_of(i, CHUNK)
        out = mm(n1[r, :], w_in[...])
        for d in range(4):
            base = d * 3 * qw
            qkv[r, base : base + qw] = (out[:, base : base + qw] * (HEAD**-0.5)).astype(BF16)
            qkv[r, base + qw : base + 3 * qw] = out[:, base + qw : base + 3 * qw].astype(BF16)
        return carry

    lax.fori_loop(0, chunks, project, 0)
    step_plane(copies_od)
    step_plane(copies_up)

    def pair(x):
        zero = jnp.zeros_like(x)
        return jnp.concatenate([jnp.where(left, x, zero), jnp.where(left, zero, x)], axis=0)

    def compact(x):
        out = []
        for h in range(2):
            x3 = x[:, h * TILE : (h + 1) * TILE].reshape(TILE // HOPS, HOPS, TILE)
            acc = x3[0]
            for r in range(1, TILE // HOPS):
                acc = jnp.where(block8 == r, x3[r], acc)
            out.append(acc)
        return out

    def expand(pairs):
        cols = []
        for x in pairs:
            zero = jnp.zeros_like(x)
            cols.append(
                jnp.concatenate([jnp.where(block8 == r, x, zero) for r in range(TILE // HOPS)], axis=0).astype(BF16)
            )
        return jnp.concatenate(cols, axis=1)

    def attend(i, carry):
        r = rows_of(i, TILE)
        keep = mask_ref[pl.ds(i, 1), :].astype(F32) > 0.5
        for d in range(4):
            base = d * 3 * qw
            q = qkv[r, base : base + qw]
            k = qkv[r, base + qw : base + 2 * qw]
            v = qkv[r, base + 2 * qw : base + 3 * qw]
            scores = compact(mm_rt(q, pair(k)))
            probs = []
            for h in range(2):
                s = jnp.where(keep, scores[h], NEGATIVE)
                e = jnp.exp(s - seg8(s, jnp.maximum, lane8))
                p = e / seg8(e, jnp.add, lane8)
                pn[i * 8 + 2 * d + h] = p
                probs.append(p)
            ctx[r, d * qw : (d + 1) * qw] = mm(expand(probs), pair(v)).astype(BF16)
        return carry

    lax.fori_loop(0, tiles, attend, 0)
    step_core(copies_od)
    step_core(copies_up)
    step_end(copies_od)
    step_end(copies_up)

    ow = w_od.shape[1]
    down_rows = ow - qw

    def w_out():
        return w_od[:, 0:qw, :].reshape(4 * qw, width)

    def w_down():
        return w_od[:, qw:ow, :].reshape(4 * down_rows, width)

    hop3 = iota((nodes_chunk, HOPS, TILE), 1)
    lane3 = iota((nodes_chunk, HOPS, TILE), 2)
    node3 = iota((nodes_chunk, HOPS, TILE), 0)
    lane_graph = (lane3 % GRAPHS).astype(F32)

    def feed(i, acc):
        r = rows_of(i, CHUNK)
        attended = mm(ctx[r, :], w_out())
        x = tok[r, :].astype(F32) + attended
        res[r, :] = x
        hat, _ = centred(x)
        normed = (hat * gain2 + shift2).astype(BF16)
        n2[r, :] = normed
        value, slope = gelu_both(mm(normed, w_up[...]))
        value = value.astype(BF16)
        act[r, :] = value
        gp[r, :] = slope.astype(BF16)
        out = x + mm(value, w_down())
        lay[r, :] = out
        dr = mm(spread_c, cot[rows_of(i, nodes_chunk), :])
        logit = jnp.sum(out * hopw, axis=-1, keepdims=True)
        gcoef = jnp.sum(out * dr, axis=-1, keepdims=True)
        shape = (nodes_chunk, HOPS, TILE)
        valid = vcol[r, :].reshape(shape)
        valid = jnp.where(hop3 > 0, valid, 0.0)
        logit = jnp.where(valid > 0.5, jnp.broadcast_to(logit, (CHUNK, TILE)).reshape(shape), NEGATIVE)
        e = jnp.exp(logit - jnp.max(logit, axis=1, keepdims=True))
        e = jnp.where(hop3 > 0, e, 0.0)
        weight = e / jnp.sum(e, axis=1, keepdims=True)
        direct = valid * jnp.broadcast_to(gcoef, (CHUNK, TILE)).reshape(shape)
        wcol[r, :] = weight.reshape(CHUNK, TILE)
        dcol[r, :] = direct.reshape(CHUNK, TILE)
        mine = gexp[r, :].reshape(shape) == lane_graph
        both = jnp.where(lane3 < GRAPHS, jnp.where(hop3 == 0, 1.0, weight), -direct)
        return acc + jnp.sum(jnp.where(mine, both, 0.0), axis=0)

    sums = lax.fori_loop(0, chunks, feed, jnp.zeros((HOPS, TILE), F32))

    def reduce_all(value, one, by_nodes, by_tp, ssem, rsem, overlap=None):
        one[0] = value
        copies = [
            remote(one.at[0], by_nodes.at[k - 1], ssem.at[k - 1], rsem.at[k - 1], node_peer(k)) for k in range(1, 8)
        ]
        for cp in copies:
            cp.start()
        if overlap is not None:
            overlap()
        for cp in copies:
            cp.wait()
        value = one[0]
        for k in range(7):
            value = value + by_nodes[k]
        at = 7
        for b in extra:
            one[at - 6] = value
            cp = remote(one.at[at - 6], by_nodes.at[at], ssem.at[at], rsem.at[at], node_peer(1 << b))
            cp.start()
            cp.wait()
            value = value + by_nodes[at]
            at += 1
        last = one.shape[0] - 1
        one[last] = value
        copies = [
            remote(one.at[last], by_tp.at[k - 1], ssem.at[at + k - 1], rsem.at[at + k - 1], tp_peer(k))
            for k in range(1, 4)
        ]
        for cp in copies:
            cp.start()
        return copies, lambda: one[last] + by_tp[0] + by_tp[1] + by_tp[2]

    def small_products():
        drdown = mm_rt(cot[...], w_down()).astype(BF16)
        hopdown = mm_rt(jnp.broadcast_to(hw_ref[...], (16, width)), w_down()).astype(BF16)
        for i in range(chunks):
            piece = drdown[i * nodes_chunk : (i + 1) * nodes_chunk]
            ab[i, 0:nodes_chunk] = piece
            ab[i, nodes_chunk : 2 * nodes_chunk] = piece
            ab[i, 2 * nodes_chunk : 2 * nodes_chunk + 16] = hopdown
            ab[i, 2 * nodes_chunk + 16 :] = jnp.zeros((TILE - 2 * nodes_chunk - 16, ab.shape[2]), BF16)

    copies, total = reduce_all(sums, ar_one, ar_nodes, ar_tp, asend, arecv, small_products)
    for cp in copies:
        cp.wait()
    sums = total()
    row = jnp.broadcast_to(sums[0:1, :], (HOPS, TILE))
    counts = jnp.where(lane8 < GRAPHS, row, pltpu.roll(row, GRAPHS, 1))
    means = (sums / (counts + 1.0))[None]

    def back_one(i, carry):
        gain_acc, shift_acc, hop_acc, zed_acc = carry
        r = rows_of(i, CHUNK)
        shape = (nodes_chunk, HOPS, TILE)
        picked = jnp.where(gexp[r, :].reshape(shape) == lane_graph, means, 0.0)
        mean_r = jnp.sum(jnp.where(lane3 < GRAPHS, picked, 0.0), axis=-1, keepdims=True)
        grad_mean = jnp.sum(jnp.where(lane3 < GRAPHS, 0.0, picked), axis=-1, keepdims=True)
        weight = wcol[r, :].reshape(shape)
        valid = vcol[r, :].reshape(shape)
        coef = jnp.where(hop3 > 0, valid * (weight - mean_r), 1.0)
        grad_w = dcol[r, :].reshape(shape) + grad_mean
        glog = weight * (grad_w - jnp.sum(weight * grad_w, axis=1, keepdims=True))
        coef_hi = coef.astype(BF16).astype(F32)
        glog_hi = glog.astype(BF16).astype(F32)
        zero = jnp.zeros_like(coef)
        mix = jnp.where(lane3 == node3, coef_hi, zero)
        mix = jnp.where(lane3 == node3 + nodes_chunk, coef - coef_hi, mix)
        mix = jnp.where(lane3 == 2 * nodes_chunk, glog_hi, mix)
        mix = jnp.where(lane3 == 2 * nodes_chunk + 1, glog - glog_hi, mix)
        mix = mix.reshape(CHUNK, TILE).astype(BF16)

        dr = cot[rows_of(i, nodes_chunk), :]
        hop16 = jnp.broadcast_to(hw_ref[...], (16, width))
        rest = jnp.zeros((TILE - 2 * nodes_chunk - 16, width), BF16)
        dh = jnp.concatenate([dr, dr, hop16, rest], axis=0)
        grad_layer = mm(mix, dh)
        gl[r, :] = grad_layer
        before_back = (mm(mix, ab[i]) * gp[r, :].astype(F32)).astype(BF16)
        gbef[r, :] = before_back

        seen = mm_lt(mix, lay[r, :].astype(BF16))
        readout_ref[rows_of(i, nodes_chunk), :] = (seen[0:nodes_chunk] + seen[nodes_chunk : 2 * nodes_chunk]).astype(
            BF16
        )
        hop_acc = hop_acc + seen[2 * nodes_chunk : 2 * nodes_chunk + 8]
        fold = mm_lt(mix, act[r, :])
        zed[rows_of(i, nodes_chunk), :] = (fold[0:nodes_chunk] + fold[nodes_chunk : 2 * nodes_chunk]).astype(BF16)
        zed_acc = zed_acc + fold[2 * nodes_chunk : 2 * nodes_chunk + 8]

        dy = mm_rt(before_back, w_up[...])
        hat, inv = centred(res[r, :])
        gain_acc = gain_acc + jnp.sum((dy * hat).reshape(nodes_chunk, HOPS, width), axis=0)
        shift_acc = shift_acc + jnp.sum(dy.reshape(nodes_chunk, HOPS, width), axis=0)
        g = dy * gain2
        back = inv * (
            g - jnp.mean(g, axis=-1, keepdims=True) - hat * jnp.mean(g * hat, axis=-1, keepdims=True)
        )
        grad_res = grad_layer + back
        gl[r, :] = grad_res
        att = grad_res.astype(BF16)
        datt[r, :] = att
        dctx[r, :] = mm_rt(att, w_out()).astype(BF16)
        return gain_acc, shift_acc, hop_acc, zed_acc

    zero8 = jnp.zeros((HOPS, width), F32)
    gain_two, shift_two, hop_sum, zed_sum = lax.fori_loop(
        0, chunks, back_one, (zero8, zero8, zero8, jnp.zeros((HOPS, zed.shape[1]), F32))
    )

    groups = []
    sets = [
        (g_dn, False, rc_dn, rz_dn, sm_dn, rp_dn, fin_dn_ref),
        (g_up, True, rc_up, rz_up, sm_up, rp_up, fin_up_ref),
        (g_out, False, rc_out, rz_out, sm_out, rp_out, fin_out_ref),
        (g_in, True, rc_in, rz_in, sm_in, rp_in, fin_in_ref),
    ]
    for i, item in enumerate(sets):
        groups.append(Group(*item, gsend.at[i], grecv.at[i]))
    dn, up, ot, qk = groups

    def core_copy(g):
        return remote(g.half(1 - c), g.recv_core, g.send.at[0], g.recv.at[0], node_peer(1))

    def z_copies(g):
        return [
            remote(g.slot(c, d), g.recv_z.at[d - 1], g.send.at[d], g.recv.at[d], tp_peer(d)) for d in range(1, 4)
        ]

    def plane_peer_piece(e):
        out = plane
        for b in range(2):
            if (e >> b) & 1:
                out = out + (1 << b) * (1 - 2 * ((plane // (1 << b)) % 2))
        return out

    def plane_copies(g):
        return [
            remote(
                g.piece(g.part, plane_peer_piece(e)),
                g.recv_plane.at[e - 1],
                g.send.at[3 + e],
                g.recv.at[3 + e],
                node_peer(2 * e),
            )
            for e in range(1, 4)
        ]

    def final_copies(g):
        mine = g.piece(g.final, plane, c * g.half_rows)
        return [remote(mine, mine, g.send.at[6 + e], g.recv.at[6 + e], node_peer(2 * e)) for e in range(1, 4)]

    def last_copy(g):
        rows = g.final.at[pl.ds(pl.multiple_of(c * g.half_rows, g.half_rows), g.half_rows)]
        return remote(rows, rows, g.send.at[10], g.recv.at[10], node_peer(1))

    def go_core(g):
        core_copy(g).start()

    def go_z(g):
        core_copy(g).wait()
        mine = g.half(c)
        mine[...] = (mine[...].astype(F32) + g.recv_core[...].astype(F32)).astype(BF16)
        for cp in z_copies(g):
            cp.start()

    def go_plane(g):
        for cp in z_copies(g):
            cp.wait()
        total = g.slot(c, 0)[...].astype(F32)
        for d in range(3):
            total = total + g.recv_z[d].astype(F32)
        g.part[...] = total.astype(BF16)
        for cp in plane_copies(g):
            cp.start()

    def go_final(g):
        for cp in plane_copies(g):
            cp.wait()
        total = g.piece(g.part, plane)[...].astype(F32)
        for e in range(3):
            total = total + g.recv_plane[e].astype(F32)
        for j, b in enumerate(extra):
            g.recv_plane[3 + 2 * j] = total.astype(BF16)
            cp = remote(
                g.recv_plane.at[3 + 2 * j],
                g.recv_plane.at[4 + 2 * j],
                g.send.at[11 + j],
                g.recv.at[11 + j],
                node_peer(1 << b),
            )
            cp.start()
            cp.wait()
            total = total + g.recv_plane[4 + 2 * j].astype(F32)
        g.piece(g.final, plane, c * g.half_rows)[...] = total.astype(BF16)
        for cp in final_copies(g):
            cp.start()

    def go_last(g):
        for cp in final_copies(g):
            cp.wait()
        last_copy(g).start()

    def finish(g):
        last_copy(g).wait()

    zed[rows_here // HOPS :, :] = jnp.concatenate([zed_sum, jnp.zeros_like(zed_sum)], axis=0).astype(BF16)
    drh = jnp.concatenate([cot[...], jnp.broadcast_to(hw_ref[...], (16, width))], axis=0)
    g_dn[...] = mm_lt(zed[...], drh).astype(BF16).reshape(g_dn.shape)
    go_core(dn)
    g_up[...] = mm_lt(n2[...], gbef[...]).astype(BF16)
    go_core(up)
    go_z(dn)
    g_out[...] = mm_lt(ctx[...], datt[...]).astype(BF16).reshape(g_out.shape)
    go_core(ot)
    go_z(up)

    def attend_back(i, carry):
        r = rows_of(i, TILE)
        keep = mt[i] > 0.5
        for d in range(4):
            base = d * 3 * qw
            q = qkv[r, base : base + qw]
            k = qkv[r, base + qw : base + 2 * qw]
            v = qkv[r, base + 2 * qw : base + 3 * qw]
            do = dctx[r, d * qw : (d + 1) * qw]
            k2, q2, v2, do2 = pair(k), pair(q), pair(v), pair(do)
            grad_p = compact(mm_rt(do, v2))
            ds = []
            for h in range(2):
                p = pn[i * 8 + 2 * d + h]
                ds.append(p * (grad_p[h] - seg8(p * grad_p[h], jnp.add, lane8)))
            dqkv[r, base : base + qw] = (mm(expand(ds), k2) * (HEAD**-0.5)).astype(BF16)
            scores = compact(mm_rt(k, q2))
            grad_pt = compact(mm_rt(v, do2))
            probs, dst = [], []
            for h in range(2):
                s = jnp.where(keep, scores[h], NEGATIVE)
                e = jnp.exp(s - jnp.max(s, axis=0, keepdims=True))
                p = e / jnp.sum(e, axis=0, keepdims=True)
                probs.append(p)
                dst.append(p * (grad_pt[h] - jnp.sum(p * grad_pt[h], axis=0, keepdims=True)))
            dqkv[r, base + qw : base + 2 * qw] = mm(expand(dst), q2).astype(BF16)
            dqkv[r, base + 2 * qw : base + 3 * qw] = mm(expand(probs), do2).astype(BF16)
        return carry

    lax.fori_loop(0, tiles, attend_back, 0)
    go_z(ot)
    go_plane(dn)
    go_plane(up)
    g_in[...] = mm_lt(n1[...], dqkv[...]).astype(BF16)
    go_core(qk)
    go_plane(ot)
    go_final(dn)
    go_final(up)

    def back_two(i, carry):
        gain_acc, shift_acc = carry
        r = rows_of(i, CHUNK)
        dy = mm_rt(dqkv[r, :], w_in[...])
        hat, inv = centred(tok[r, :].astype(F32))
        gain_acc = gain_acc + jnp.sum((dy * hat).reshape(nodes_chunk, HOPS, width), axis=0)
        shift_acc = shift_acc + jnp.sum(dy.reshape(nodes_chunk, HOPS, width), axis=0)
        g = dy * gain1
        back = inv * (
            g - jnp.mean(g, axis=-1, keepdims=True) - hat * jnp.mean(g * hat, axis=-1, keepdims=True)
        )
        gtok_ref[r, :] = (gl[r, :] + back).astype(BF16)
        return gain_acc, shift_acc

    go_z(qk)
    gain_one, shift_one = lax.fori_loop(0, chunks, back_two, (zero8, zero8))

    def fold8(x):
        return jnp.sum(x, axis=0, keepdims=True)

    small = jnp.concatenate(
        [fold8(gain_one), fold8(shift_one), fold8(gain_two), fold8(shift_two), fold8(hop_sum[0:2]), zero8[0:3]], axis=0
    )

    def rest_of():
        go_final(ot)
        go_last(dn)
        go_last(up)
        go_plane(qk)

    copies, total_small = reduce_all(small, sv_one, sv_nodes, sv_tp, bsend, brecv, rest_of)
    go_last(ot)
    go_final(qk)
    finish(dn)
    finish(up)
    finish(ot)
    for cp in copies:
        cp.wait()
    small_ref[...] = total_small()
    go_last(qk)
    finish(qk)


def shards(
    nn,
    tokens,
    hop_mask,
    graph_ids,
    norm1_gain,
    norm1_shift,
    w_query,
    w_key,
    w_value,
    w_out,
    norm2_gain,
    norm2_shift,
    w_up,
    w_down,
    hop_weight,
    cotangent,
):
    rows, width = tokens.shape
    nodes = rows // HOPS
    qw, uw = w_query.shape[1], w_up.shape[1]
    vm = pl.BlockSpec(memory_space=pltpu.VMEM)
    hbm = pl.BlockSpec(memory_space=pl.ANY)
    extra = len([b for b in range(3, 12) if (1 << b) < nn])

    def v(*shape, dtype=BF16):
        return pltpu.VMEM(shape, dtype)

    tiles, chunks = rows // TILE, rows // CHUNK
    half = width // 2
    scratch = [
        v(width, 12 * qw),
        v(width, 4 * uw),
        v(4, qw + uw, width),
        v(rows, width),
        v(nodes, width),
        v(rows, width),
        v(rows, 12 * qw),
        v(tiles * 8, HOPS, TILE, dtype=F32),
        v(rows, width),
        v(rows, width, dtype=F32),
        v(rows, width),
        v(rows, 4 * uw),
        v(rows, 4 * uw),
        v(rows, width, dtype=F32),
        v(rows, TILE, dtype=F32),
        v(tiles, HOPS, TILE, dtype=F32),
        v(rows, TILE, dtype=F32),
        v(rows, TILE, dtype=F32),
        v(rows, TILE, dtype=F32),
        v(chunks, TILE, 4 * uw),
        v(nodes + 16, 4 * uw),
        v(rows, 4 * uw),
        v(rows, width, dtype=F32),
        v(rows, width),
        v(rows, width),
        v(rows, 12 * qw),
        v(width, 4 * uw),
        v(4, uw, width),
        v(4, qw, width),
        v(width, 12 * qw),
        v(half, 4 * uw),
        v(4, uw // 2, width),
        v(4, qw // 2, width),
        v(half, 12 * qw),
        v(3, half, uw),
        v(3, uw // 2, width),
        v(3, qw // 2, width),
        v(3, half, 3 * qw),
        v(half, uw),
        v(uw // 2, width),
        v(qw // 2, width),
        v(half, 3 * qw),
        v(3 + 2 * extra, half // 4, uw),
        v(3 + 2 * extra, uw // 8, width),
        v(3 + 2 * extra, qw // 8, width),
        v(3 + 2 * extra, half // 4, 3 * qw),
        v(2 + extra, HOPS, TILE, dtype=F32),
        v(7 + extra, HOPS, TILE, dtype=F32),
        v(3, HOPS, TILE, dtype=F32),
        v(2 + extra, 8, width, dtype=F32),
        v(7 + extra, 8, width, dtype=F32),
        v(3, 8, width, dtype=F32),
        pltpu.SemaphoreType.DMA((8,)),
        pltpu.SemaphoreType.DMA((21,)),
        pltpu.SemaphoreType.DMA((21,)),
        pltpu.SemaphoreType.DMA((4, 11 + extra)),
        pltpu.SemaphoreType.DMA((4, 11 + extra)),
        pltpu.SemaphoreType.DMA((10 + extra,)),
        pltpu.SemaphoreType.DMA((10 + extra,)),
        pltpu.SemaphoreType.DMA((10 + extra,)),
        pltpu.SemaphoreType.DMA((10 + extra,)),
    ]
    outs = [
        jax.ShapeDtypeStruct((nodes, width), BF16),
        jax.ShapeDtypeStruct((rows, width), BF16),
        jax.ShapeDtypeStruct((8, width), F32),
        jax.ShapeDtypeStruct((width, 3 * qw), BF16),
        jax.ShapeDtypeStruct((qw, width), BF16),
        jax.ShapeDtypeStruct((width, uw), BF16),
        jax.ShapeDtypeStruct((uw, width), BF16),
    ]
    line = (1, width)
    readout, gtok, small, fin_in, fin_out, fin_up, fin_dn = pl.pallas_call(
        functools.partial(kernel, nn),
        out_shape=outs,
        in_specs=[hbm, vm, vm, vm, vm, hbm, hbm, hbm, hbm, vm, vm, hbm, hbm, vm, hbm],
        out_specs=[vm] * 7,
        scratch_shapes=scratch,
        compiler_params=pltpu.CompilerParams(
            collective_id=0, has_side_effects=True, vmem_limit_bytes=60 * 1024 * 1024
        ),
        name="layer",
    )(
        tokens,
        hop_mask.reshape(tiles, TILE),
        graph_ids.reshape(1, nodes),
        norm1_gain.reshape(line),
        norm1_shift.reshape(line),
        w_query,
        w_key,
        w_value,
        w_out,
        norm2_gain.reshape(line),
        norm2_shift.reshape(line),
        w_up,
        w_down,
        hop_weight.reshape(line),
        cotangent,
    )
    fin_in = fin_in.astype(F32)
    return (
        readout,
        gtok,
        small[0],
        small[1],
        fin_in[:, 0:qw],
        fin_in[:, qw : 2 * qw],
        fin_in[:, 2 * qw :],
        fin_out.astype(F32),
        small[2],
        small[3],
        fin_up.astype(F32),
        fin_dn.astype(F32),
        small[4],
    )


def solution(mesh):
    spread = P(("nodes", "tp"), None)
    flat = P(("nodes", "tp"))
    cols, rows = P(None, "tp"), P("tp", None)
    return jax.shard_map(
        functools.partial(shards, mesh.shape["nodes"]),
        mesh=mesh,
        in_specs=(spread, flat, flat, P(), P(), cols, cols, cols, rows, P(), P(), cols, rows, P(), spread),
        out_specs=(spread, spread, P(), P(), cols, cols, cols, rows, P(), P(), cols, rows, P()),
        check_vma=False,
    )
```

time: 928 us -> 140 us (0.15)
  waiting for transfers between devices: 608 us -> 0 us
  Pallas kernels: 0 us -> 125 us
  matrix products: 97.8 us -> 0 us
  blocking collectives: 96 us -> 0 us
  local copies, waits for them, and re-layouts: 74.2 us -> 9.42 us
  other arithmetic: 31.6 us -> 2.41 us
  between operations: 14.8 us -> 0.68 us
    all_gather x4 -> x0, waiting for transfers between devices: 313 us -> none  [the longest x1 81.4 us: shards(): gathered_two = lax.all_gather(normed_two, 'tp', axis=0, tiled=True)]
    reduce_scatter x4 -> x0, waiting for transfers between devices: 276 us -> none  [the longest x1 75.4 us: shards(): lax.psum_scatter(jnp.einsum('rf,df->rd', piece, up_w, preferred_element_t...]
    pallas_call x0 -> x1, Pallas kernels: none -> 125 us  [shards(): pl.pallas_call(functools.partial(kernel, nn), out_shape=outs, in_specs=[h...]
    dot_general x32 -> x0, matrix products: 97.8 us -> none  [the longest x1 12.5 us: shards(): before = jnp.dot(gathered_two, up_w, preferred_element_type=jnp.float32)]
    psum x2 -> x0, blocking collectives: 82.5 us -> none  [the longest x1 41.5 us: shards(): lax.psum((jnp.dot(member.T, weights, precision=HIGHEST), jnp.sum(member,...]
    convert_element_type x6 -> x0, local copies, waits for them, and re-layouts: 23.3 us -> none  [the longest x1 5.46 us: shards(): grad_queries = (jnp.einsum('hqkn,nkhe->nqhe', grad_scores, key_four, pref...]
    reshape x9 -> x5, local copies, waits for them, and re-layouts: 25.3 us -> 2.9 us  [the longest x1 0.58 us: shards(): norm2_shift.reshape(line)]
    psum x1 -> x0, waiting for transfers between devices: 18.9 us -> none  [shards(): lax.psum((grad_qw, grad_kw, grad_vw, grad_outw, grad_up, grad_down), 'nod...]
  transfers between devices with their start and end apart: 9 -> 0, of which waited for: 9 -> 0; matrix products, arithmetic and copies ran while one was open for 3% -> 0% of each run, Pallas kernels for 0% -> 0%
where the time goes in v2:
time: 140 us; the launch traced here: 138 us
  Pallas kernels  125 us (89%)
  local copies, waits for them, and re-layouts  9.42 us (7%)
  other arithmetic  2.41 us (2%)
    pallas_call x1, Pallas kernels, shards(): pl.pallas_call(functools.partial(kernel, nn), out_shape=outs, in_specs=[h...  125 us
    unnamed x22, local copies, waits for them, and re-layouts  3.04 us

profile of v2, /device:TPU:0, one launch (start us, length us, event | category | flops | bytes accessed | tf_op | source)
XLA Modules:
  0.0 138.0 jit_solution(14287093391683288939)
XLA Ops:
  0.6 0.0 copy-start.5
  0.7 0.7 copy-done.5
  1.3 0.6 reshape.49.g1_ref
  1.9 0.1 copy-done.6
  2.0 0.6 reshape.50.s1_ref
  2.6 0.1 copy-done.7
  2.7 0.6 reshape.51.g2_ref
  3.3 0.1 copy-done.8
  3.4 0.6 reshape.52.s2_ref
  4.0 0.1 copy-done.9
  4.1 0.6 reshape.53.hw_ref
  4.6 125.5 %layer.1 = (bf16[128,512]{1,0:T(8,128)(2,1)}, bf16[1024,512]{1,0:T(8,128)(2,1)}, f32[8,512]{1,0:T(8,128)}, bf16[512,384]{1,0:T(8,128)(2,1)}, bf16[128,512]{1,0:T...) custom-call(bf16[1024,512]{1,0:T(8,128)(2,1)} %tok_hbm.1, s32[8,128]{1,0:T(8,128)} %bitcast.7, ...), custom_call_target="tpu_custom_call" | custom-call | tf_op jit(solution)/shard_map/layer/pallas_call | solution.py:847
  130.1 1.5 %fusion.1 = (f32[1,512]{1,0:T(1,128)}, f32[1,512]{1,0:T(1,128)}, f32[1,512]{1,0:T(1,128)}, f32[1,512]{1,0:T(1,128)}, f32[1,512]{1,0:T(1,128)}) fusion(f32[8,512]{1,0:T(8,128)} %get-tuple-element.22), kind=kLoop, calls=%fused_computation.1 | loop fusion | bytes 20480 | tf_op jit(solution)/shard_map/slice | solution.py:888
  131.6 2.0 %fusion = (f32[512,128]{1,0:T(8,128)}, f32[512,128]{1,0:T(8,128)}, f32[512,128]{1,0:T(8,128)}) fusion(bf16[512,384]{1,0:T(8,128)(2,1)} %get-tuple-element.23), kind=kLoop, calls=%fused_computation | loop fusion | bytes 1572864 | tf_op jit(solution)/shard_map/slice | solution.py:882
  133.6 0.0 copy-done.3
  133.6 0.7 convert_element_type.13
  134.3 0.3 copy-done.2
  134.6 0.8 convert_element_type.14
  135.5 0.0 copy-done.1
  135.5 0.9 convert_element_type.15
  136.3 0.0 copy-done.4
  136.4 0.7 copy.30
  137.0 0.0 copy-done
  137.0 1.0 copy.31
  (9 shorter events, 0.0 us)
Async XLA Ops:
  0.6 0.7 copy-start.5
  1.3 0.7 copy-start.6
  2.0 0.7 copy-start.7
  2.7 0.7 copy-start.8
  3.4 0.7 copy-start.9
  131.6 2.0 %copy-start.3 = (bf16[128,512]{1,0:T(8,128)(2,1)S(1)}, bf16[128,512]{1,0:T(8,128)(2,1)}, u32[]{:S(2)}) copy-start(bf16[128,512]{1,0:T(8,128)(2,1)} %get-tuple-element.24) | copy-start | bytes 393220
  131.6 3.8 %copy-start.1 = (bf16[256,512]{1,0:T(8,128)(2,1)S(1)}, bf16[256,512]{1,0:T(8,128)(2,1)}, u32[]{:S(2)}) copy-start(bf16[256,512]{1,0:T(8,128)(2,1)} %get-tuple-element.26) | copy-start | bytes 786436
  133.6 1.0 copy-start.2
  133.6 3.4 %copy-start = (bf16[1024,512]{1,0:T(8,128)(2,1)S(1)}, bf16[1024,512]{1,0:T(8,128)(2,1)}, u32[]{:S(2)}) copy-start(bf16[1024,512]{1,0:T(8,128)(2,1)} %get-tuple-element.49) | copy-start | bytes 3145732
  135.5 0.9 copy-start.4

commit v3 on v2

--- a/solution.py
+++ b/solution.py
@@ -54,37 +54,39 @@
     return x * phi, phi + x * (bell * 0.3989422804014327)
 
 
-def seg8(x, op, lane):
-    for bit in (1, 2, 4):
-        up = pltpu.roll(x, bit, x.ndim - 1)
-        down = pltpu.roll(x, 128 - bit, x.ndim - 1)
-        x = op(x, jnp.where((lane & bit) != 0, up, down))
-    return x
+def tokens_of(ref):
+    return ref[...].astype(F32).reshape(1, ref.shape[0])
 
 
 class Group:
-    def __init__(self, array, wide, recv_core, recv_z, part, recv_plane, final, send, recv):
+    def __init__(self, array, wide, cols, recv_core, recv_plane, recv_z, final, send, recv, base):
         self.array, self.wide = array, wide
-        self.recv_core, self.recv_z, self.part = recv_core, recv_z, part
-        self.recv_plane, self.final = recv_plane, final
-        self.send, self.recv = send, recv
-        self.half_rows = part.shape[0]
-        self.piece_rows = part.shape[0] // 4
-        self.width = part.shape[1]
-
-    def half(self, c):
-        rows = pl.ds(pl.multiple_of(c * self.half_rows, self.half_rows), self.half_rows)
-        return self.array.at[rows] if self.wide else self.array.at[:, rows]
-
-    def slot(self, c, d):
-        rows = pl.ds(pl.multiple_of(c * self.half_rows, self.half_rows), self.half_rows)
+        self.cols = cols
+        self.recv_core, self.recv_plane, self.recv_z = recv_core, recv_plane, recv_z
+        self.final = final
+        self.send, self.recv, self.base = send, recv, base
+        rows = final.shape[0]
+        self.half_rows = rows // 2
+        self.piece_rows = rows // 8
+        self.width = final.shape[1]
+
+    def sems(self, k):
+        return self.send.at[self.base + k], self.recv.at[self.base + k]
+
+    def rows(self, c, p=None):
+        if p is None:
+            return pl.ds(pl.multiple_of(c * self.half_rows, 16), self.half_rows)
+        return pl.ds(pl.multiple_of(c * self.half_rows + p * self.piece_rows, 16), self.piece_rows)
+
+    def block(self, rows):
+        if self.wide:
+            return self.array.at[rows, self.cols[0] * self.width : self.cols[1] * self.width]
+        return self.array.at[:, rows]
+
+    def slot(self, rows, d):
         if self.wide:
             return self.array.at[rows, d * self.width : (d + 1) * self.width]
         return self.array.at[d, rows]
-
-    def piece(self, ref, p, base=0):
-        start = pl.multiple_of(base + p * self.piece_rows, 16)
-        return ref.at[pl.ds(start, self.piece_rows)]
 
 
 def kernel(
@@ -125,6 +127,8 @@
     act,
     gp,
     lay,
+    emask,
+    pmask,
     vcol,
     mt,
     gexp,
@@ -145,18 +149,14 @@
     rc_dn,
     rc_out,
     rc_in,
+    rp_up,
+    rp_dn,
+    rp_out,
+    rp_in,
     rz_up,
     rz_dn,
     rz_out,
     rz_in,
-    sm_up,
-    sm_dn,
-    sm_out,
-    sm_in,
-    rp_up,
-    rp_dn,
-    rp_out,
-    rp_in,
     ar_one,
     ar_nodes,
     ar_tp,
@@ -179,9 +179,7 @@
     tiles = rows_here // TILE
     c = n % 2
     plane = (n // 2) % 4
-    half = (plane % 2 + plane // 2) % 2
-    quarter = 2 * half + c
-    other = 2 * (1 - half) + c
+    eighth = 4 * c + plane
     extra = [b for b in range(3, 12) if (1 << b) < nn]
 
     def node_peer(k):
@@ -226,78 +224,76 @@
         pl.semaphore_signal(barrier, inc=1, device_id=peer, device_id_type=MESH)
     pl.semaphore_wait(barrier, len(greet))
 
-    def block_of(ref, group, rows, d0, d1):
-        if group == 1:
+    def weight_block(ref, off, size, d0, d1):
+        rows = pl.ds(pl.multiple_of(off, 16), size)
+        if len(ref.shape) == 3:
             return ref.at[d0:d1, rows]
         w = ref.shape[1] // 4
         return ref.at[rows, d0 * w : d1 * w]
 
-    weights = [(w_in, 0), (w_od, 1), (w_up, 2)]
-
-    def weight_copies(which):
-        ref, group = weights[which]
-        total = ref.shape[1] if group == 1 else ref.shape[0]
-        quart = total // 4
-
-        def rows(q, off, size):
-            return pl.ds(pl.multiple_of(q * quart + off, 16), size)
-
-        base = which * 7
-        out = []
-        for d in range(1, 4):
-            out.append(
-                remote(
-                    block_of(ref, group, rows(quarter, 0, quart), 0, 1),
-                    block_of(ref, group, rows(quarter, 0, quart), d, d + 1),
-                    wsend.at[base + d - 1],
-                    wrecv.at[base + d - 1],
-                    tp_peer(d),
-                )
-            )
-        for e, peer in enumerate((2, 4)):
-            piece = block_of(ref, group, rows(quarter, e * (quart // 2), quart // 2), 1, 4)
-            out.append(remote(piece, piece, wsend.at[base + 3 + e], wrecv.at[base + 3 + e], node_peer(peer)))
-        for e, q in enumerate((quarter, other)):
-            piece = block_of(ref, group, rows(q, 0, quart), 1, 4)
-            out.append(remote(piece, piece, wsend.at[base + 5 + e], wrecv.at[base + 5 + e], node_peer(1)))
-        return out
-
-    copies_in, copies_od, copies_up = weight_copies(0), weight_copies(1), weight_copies(2)
-
-    def step_z(copies):
-        for cp in copies[0:3]:
-            cp.start()
-
-    def step_plane(copies):
-        for cp in copies[0:3]:
-            cp.wait()
-        for cp in copies[3:6]:
-            cp.start()
-
-    def step_core(copies):
-        for cp in copies[3:5]:
-            cp.wait()
-        copies[6].start()
-
-    def step_end(copies):
-        for cp in copies[5:7]:
-            cp.wait()
+    class Fetch:
+        def __init__(self, ref, slots, base):
+            total = ref.shape[1] if len(ref.shape) == 3 else ref.shape[0]
+            part = total // 8
+            d0, d1 = slots
+            sems = iter(range(base, base + 8))
+
+            def go(src, dst, peer):
+                k = next(sems)
+                return remote(src, dst, wsend.at[k], wrecv.at[k], peer)
+
+            own = eighth * part
+            self.z = [
+                go(weight_block(ref, own, part, 0, 1), weight_block(ref, own, part, d, d + 1), tp_peer(d))
+                for d in range(d0, d1)
+            ]
+            mine = weight_block(ref, own, part, d0, d1)
+            self.plane = [go(mine, mine, node_peer(2 * e)) for e in (1, 2, 3)]
+            lot = weight_block(ref, c * (total // 2), total // 2, d0, d1)
+            self.core = [go(lot, lot, node_peer(1))]
+
+        def start_z(self):
+            for cp in self.z:
+                cp.start()
+
+        def start_plane(self):
+            for cp in self.z:
+                cp.wait()
+            for cp in self.plane:
+                cp.start()
+
+        def start_core(self):
+            for cp in self.plane:
+                cp.wait()
+            self.core[0].start()
+
+        def end(self):
+            self.core[0].wait()
+
+    fetch_in = [None] + [Fetch(w_in, (d, d + 1), 8 * (d - 1)) for d in (1, 2, 3)]
+    fetch_od = Fetch(w_od, (1, 4), 24)
+    fetch_up = Fetch(w_up, (1, 4), 32)
 
     for i in (0, 1, 2):
         local[i].wait()
-    step_z(copies_in)
-
-    gain1 = g1_ref[...].astype(F32)
-    shift1 = s1_ref[...].astype(F32)
-    gain2 = g2_ref[...].astype(F32)
-    shift2 = s2_ref[...].astype(F32)
-    hopw = hw_ref[...].astype(F32)
+    for d in (1, 2, 3):
+        fetch_in[d].start_z()
+
+    gain1 = tokens_of(g1_ref)
+    shift1 = tokens_of(s1_ref)
+    gain2 = tokens_of(g2_ref)
+    shift2 = tokens_of(s2_ref)
+    hopw = tokens_of(hw_ref)
+    hop16 = jnp.broadcast_to(hopw, (16, width)).astype(BF16)
 
     eye = iota((TILE, TILE), 0) == iota((TILE, TILE), 1)
     ones = jnp.ones((TILE, TILE), BF16)
     lane8 = iota((HOPS, TILE), 1)
     block8 = lane8 // HOPS
-    left = iota((TILE, TILE), 1) < HEAD
+    eye16 = eye.astype(F32).astype(BF16)
+    emask[...] = (iota((TILE, TILE), 0) // HOPS == iota((TILE, TILE), 1) // HOPS).astype(F32).astype(BF16)
+    first = (iota((2 * TILE, TILE), 0) < TILE) == (iota((2 * TILE, TILE), 1) < HEAD)
+    pmask[...] = first.astype(F32).astype(BF16)
     nodes_chunk = CHUNK // HOPS
     spread_c = (iota((CHUNK, nodes_chunk), 0) // HOPS == iota((CHUNK, nodes_chunk), 1)).astype(F32).astype(BF16)
 
@@ -327,74 +323,97 @@
 
     lax.fori_loop(0, chunks, norm_one, 0)
 
-    for i in (4, 5, 6, 7):
-        local[i].wait()
-    step_plane(copies_in)
-    step_z(copies_od)
-    step_z(copies_up)
-    step_core(copies_in)
-    step_end(copies_in)
-
-    def project(i, carry):
-        r = rows_of(i, CHUNK)
-        out = mm(n1[r, :], w_in[...])
-        for d in range(4):
-            base = d * 3 * qw
-            qkv[r, base : base + qw] = (out[:, base : base + qw] * (HEAD**-0.5)).astype(BF16)
-            qkv[r, base + qw : base + 3 * qw] = out[:, base + qw : base + 3 * qw].astype(BF16)
-        return carry
-
-    lax.fori_loop(0, chunks, project, 0)
-    step_plane(copies_od)
-    step_plane(copies_up)
+    def project(d):
+        base = d * 3 * qw
+
+        def step(i, carry):
+            r = rows_of(i, CHUNK)
+            out = mm(n1[r, :], w_in[:, base : base + 3 * qw])
+            qkv[r, base : base + qw] = (out[:, 0:qw] * (HEAD**-0.5)).astype(BF16)
+            qkv[r, base + qw : base + 3 * qw] = out[:, qw:].astype(BF16)
+            return carry
+
+        lax.fori_loop(0, chunks, step, 0)
 
     def pair(x):
-        zero = jnp.zeros_like(x)
-        return jnp.concatenate([jnp.where(left, x, zero), jnp.where(left, zero, x)], axis=0)
+        return jnp.concatenate([x, x], axis=0) * pmask[...]
+
+    bits = [((lane8 // (HOPS << b)) % 2) == 1 for b in range(4)]
 
     def compact(x):
         out = []
         for h in range(2):
             x3 = x[:, h * TILE : (h + 1) * TILE].reshape(TILE // HOPS, HOPS, TILE)
-            acc = x3[0]
-            for r in range(1, TILE // HOPS):
-                acc = jnp.where(block8 == r, x3[r], acc)
-            out.append(acc)
+            parts = [x3[r] for r in range(TILE // HOPS)]
+            for b in range(4):
+                parts = [jnp.where(bits[b], parts[2 * m + 1], parts[2 * m]) for m in range(len(parts) // 2)]
+            out.append(parts[0])
         return out
 
-    def expand(pairs):
-        cols = []
-        for x in pairs:
-            zero = jnp.zeros_like(x)
-            cols.append(
-                jnp.concatenate([jnp.where(block8 == r, x, zero) for r in range(TILE // HOPS)], axis=0).astype(BF16)
-            )
-        return jnp.concatenate(cols, axis=1)
-
-    def attend(i, carry):
-        r = rows_of(i, TILE)
-        keep = mask_ref[pl.ds(i, 1), :].astype(F32) > 0.5
-        for d in range(4):
-            base = d * 3 * qw
-            q = qkv[r, base : base + qw]
-            k = qkv[r, base + qw : base + 2 * qw]
-            v = qkv[r, base + 2 * qw : base + 3 * qw]
-            scores = compact(mm_rt(q, pair(k)))
-            probs = []
-            for h in range(2):
-                s = jnp.where(keep, scores[h], NEGATIVE)
-                e = jnp.exp(s - seg8(s, jnp.maximum, lane8))
-                p = e / seg8(e, jnp.add, lane8)
-                pn[i * 8 + 2 * d + h] = p
-                probs.append(p)
-            ctx[r, d * qw : (d + 1) * qw] = mm(expand(probs), pair(v)).astype(BF16)
-        return carry
-
-    lax.fori_loop(0, tiles, attend, 0)
-    step_core(copies_od)
-    step_core(copies_up)
-    step_end(copies_od)
-    step_end(copies_up)
+    def expand(x):
+        twice = jnp.concatenate([x, x], axis=0).astype(BF16)
+        return jnp.concatenate([twice] * (TILE // 16), axis=0) * emask[...]
+
+    together = 4
+
+    def attend(d):
+        base = d * 3 * qw
+
+        def step(i, carry):
+            at = [i * together + m for m in range(together)]
+            rs = [rows_of(a, TILE) for a in at]
+            q2 = [pair(qkv[r, base : base + qw]) for r in rs]
+            scores = [compact(mm_rt(qkv[r, base + qw : base + 2 * qw], x)) for r, x in zip(rs, q2, strict=True)]
+            wide = []
+            for m, a in enumerate(at):
+                keep = mt[a] > 0.5
+                for h in range(2):
+                    wide.append(jnp.where(keep, scores[m][h], NEGATIVE))
+            peaks = [jnp.max(x, axis=0, keepdims=True) for x in wide]
+            wide = [jnp.exp(x - y) for x, y in zip(wide, peaks, strict=True)]
+            totals = [jnp.sum(x, axis=0, keepdims=True) for x in wide]
+            wide = [x / y for x, y in zip(wide, totals, strict=True)]
+            for m, a in enumerate(at):
+                for h in range(2):
+                    pn[a * 8 + 2 * d + h] = wide[2 * m + h]
+            turned = [
+                mm_rt(eye16, jnp.concatenate([expand(wide[2 * m]), expand(wide[2 * m + 1])], axis=0)).astype(BF16)
+                for m in range(together)
+            ]
+            v2 = [pair(qkv[r, base + 2 * qw : base + 3 * qw]) for r in rs]
+            for m, r in enumerate(rs):
+                ctx[r, d * qw : (d + 1) * qw] = mm(turned[m], v2[m]).astype(BF16)
+            return carry
+
+        lax.fori_loop(0, tiles // together, step, 0)
+
+    project(0)
+    fetch_in[1].start_plane()
+    attend(0)
+    for i in (4, 5, 6, 7):
+        local[i].wait()
+    fetch_in[2].start_plane()
+    fetch_in[3].start_plane()
+    fetch_od.start_z()
+    fetch_up.start_z()
+    fetch_in[1].start_core()
+    fetch_in[1].end()
+    project(1)
+    fetch_in[2].start_core()
+    attend(1)
+    fetch_in[2].end()
+    fetch_in[3].start_core()
+    fetch_od.start_plane()
+    project(2)
+    attend(2)
+    fetch_in[3].end()
+    fetch_up.start_plane()
+    project(3)
+    fetch_od.start_core()
+    attend(3)
+    fetch_od.end()
+    fetch_up.start_core()
+    fetch_up.end()
 
     ow = w_od.shape[1]
     down_rows = ow - qw
@@ -477,7 +496,7 @@
 
     def small_products():
         drdown = mm_rt(cot[...], w_down()).astype(BF16)
-        hopdown = mm_rt(jnp.broadcast_to(hw_ref[...], (16, width)), w_down()).astype(BF16)
+        hopdown = mm_rt(hop16, w_down()).astype(BF16)
         for i in range(chunks):
             piece = drdown[i * nodes_chunk : (i + 1) * nodes_chunk]
             ab[i, 0:nodes_chunk] = piece
@@ -515,7 +534,6 @@
         mix = mix.reshape(CHUNK, TILE).astype(BF16)
 
         dr = cot[rows_of(i, nodes_chunk), :]
-        hop16 = jnp.broadcast_to(hw_ref[...], (16, width))
         rest = jnp.zeros((TILE - 2 * nodes_chunk - 16, width), BF16)
         dh = jnp.concatenate([dr, dr, hop16, rest], axis=0)
         grad_layer = mm(mix, dh)
@@ -552,91 +570,80 @@
         0, chunks, back_one, (zero8, zero8, zero8, jnp.zeros((HOPS, zed.shape[1]), F32))
     )
 
-    groups = []
-    sets = [
-        (g_dn, False, rc_dn, rz_dn, sm_dn, rp_dn, fin_dn_ref),
-        (g_up, True, rc_up, rz_up, sm_up, rp_up, fin_up_ref),
-        (g_out, False, rc_out, rz_out, sm_out, rp_out, fin_out_ref),
-        (g_in, True, rc_in, rz_in, sm_in, rp_in, fin_in_ref),
+    def group(at, array, wide, cols, rc, rp, rz, final):
+        return Group(array, wide, cols, rc, rp, rz, final, gsend, grecv, at * (11 + len(extra)))
+
+    dn = group(0, g_dn, False, (0, 4), rc_dn, rp_dn, rz_dn, fin_dn_ref)
+    up = group(1, g_up, True, (0, 4), rc_up, rp_up, rz_up, fin_up_ref)
+    ot = group(2, g_out, False, (0, 4), rc_out, rp_out, rz_out, fin_out_ref)
+    qk = [
+        group(3 + d, g_in, True, (d, d + 1), rc_in.at[d], rp_in.at[d], rz_in, fin_in_ref) for d in range(4)
     ]
-    for i, item in enumerate(sets):
-        groups.append(Group(*item, gsend.at[i], grecv.at[i]))
-    dn, up, ot, qk = groups
-
-    def core_copy(g):
-        return remote(g.half(1 - c), g.recv_core, g.send.at[0], g.recv.at[0], node_peer(1))
-
-    def z_copies(g):
-        return [
-            remote(g.slot(c, d), g.recv_z.at[d - 1], g.send.at[d], g.recv.at[d], tp_peer(d)) for d in range(1, 4)
-        ]
-
-    def plane_peer_piece(e):
+
+    def plane_of(e):
         out = plane
         for b in range(2):
             if (e >> b) & 1:
                 out = out + (1 << b) * (1 - 2 * ((plane // (1 << b)) % 2))
         return out
 
+    def core_copy(g):
+        s, r = g.sems(0)
+        return remote(g.block(g.rows(1 - c)), g.recv_core, s, r, node_peer(1))
+
     def plane_copies(g):
         return [
-            remote(
-                g.piece(g.part, plane_peer_piece(e)),
-                g.recv_plane.at[e - 1],
-                g.send.at[3 + e],
-                g.recv.at[3 + e],
-                node_peer(2 * e),
-            )
-            for e in range(1, 4)
+            remote(g.block(g.rows(c, plane_of(e))), g.recv_plane.at[e - 1], *g.sems(e), node_peer(2 * e))
+            for e in (1, 2, 3)
         ]
 
+    def z_copies(g, slots):
+        return [
+            remote(g.slot(g.rows(c, plane), d), g.recv_z.at[d - 1], *g.sems(3 + d), tp_peer(d)) for d in slots
+        ]
+
     def final_copies(g):
-        mine = g.piece(g.final, plane, c * g.half_rows)
-        return [remote(mine, mine, g.send.at[6 + e], g.recv.at[6 + e], node_peer(2 * e)) for e in range(1, 4)]
+        mine = g.final.at[g.rows(c, plane)]
+        return [remote(mine, mine, *g.sems(6 + e), node_peer(2 * e)) for e in (1, 2, 3)]
 
     def last_copy(g):
-        rows = g.final.at[pl.ds(pl.multiple_of(c * g.half_rows, g.half_rows), g.half_rows)]
-        return remote(rows, rows, g.send.at[10], g.recv.at[10], node_peer(1))
+        mine = g.final.at[g.rows(c)]
+        return remote(mine, mine, *g.sems(10), node_peer(1))
 
     def go_core(g):
         core_copy(g).start()
 
-    def go_z(g):
+    def go_plane(g):
         core_copy(g).wait()
-        mine = g.half(c)
+        mine = g.block(g.rows(c))
         mine[...] = (mine[...].astype(F32) + g.recv_core[...].astype(F32)).astype(BF16)
-        for cp in z_copies(g):
+        for cp in plane_copies(g):
             cp.start()
 
-    def go_plane(g):
-        for cp in z_copies(g):
+    def go_z(g, slots):
+        for cp in plane_copies(g):
             cp.wait()
-        total = g.slot(c, 0)[...].astype(F32)
+        mine = g.block(g.rows(c, plane))
+        total = mine[...].astype(F32)
+        for e in range(3):
+            total = total + g.recv_plane[e].astype(F32)
+        mine[...] = total.astype(BF16)
+        for cp in z_copies(g, slots):
+            cp.start()
+
+    def go_final(g, waits):
+        for cp in waits:
+            cp.wait()
+        total = g.slot(g.rows(c, plane), 0)[...].astype(F32)
         for d in range(3):
             total = total + g.recv_z[d].astype(F32)
-        g.part[...] = total.astype(BF16)
-        for cp in plane_copies(g):
-            cp.start()
-
-    def go_final(g):
-        for cp in plane_copies(g):
-            cp.wait()
-        total = g.piece(g.part, plane)[...].astype(F32)
-        for e in range(3):
-            total = total + g.recv_plane[e].astype(F32)
         for j, b in enumerate(extra):
-            g.recv_plane[3 + 2 * j] = total.astype(BF16)
-            cp = remote(
-                g.recv_plane.at[3 + 2 * j],
-                g.recv_plane.at[4 + 2 * j],
-                g.send.at[11 + j],
-                g.recv.at[11 + j],
-                node_peer(1 << b),
-            )
+            g.recv_z[3 + 2 * j] = total.astype(BF16)
+            cp = remote(g.recv_z.at[3 + 2 * j], g.recv_z.at[4 + 2 * j], *g.sems(11 + j), node_peer(1 << b))
             cp.start()
             cp.wait()
-            total = total + g.recv_plane[4 + 2 * j].astype(F32)
-        g.piece(g.final, plane, c * g.half_rows)[...] = total.astype(BF16)
+            total = total + g.recv_z[4 + 2 * j].astype(F32)
+        g.final.at[g.rows(c, plane)][...] = total.astype(BF16)
         for cp in final_copies(g):
             cp.start()
 
@@ -648,55 +655,63 @@
     def finish(g):
         last_copy(g).wait()
 
+    every = (1, 2, 3)
+
     zed[rows_here // HOPS :, :] = jnp.concatenate([zed_sum, jnp.zeros_like(zed_sum)], axis=0).astype(BF16)
-    drh = jnp.concatenate([cot[...], jnp.broadcast_to(hw_ref[...], (16, width))], axis=0)
+    drh = jnp.concatenate([cot[...], hop16], axis=0)
     g_dn[...] = mm_lt(zed[...], drh).astype(BF16).reshape(g_dn.shape)
     go_core(dn)
     g_up[...] = mm_lt(n2[...], gbef[...]).astype(BF16)
     go_core(up)
-    go_z(dn)
+    go_plane(dn)
     g_out[...] = mm_lt(ctx[...], datt[...]).astype(BF16).reshape(g_out.shape)
     go_core(ot)
-    go_z(up)
-
-    def attend_back(i, carry):
-        r = rows_of(i, TILE)
-        keep = mt[i] > 0.5
-        for d in range(4):
-            base = d * 3 * qw
-            q = qkv[r, base : base + qw]
-            k = qkv[r, base + qw : base + 2 * qw]
-            v = qkv[r, base + 2 * qw : base + 3 * qw]
-            do = dctx[r, d * qw : (d + 1) * qw]
-            k2, q2, v2, do2 = pair(k), pair(q), pair(v), pair(do)
-            grad_p = compact(mm_rt(do, v2))
-            ds = []
-            for h in range(2):
-                p = pn[i * 8 + 2 * d + h]
-                ds.append(p * (grad_p[h] - seg8(p * grad_p[h], jnp.add, lane8)))
-            dqkv[r, base : base + qw] = (mm(expand(ds), k2) * (HEAD**-0.5)).astype(BF16)
-            scores = compact(mm_rt(k, q2))
-            grad_pt = compact(mm_rt(v, do2))
-            probs, dst = [], []
-            for h in range(2):
-                s = jnp.where(keep, scores[h], NEGATIVE)
-                e = jnp.exp(s - jnp.max(s, axis=0, keepdims=True))
-                p = e / jnp.sum(e, axis=0, keepdims=True)
-                probs.append(p)
-                dst.append(p * (grad_pt[h] - jnp.sum(p * grad_pt[h], axis=0, keepdims=True)))
-            dqkv[r, base + qw : base + 2 * qw] = mm(expand(dst), q2).astype(BF16)
-            dqkv[r, base + 2 * qw : base + 3 * qw] = mm(expand(probs), do2).astype(BF16)
-        return carry
-
-    lax.fori_loop(0, tiles, attend_back, 0)
-    go_z(ot)
-    go_plane(dn)
     go_plane(up)
-    g_in[...] = mm_lt(n1[...], dqkv[...]).astype(BF16)
-    go_core(qk)
+
+    def attend_back(d):
+        base = d * 3 * qw
+
+        def step(i, carry):
+            at = [i * together + m for m in range(together)]
+            rs = [rows_of(a, TILE) for a in at]
+            do2 = [pair(dctx[r, d * qw : (d + 1) * qw]) for r in rs]
+            grads = [
+                compact(mm_rt(qkv[r, base + 2 * qw : base + 3 * qw], x)) for r, x in zip(rs, do2, strict=True)
+            ]
+            probs = [[pn[a * 8 + 2 * d + h] for h in range(2)] for a in at]
+            probs_wide = [jnp.concatenate([expand(p) for p in ps], axis=1) for ps in probs]
+            for m, r in enumerate(rs):
+                dqkv[r, base + 2 * qw : base + 3 * qw] = mm(probs_wide[m], do2[m]).astype(BF16)
+            inner = [[jnp.sum(p * g, axis=0, keepdims=True) for p, g in zip(*x, strict=True)] for x in zip(probs, grads, strict=True)]
+            back = [
+                [expand(probs[m][h] * (grads[m][h] - inner[m][h])) for h in range(2)] for m in range(together)
+            ]
+            q2 = [pair(qkv[r, base : base + qw]) for r in rs]
+            for m, r in enumerate(rs):
+                wide = jnp.concatenate(back[m], axis=1)
+                dqkv[r, base + qw : base + 2 * qw] = mm(wide, q2[m]).astype(BF16)
+            turned = [mm_rt(eye16, jnp.concatenate(x, axis=0)).astype(BF16) for x in back]
+            k2 = [pair(qkv[r, base + qw : base + 2 * qw]) for r in rs]
+            for m, r in enumerate(rs):
+                dqkv[r, base : base + qw] = (mm(turned[m], k2[m]) * (HEAD**-0.5)).astype(BF16)
+            return carry
+
+        lax.fori_loop(0, tiles // together, step, 0)
+        g_in[:, base : base + 3 * qw] = mm_lt(n1[...], dqkv[:, base : base + 3 * qw]).astype(BF16)
+        go_core(qk[d])
+
+    attend_back(3)
     go_plane(ot)
-    go_final(dn)
-    go_final(up)
+    go_z(dn, every)
+    attend_back(2)
+    go_plane(qk[3])
+    go_z(up, every)
+    go_z(ot, every)
+    attend_back(1)
+    go_plane(qk[2])
+    go_z(qk[3], (3,))
+    go_final(dn, z_copies(dn, every))
+    attend_back(0)
 
     def back_two(i, carry):
         gain_acc, shift_acc = carry
@@ -712,8 +727,15 @@
         gtok_ref[r, :] = (gl[r, :] + back).astype(BF16)
         return gain_acc, shift_acc
 
-    go_z(qk)
-    gain_one, shift_one = lax.fori_loop(0, chunks, back_two, (zero8, zero8))
+    go_plane(qk[1])
+    go_z(qk[2], (2,))
+    go_final(up, z_copies(up, every))
+    go_plane(qk[0])
+    norm_sums = lax.fori_loop(0, chunks // 2, back_two, (zero8, zero8))
+    go_z(qk[1], (1,))
+    go_final(ot, z_copies(ot, every))
+    go_last(dn)
+    gain_one, shift_one = lax.fori_loop(chunks // 2, chunks, back_two, norm_sums)
 
     def fold8(x):
         return jnp.sum(x, axis=0, keepdims=True)
@@ -723,22 +745,34 @@
     )
 
     def rest_of():
-        go_final(ot)
-        go_last(dn)
-        go_last(up)
-        go_plane(qk)
+        go_z(qk[0], ())
+        go_final(qk[0], [z_copies(qk[d], (d,))[0] for d in every])
 
     copies, total_small = reduce_all(small, sv_one, sv_nodes, sv_tp, bsend, brecv, rest_of)
+    go_last(up)
     go_last(ot)
-    go_final(qk)
+    for cp in copies:
+        cp.wait()
+    small_ref[...] = total_small()
+    go_last(qk[0])
     finish(dn)
     finish(up)
     finish(ot)
-    for cp in copies:
-        cp.wait()
-    small_ref[...] = total_small()
-    go_last(qk)
-    finish(qk)
+    finish(qk[0])
+
+
+def results_kernel(readout, gtok, small, fin_in, fin_out, fin_up, fin_dn, o_read, o_tok, o_g1, o_s1, o_q, o_k, o_v, o_out, o_g2, o_s2, o_up, o_dn, o_hop):
+    o_tok[...] = gtok[...]
+    o_read[...] = readout[...]
+    width = small.shape[1]
+    for i, o in enumerate((o_g1, o_s1, o_g2, o_s2, o_hop)):
+        o[...] = small[i : i + 1, :].reshape(width)
+    qw = o_q.shape[1]
+    for i, o in enumerate((o_q, o_k, o_v)):
+        o[...] = fin_in[:, i * qw : (i + 1) * qw].astype(F32)
+    o_out[...] = fin_out[...].astype(F32)
+    o_up[...] = fin_up[...].astype(F32)
+    o_dn[...] = fin_dn[...].astype(F32)
 
 
 def shards(
@@ -786,6 +820,8 @@
         v(rows, 4 * uw),
         v(rows, 4 * uw),
         v(rows, width, dtype=F32),
+        v(TILE, TILE),
+        v(2 * TILE, TILE),
         v(rows, TILE, dtype=F32),
         v(tiles, HOPS, TILE, dtype=F32),
         v(rows, TILE, dtype=F32),
@@ -805,15 +841,11 @@
         v(half, 4 * uw),
         v(4, uw // 2, width),
         v(4, qw // 2, width),
-        v(half, 12 * qw),
-        v(3, half, uw),
-        v(3, uw // 2, width),
-        v(3, qw // 2, width),
-        v(3, half, 3 * qw),
-        v(half, uw),
-        v(uw // 2, width),
-        v(qw // 2, width),
-        v(half, 3 * qw),
+        v(4, half, 3 * qw),
+        v(3, half // 4, 4 * uw),
+        v(3, 4, uw // 8, width),
+        v(3, 4, qw // 8, width),
+        v(4, 3, half // 4, 3 * qw),
         v(3 + 2 * extra, half // 4, uw),
         v(3 + 2 * extra, uw // 8, width),
         v(3 + 2 * extra, qw // 8, width),
@@ -825,10 +857,10 @@
         v(7 + extra, 8, width, dtype=F32),
         v(3, 8, width, dtype=F32),
         pltpu.SemaphoreType.DMA((8,)),
-        pltpu.SemaphoreType.DMA((21,)),
-        pltpu.SemaphoreType.DMA((21,)),
-        pltpu.SemaphoreType.DMA((4, 11 + extra)),
-        pltpu.SemaphoreType.DMA((4, 11 + extra)),
+        pltpu.SemaphoreType.DMA((40,)),
+        pltpu.SemaphoreType.DMA((40,)),
+        pltpu.SemaphoreType.DMA((7 * (11 + extra),)),
+        pltpu.SemaphoreType.DMA((7 * (11 + extra),)),
         pltpu.SemaphoreType.DMA((10 + extra,)),
         pltpu.SemaphoreType.DMA((10 + extra,)),
         pltpu.SemaphoreType.DMA((10 + extra,)),
@@ -843,7 +875,6 @@
         jax.ShapeDtypeStruct((width, uw), BF16),
         jax.ShapeDtypeStruct((uw, width), BF16),
     ]
-    line = (1, width)
     readout, gtok, small, fin_in, fin_out, fin_up, fin_dn = pl.pallas_call(
         functools.partial(kernel, nn),
         out_shape=outs,
@@ -858,35 +889,42 @@
         tokens,
         hop_mask.reshape(tiles, TILE),
         graph_ids.reshape(1, nodes),
-        norm1_gain.reshape(line),
-        norm1_shift.reshape(line),
+        norm1_gain,
+        norm1_shift,
         w_query,
         w_key,
         w_value,
         w_out,
-        norm2_gain.reshape(line),
-        norm2_shift.reshape(line),
+        norm2_gain,
+        norm2_shift,
         w_up,
         w_down,
-        hop_weight.reshape(line),
+        hop_weight,
         cotangent,
     )
-    fin_in = fin_in.astype(F32)
-    return (
-        readout,
-        gtok,
-        small[0],
-        small[1],
-        fin_in[:, 0:qw],
-        fin_in[:, qw : 2 * qw],
-        fin_in[:, 2 * qw :],
-        fin_out.astype(F32),
-        small[2],
-        small[3],
-        fin_up.astype(F32),
-        fin_dn.astype(F32),
-        small[4],
-    )
+    line = jax.ShapeDtypeStruct((width,), F32)
+    square = jax.ShapeDtypeStruct((width, qw), F32)
+    return pl.pallas_call(
+        results_kernel,
+        out_shape=[
+            jax.ShapeDtypeStruct((nodes, width), BF16),
+            jax.ShapeDtypeStruct((rows, width), BF16),
+            line,
+            line,
+            square,
+            square,
+            square,
+            jax.ShapeDtypeStruct((qw, width), F32),
+            line,
+            line,
+            jax.ShapeDtypeStruct((width, uw), F32),
+            jax.ShapeDtypeStruct((uw, width), F32),
+            line,
+        ],
+        in_specs=[vm] * 7,
+        out_specs=[vm] * 13,
+        name="results",
+    )(readout, gtok, small, fin_in, fin_out, fin_up, fin_dn)
 
 
 def solution(mesh):

time: 140 us -> 102 us (0.73)
  Pallas kernels: 125 us -> 101 us
  local copies, waits for them, and re-layouts: 9.42 us -> 0 us
  other arithmetic: 2.41 us -> 0 us
    pallas_call x1, Pallas kernels: 125 us -> 97.4 us  [shards(): pl.pallas_call(functools.partial(kernel, nn), out_shape=outs, in_specs=[h...]
    slice x2 -> x0, local copies, waits for them, and re-layouts: 3.48 us -> none  [the longest x1 1.97 us: shards(): fin_in[:, 2 * qw:]]
    pallas_call x0 -> x1, Pallas kernels: none -> 3.34 us  [shards(): pl.pallas_call(results_kernel, out_shape=[jax.ShapeDtypeStruct((nodes, wi...]
    unnamed x22 -> x0, local copies, waits for them, and re-layouts: 3.04 us -> none
    reshape x5 -> x0, local copies, waits for them, and re-layouts: 2.9 us -> none  [the longest x1 0.58 us: shards(): norm2_shift.reshape(line)]
    convert_element_type x3 -> x0, other arithmetic: 2.41 us -> none  [the longest x1 0.85 us: shards(): fin_dn.astype(F32)]
where the time goes in v3:
time: 102 us; the launch traced here: 101 us
  Pallas kernels  101 us (99%)
    pallas_call x1, Pallas kernels, shards(): pl.pallas_call(functools.partial(kernel, nn), out_shape=outs, in_specs=[h...  97.4 us
    pallas_call x1, Pallas kernels, shards(): pl.pallas_call(results_kernel, out_shape=[jax.ShapeDtypeStruct((nodes, wi...  3.34 us

profile of v3, /device:TPU:0, one launch (start us, length us, event | category | flops | bytes accessed | tf_op | source)
XLA Modules:
  0.0 101.4 jit_solution(11429534138854121701)
XLA Ops:
  0.7 97.4 %layer.1 = (bf16[128,512]{1,0:T(8,128)(2,1)}, bf16[1024,512]{1,0:T(8,128)(2,1)}, f32[8,512]{1,0:T(8,128)}, bf16[512,384]{1,0:T(8,128)(2,1)}, bf16[128,512]{1,0:T...) custom-call(bf16[1024,512]{1,0:T(8,128)(2,1)} %tok_hbm.1, s32[8,128]{1,0:T(8,128)} %bitcast.2, ...), custom_call_target="tpu_custom_call" | custom-call | tf_op jit(solution)/shard_map/layer/pallas_call | solution.py:878
  98.0 3.3 %results.1 = (bf16[128,512]{1,0:T(8,128)(2,1)}, bf16[1024,512]{1,0:T(8,128)(2,1)}, f32[512]{0:T(512)}, f32[512]{0:T(512)}, f32[512,128]{1,0:T(8,128)}, /*index=5...) custom-call(bf16[128,512]{1,0:T(8,128)(2,1)} %get-tuple-element.20.r, ...), custom_call_target="tpu_custom_call" | custom-call | tf_op jit(solution)/shard_map/results/pallas_call | solution.py:907

commit v4 on v3

--- a/solution.py
+++ b/solution.py
@@ -59,11 +59,12 @@
 
 
 class Group:
-    def __init__(self, array, wide, cols, recv_core, recv_plane, recv_z, final, send, recv, base):
+    def __init__(self, array, wide, cols, recv_core, recv_plane, recv_z, final, more, send, recv, base):
         self.array, self.wide = array, wide
         self.cols = cols
         self.recv_core, self.recv_plane, self.recv_z = recv_core, recv_plane, recv_z
         self.final = final
+        self.more = more
         self.send, self.recv, self.base = send, recv, base
         rows = final.shape[0]
         self.half_rows = rows // 2
@@ -115,7 +116,8 @@
     fin_dn_ref,
     w_in,
     w_up,
-    w_od,
+    w_ot,
+    w_dn,
     tok,
     cot,
     n1,
@@ -157,6 +159,10 @@
     rz_dn,
     rz_out,
     rz_in,
+    mo_up,
+    mo_dn,
+    mo_out,
+    mo_in,
     ar_one,
     ar_nodes,
     ar_tp,
@@ -180,6 +186,7 @@
     c = n % 2
     plane = (n // 2) % 4
     eighth = 4 * c + plane
+    side = (plane % 2 + plane // 2) % 2
     extra = [b for b in range(3, 12) if (1 << b) < nn]
 
     def node_peer(k):
@@ -209,8 +216,8 @@
         pltpu.make_async_copy(wk_hbm, w_in.at[:, qw : 2 * qw], lsem.at[1]),
         pltpu.make_async_copy(wv_hbm, w_in.at[:, 2 * qw : 3 * qw], lsem.at[2]),
         pltpu.make_async_copy(tok_hbm, tok, lsem.at[3]),
-        pltpu.make_async_copy(wo_hbm, w_od.at[0, 0:qw], lsem.at[4]),
-        pltpu.make_async_copy(wd_hbm, w_od.at[0, qw:], lsem.at[5]),
+        pltpu.make_async_copy(wo_hbm, w_ot.at[0], lsem.at[4]),
+        pltpu.make_async_copy(wd_hbm, w_dn.at[0], lsem.at[5]),
         pltpu.make_async_copy(wu_hbm, w_up.at[:, 0 : wu_hbm.shape[1]], lsem.at[6]),
         pltpu.make_async_copy(cot_hbm, cot, lsem.at[7]),
     ]
@@ -232,9 +239,8 @@
         return ref.at[rows, d0 * w : d1 * w]
 
     class Fetch:
-        def __init__(self, ref, slots, base):
+        def __init__(self, ref, slots, base, halves=False):
             total = ref.shape[1] if len(ref.shape) == 3 else ref.shape[0]
-            part = total // 8
             d0, d1 = slots
             sems = iter(range(base, base + 8))
 
@@ -242,15 +248,23 @@
                 k = next(sems)
                 return remote(src, dst, wsend.at[k], wrecv.at[k], peer)
 
-            own = eighth * part
+            def rows(off, size):
+                return weight_block(ref, off, size, d0, d1)
+
+            part = total // 4 if halves else total // 8
+            own = (2 * side + c if halves else eighth) * part
             self.z = [
                 go(weight_block(ref, own, part, 0, 1), weight_block(ref, own, part, d, d + 1), tp_peer(d))
                 for d in range(d0, d1)
             ]
-            mine = weight_block(ref, own, part, d0, d1)
-            self.plane = [go(mine, mine, node_peer(2 * e)) for e in (1, 2, 3)]
-            lot = weight_block(ref, c * (total // 2), total // 2, d0, d1)
-            self.core = [go(lot, lot, node_peer(1))]
+            if halves:
+                some = [rows(own + e * (part // 2), part // 2) for e in range(2)]
+                self.plane = [go(x, x, node_peer(2 << e)) for e, x in enumerate(some)]
+                lots = [rows(own, part), rows((2 * (1 - side) + c) * part, part)]
+            else:
+                self.plane = [go(rows(own, part), rows(own, part), node_peer(2 * e)) for e in (1, 2, 3)]
+                lots = [rows(c * (total // 2), total // 2)]
+            self.core = [go(x, x, node_peer(1)) for x in lots]
 
         def start_z(self):
             for cp in self.z:
@@ -265,14 +279,17 @@
         def start_core(self):
             for cp in self.plane:
                 cp.wait()
-            self.core[0].start()
+            for cp in self.core:
+                cp.start()
 
         def end(self):
-            self.core[0].wait()
+            for cp in self.core:
+                cp.wait()
 
     fetch_in = [None] + [Fetch(w_in, (d, d + 1), 8 * (d - 1)) for d in (1, 2, 3)]
-    fetch_od = Fetch(w_od, (1, 4), 24)
-    fetch_up = Fetch(w_up, (1, 4), 32)
+    fetch_ot = Fetch(w_ot, (1, 4), 24)
+    fetch_up = Fetch(w_up, (1, 4), 32, halves=True)
+    fetch_dn = Fetch(w_dn, (1, 4), 40)
 
     for i in (0, 1, 2):
         local[i].wait()
@@ -356,7 +373,10 @@
 
     together = 4
 
-    def attend(d):
+    steps = tiles // together
+    mid = steps // 2
+
+    def attend(d, lo, hi):
         base = d * 3 * qw
 
         def step(i, carry):
@@ -385,51 +405,54 @@
                 ctx[r, d * qw : (d + 1) * qw] = mm(turned[m], v2[m]).astype(BF16)
             return carry
 
-        lax.fori_loop(0, tiles // together, step, 0)
-
-    project(0)
+        lax.fori_loop(lo, hi, step, 0)
+
     fetch_in[1].start_plane()
-    attend(0)
     for i in (4, 5, 6, 7):
         local[i].wait()
+    fetch_ot.start_z()
+    project(0)
     fetch_in[2].start_plane()
+    attend(0, 0, mid)
     fetch_in[3].start_plane()
-    fetch_od.start_z()
     fetch_up.start_z()
+    attend(0, mid, steps)
     fetch_in[1].start_core()
+    fetch_ot.start_plane()
     fetch_in[1].end()
     project(1)
     fetch_in[2].start_core()
-    attend(1)
+    attend(1, 0, mid)
+    fetch_in[3].start_core()
+    fetch_dn.start_z()
     fetch_in[2].end()
-    fetch_in[3].start_core()
-    fetch_od.start_plane()
+    attend(1, mid, steps)
     project(2)
-    attend(2)
+    fetch_ot.start_core()
+    attend(2, 0, mid)
+    fetch_up.start_plane()
+    attend(2, mid, steps)
     fetch_in[3].end()
-    fetch_up.start_plane()
     project(3)
-    fetch_od.start_core()
-    attend(3)
-    fetch_od.end()
+    attend(3, 0, mid)
+    fetch_dn.start_plane()
+    attend(3, mid, steps)
+    fetch_ot.end()
     fetch_up.start_core()
     fetch_up.end()
 
-    ow = w_od.shape[1]
-    down_rows = ow - qw
-
     def w_out():
-        return w_od[:, 0:qw, :].reshape(4 * qw, width)
+        return w_ot[...].reshape(4 * qw, width)
 
     def w_down():
-        return w_od[:, qw:ow, :].reshape(4 * down_rows, width)
+        return w_dn[...].reshape(4 * w_dn.shape[1], width)
 
     hop3 = iota((nodes_chunk, HOPS, TILE), 1)
     lane3 = iota((nodes_chunk, HOPS, TILE), 2)
     node3 = iota((nodes_chunk, HOPS, TILE), 0)
     lane_graph = (lane3 % GRAPHS).astype(F32)
 
-    def feed(i, acc):
+    def feed_up(i, carry):
         r = rows_of(i, CHUNK)
         attended = mm(ctx[r, :], w_out())
         x = tok[r, :].astype(F32) + attended
@@ -441,7 +464,11 @@
         value = value.astype(BF16)
         act[r, :] = value
         gp[r, :] = slope.astype(BF16)
-        out = x + mm(value, w_down())
+        return carry
+
+    def feed_down(i, acc):
+        r = rows_of(i, CHUNK)
+        out = res[r, :] + mm(act[r, :], w_down())
         lay[r, :] = out
         dr = mm(spread_c, cot[rows_of(i, nodes_chunk), :])
         logit = jnp.sum(out * hopw, axis=-1, keepdims=True)
@@ -460,7 +487,11 @@
         both = jnp.where(lane3 < GRAPHS, jnp.where(hop3 == 0, 1.0, weight), -direct)
         return acc + jnp.sum(jnp.where(mine, both, 0.0), axis=0)
 
-    sums = lax.fori_loop(0, chunks, feed, jnp.zeros((HOPS, TILE), F32))
+    lax.fori_loop(0, chunks // 2, feed_up, 0)
+    fetch_dn.start_core()
+    lax.fori_loop(chunks // 2, chunks, feed_up, 0)
+    fetch_dn.end()
+    sums = lax.fori_loop(0, chunks, feed_down, jnp.zeros((HOPS, TILE), F32))
 
     def reduce_all(value, one, by_nodes, by_tp, ssem, rsem, overlap=None):
         one[0] = value
@@ -570,15 +601,16 @@
         0, chunks, back_one, (zero8, zero8, zero8, jnp.zeros((HOPS, zed.shape[1]), F32))
     )
 
-    def group(at, array, wide, cols, rc, rp, rz, final):
-        return Group(array, wide, cols, rc, rp, rz, final, gsend, grecv, at * (11 + len(extra)))
-
-    dn = group(0, g_dn, False, (0, 4), rc_dn, rp_dn, rz_dn, fin_dn_ref)
-    up = group(1, g_up, True, (0, 4), rc_up, rp_up, rz_up, fin_up_ref)
-    ot = group(2, g_out, False, (0, 4), rc_out, rp_out, rz_out, fin_out_ref)
+    def group(at, array, wide, cols, rc, rp, rz, final, more):
+        return Group(array, wide, cols, rc, rp, rz, final, more, gsend, grecv, at * (15 + len(extra)))
+
+    dn = group(0, g_dn, False, (0, 4), rc_dn, rp_dn, rz_dn, fin_dn_ref, mo_dn)
+    up = group(1, g_up, True, (0, 4), rc_up, rp_up, rz_up, fin_up_ref, mo_up)
+    ot = group(2, g_out, False, (0, 4), rc_out, rp_out, rz_out, fin_out_ref, mo_out)
     qk = [
-        group(3 + d, g_in, True, (d, d + 1), rc_in.at[d], rp_in.at[d], rz_in, fin_in_ref) for d in range(4)
+        group(3 + d, g_in, True, (d, d + 1), rc_in.at[d], rp_in.at[d], rz_in, fin_in_ref, mo_in) for d in range(4)
     ]
+    every = (1, 2, 3)
 
     def plane_of(e):
         out = plane
@@ -591,34 +623,78 @@
         s, r = g.sems(0)
         return remote(g.block(g.rows(1 - c)), g.recv_core, s, r, node_peer(1))
 
+    def go_core(g):
+        core_copy(g).start()
+
+    def add_core(g):
+        core_copy(g).wait()
+        mine = g.block(g.rows(c))
+        mine[...] = (mine[...].astype(F32) + g.recv_core[...].astype(F32)).astype(BF16)
+
     def plane_copies(g):
         return [
             remote(g.block(g.rows(c, plane_of(e))), g.recv_plane.at[e - 1], *g.sems(e), node_peer(2 * e))
             for e in (1, 2, 3)
         ]
 
+    def go_plane(g):
+        add_core(g)
+        for cp in plane_copies(g):
+            cp.start()
+
+    def cut(g, rows, e):
+        w = (g.cols[1] - g.cols[0]) * g.width // 2
+        base = g.cols[0] * g.width + e * w
+        return g.array.at[rows, base : base + w]
+
+    def fold_copies(g):
+        w = (g.cols[1] - g.cols[0]) * g.width // 2
+        out = []
+        for e in range(2):
+            away = plane_of(1 << e)
+            for m, far in enumerate((away, plane_of(3))):
+                dst = g.recv_plane.at[m, :, e * w : (e + 1) * w]
+                out.append(remote(cut(g, g.rows(c, far), e), dst, *g.sems(11 + 2 * e + m), node_peer(2 << e)))
+        return out
+
+    def go_fold(g):
+        add_core(g)
+        for cp in fold_copies(g):
+            cp.start()
+
+    def fold_last(g):
+        w = (g.cols[1] - g.cols[0]) * g.width // 2
+        out = []
+        for e in range(2):
+            dst = g.recv_plane.at[2, :, e * w : (e + 1) * w]
+            far = plane_of(2 >> e)
+            out.append(remote(cut(g, g.rows(c, far), e), dst, *g.sems(1 + e), node_peer(4 >> e)))
+        return out
+
+    def go_fold_last(g):
+        for cp in fold_copies(g):
+            cp.wait()
+        w = (g.cols[1] - g.cols[0]) * g.width // 2
+        for e in range(2):
+            for m, keep in enumerate((plane, plane_of(2 >> e))):
+                mine = cut(g, g.rows(c, keep), e)
+                got = g.recv_plane[m, :, e * w : (e + 1) * w]
+                mine[...] = (mine[...].astype(F32) + got.astype(F32)).astype(BF16)
+        for cp in fold_last(g):
+            cp.start()
+
+    def go_z_fold(g, slots):
+        for cp in fold_last(g):
+            cp.wait()
+        mine = g.block(g.rows(c, plane))
+        mine[...] = (mine[...].astype(F32) + g.recv_plane[2].astype(F32)).astype(BF16)
+        for cp in z_copies(g, slots):
+            cp.start()
+
     def z_copies(g, slots):
         return [
             remote(g.slot(g.rows(c, plane), d), g.recv_z.at[d - 1], *g.sems(3 + d), tp_peer(d)) for d in slots
         ]
-
-    def final_copies(g):
-        mine = g.final.at[g.rows(c, plane)]
-        return [remote(mine, mine, *g.sems(6 + e), node_peer(2 * e)) for e in (1, 2, 3)]
-
-    def last_copy(g):
-        mine = g.final.at[g.rows(c)]
-        return remote(mine, mine, *g.sems(10), node_peer(1))
-
-    def go_core(g):
-        core_copy(g).start()
-
-    def go_plane(g):
-        core_copy(g).wait()
-        mine = g.block(g.rows(c))
-        mine[...] = (mine[...].astype(F32) + g.recv_core[...].astype(F32)).astype(BF16)
-        for cp in plane_copies(g):
-            cp.start()
 
     def go_z(g, slots):
         for cp in plane_copies(g):
@@ -631,18 +707,62 @@
         for cp in z_copies(g, slots):
             cp.start()
 
+    def z_first(g):
+        return [remote(g.slot(g.rows(c), d), g.recv_z.at[d - 1], *g.sems(3 + d), tp_peer(d)) for d in every]
+
+    def go_z_first(g):
+        add_core(g)
+        for cp in z_first(g):
+            cp.start()
+
+    def own_pieces(g):
+        return [
+            remote(g.slot(g.rows(c, plane_of(e)), 0), g.recv_plane.at[e - 1], *g.sems(e), node_peer(2 * e))
+            for e in (1, 2, 3)
+        ]
+
+    def go_own_plane(g):
+        for cp in z_first(g):
+            cp.wait()
+        mine = g.slot(g.rows(c), 0)
+        total = mine[...].astype(F32)
+        for d in range(3):
+            total = total + g.recv_z[d].astype(F32)
+        mine[...] = total.astype(BF16)
+        for cp in own_pieces(g):
+            cp.start()
+
+    def go_own_final(g):
+        for cp in own_pieces(g):
+            cp.wait()
+        total = g.slot(g.rows(c, plane), 0)[...].astype(F32)
+        for e in range(3):
+            total = total + g.recv_plane[e].astype(F32)
+        share(g, total)
+
+    def final_copies(g):
+        mine = g.final.at[g.rows(c, plane)]
+        return [remote(mine, mine, *g.sems(6 + e), node_peer(2 * e)) for e in (1, 2, 3)]
+
+    def last_copy(g):
+        mine = g.final.at[g.rows(c)]
+        return remote(mine, mine, *g.sems(10), node_peer(1))
+
     def go_final(g, waits):
         for cp in waits:
             cp.wait()
         total = g.slot(g.rows(c, plane), 0)[...].astype(F32)
         for d in range(3):
             total = total + g.recv_z[d].astype(F32)
+        share(g, total)
+
+    def share(g, total):
         for j, b in enumerate(extra):
-            g.recv_z[3 + 2 * j] = total.astype(BF16)
-            cp = remote(g.recv_z.at[3 + 2 * j], g.recv_z.at[4 + 2 * j], *g.sems(11 + j), node_peer(1 << b))
+            g.more[2 * j] = total.astype(BF16)
+            cp = remote(g.more.at[2 * j], g.more.at[2 * j + 1], *g.sems(15 + j), node_peer(1 << b))
             cp.start()
             cp.wait()
-            total = total + g.recv_z[4 + 2 * j].astype(F32)
+            total = total + g.more[2 * j + 1].astype(F32)
         g.final.at[g.rows(c, plane)][...] = total.astype(BF16)
         for cp in final_copies(g):
             cp.start()
@@ -654,8 +774,6 @@
 
     def finish(g):
         last_copy(g).wait()
-
-    every = (1, 2, 3)
 
     zed[rows_here // HOPS :, :] = jnp.concatenate([zed_sum, jnp.zeros_like(zed_sum)], axis=0).astype(BF16)
     drh = jnp.concatenate([cot[...], hop16], axis=0)
@@ -663,10 +781,10 @@
     go_core(dn)
     g_up[...] = mm_lt(n2[...], gbef[...]).astype(BF16)
     go_core(up)
-    go_plane(dn)
+    go_z_first(dn)
     g_out[...] = mm_lt(ctx[...], datt[...]).astype(BF16).reshape(g_out.shape)
     go_core(ot)
-    go_plane(up)
+    go_fold(up)
 
     def attend_back(d):
         base = d * 3 * qw
@@ -700,19 +818,6 @@
         g_in[:, base : base + 3 * qw] = mm_lt(n1[...], dqkv[:, base : base + 3 * qw]).astype(BF16)
         go_core(qk[d])
 
-    attend_back(3)
-    go_plane(ot)
-    go_z(dn, every)
-    attend_back(2)
-    go_plane(qk[3])
-    go_z(up, every)
-    go_z(ot, every)
-    attend_back(1)
-    go_plane(qk[2])
-    go_z(qk[3], (3,))
-    go_final(dn, z_copies(dn, every))
-    attend_back(0)
-
     def back_two(i, carry):
         gain_acc, shift_acc = carry
         r = rows_of(i, CHUNK)
@@ -727,15 +832,29 @@
         gtok_ref[r, :] = (gl[r, :] + back).astype(BF16)
         return gain_acc, shift_acc
 
+    attend_back(3)
+    go_plane(ot)
+    attend_back(2)
+    go_fold_last(up)
+    go_plane(qk[3])
+    attend_back(1)
+    go_plane(qk[2])
+    go_z_fold(up, every)
+    attend_back(0)
     go_plane(qk[1])
+    go_z(ot, every)
+    go_own_plane(dn)
+    go_z(qk[3], (3,))
+    quarter = chunks // 4
+    norm_sums = lax.fori_loop(0, quarter, back_two, (zero8, zero8))
+    go_plane(qk[0])
     go_z(qk[2], (2,))
+    norm_sums = lax.fori_loop(quarter, 2 * quarter, back_two, norm_sums)
+    go_z(qk[1], (1,))
     go_final(up, z_copies(up, every))
-    go_plane(qk[0])
-    norm_sums = lax.fori_loop(0, chunks // 2, back_two, (zero8, zero8))
-    go_z(qk[1], (1,))
+    go_own_final(dn)
     go_final(ot, z_copies(ot, every))
-    go_last(dn)
-    gain_one, shift_one = lax.fori_loop(chunks // 2, chunks, back_two, norm_sums)
+    gain_one, shift_one = lax.fori_loop(2 * quarter, chunks, back_two, norm_sums)
 
     def fold8(x):
         return jnp.sum(x, axis=0, keepdims=True)
@@ -750,29 +869,44 @@
 
     copies, total_small = reduce_all(small, sv_one, sv_nodes, sv_tp, bsend, brecv, rest_of)
     go_last(up)
+    go_last(dn)
     go_last(ot)
+    go_last(qk[0])
     for cp in copies:
         cp.wait()
     small_ref[...] = total_small()
-    go_last(qk[0])
     finish(dn)
     finish(up)
     finish(ot)
     finish(qk[0])
 
 
-def results_kernel(readout, gtok, small, fin_in, fin_out, fin_up, fin_dn, o_read, o_tok, o_g1, o_s1, o_q, o_k, o_v, o_out, o_g2, o_s2, o_up, o_dn, o_hop):
-    o_tok[...] = gtok[...]
-    o_read[...] = readout[...]
+def results_kernel(readout, gtok, small, fin_in, fin_out, fin_up, fin_dn, *rest):
+    o_read, o_tok, o_g1, o_s1, o_q, o_k, o_v, o_out, o_g2, o_s2, o_up, o_dn, o_hop = rest[:13]
+    v_q, v_k, v_v, v_out, v_up, v_dn, sems = rest[13:]
+    moves = []
+
+    def send(src, dst):
+        moves.append(pltpu.make_async_copy(src, dst, sems.at[len(moves)]))
+        moves[-1].start()
+
+    send(gtok, o_tok)
+    send(readout, o_read)
+    v_up[...] = fin_up[...].astype(F32)
+    send(v_up, o_up)
+    v_dn[...] = fin_dn[...].astype(F32)
+    send(v_dn, o_dn)
+    qw = o_q.shape[1]
+    for i, (x, o) in enumerate(((v_q, o_q), (v_k, o_k), (v_v, o_v))):
+        x[...] = fin_in[:, i * qw : (i + 1) * qw].astype(F32)
+        send(x, o)
+    v_out[...] = fin_out[...].astype(F32)
+    send(v_out, o_out)
     width = small.shape[1]
     for i, o in enumerate((o_g1, o_s1, o_g2, o_s2, o_hop)):
         o[...] = small[i : i + 1, :].reshape(width)
-    qw = o_q.shape[1]
-    for i, o in enumerate((o_q, o_k, o_v)):
-        o[...] = fin_in[:, i * qw : (i + 1) * qw].astype(F32)
-    o_out[...] = fin_out[...].astype(F32)
-    o_up[...] = fin_up[...].astype(F32)
-    o_dn[...] = fin_dn[...].astype(F32)
+    for cp in moves:
+        cp.wait()
 
 
 def shards(
@@ -805,10 +939,12 @@
 
     tiles, chunks = rows // TILE, rows // CHUNK
     half = width // 2
+    more = max(2 * extra, 1)
     scratch = [
         v(width, 12 * qw),
         v(width, 4 * uw),
-        v(4, qw + uw, width),
+        v(4, qw, width),
+        v(4, uw, width),
         v(rows, width),
         v(nodes, width),
         v(rows, width),
@@ -843,13 +979,17 @@
         v(4, qw // 2, width),
         v(4, half, 3 * qw),
         v(3, half // 4, 4 * uw),
-        v(3, 4, uw // 8, width),
+        v(3, uw // 8, width),
         v(3, 4, qw // 8, width),
         v(4, 3, half // 4, 3 * qw),
-        v(3 + 2 * extra, half // 4, uw),
-        v(3 + 2 * extra, uw // 8, width),
-        v(3 + 2 * extra, qw // 8, width),
-        v(3 + 2 * extra, half // 4, 3 * qw),
+        v(3, half // 4, uw),
+        v(3, uw // 2, width),
+        v(3, qw // 8, width),
+        v(3, half // 4, 3 * qw),
+        v(more, half // 4, uw),
+        v(more, uw // 8, width),
+        v(more, qw // 8, width),
+        v(more, half // 4, 3 * qw),
         v(2 + extra, HOPS, TILE, dtype=F32),
         v(7 + extra, HOPS, TILE, dtype=F32),
         v(3, HOPS, TILE, dtype=F32),
@@ -857,23 +997,23 @@
         v(7 + extra, 8, width, dtype=F32),
         v(3, 8, width, dtype=F32),
         pltpu.SemaphoreType.DMA((8,)),
-        pltpu.SemaphoreType.DMA((40,)),
-        pltpu.SemaphoreType.DMA((40,)),
-        pltpu.SemaphoreType.DMA((7 * (11 + extra),)),
-        pltpu.SemaphoreType.DMA((7 * (11 + extra),)),
+        pltpu.SemaphoreType.DMA((48,)),
+        pltpu.SemaphoreType.DMA((48,)),
+        pltpu.SemaphoreType.DMA((7 * (15 + extra),)),
+        pltpu.SemaphoreType.DMA((7 * (15 + extra),)),
         pltpu.SemaphoreType.DMA((10 + extra,)),
         pltpu.SemaphoreType.DMA((10 + extra,)),
         pltpu.SemaphoreType.DMA((10 + extra,)),
         pltpu.SemaphoreType.DMA((10 + extra,)),
     ]
     outs = [
-        jax.ShapeDtypeStruct((nodes, width), BF16),
-        jax.ShapeDtypeStruct((rows, width), BF16),
-        jax.ShapeDtypeStruct((8, width), F32),
-        jax.ShapeDtypeStruct((width, 3 * qw), BF16),
-        jax.ShapeDtypeStruct((qw, width), BF16),
-        jax.ShapeDtypeStruct((width, uw), BF16),
-        jax.ShapeDtypeStruct((uw, width), BF16),
+        pltpu.VMEM((nodes, width), BF16),
+        pltpu.VMEM((rows, width), BF16),
+        pltpu.VMEM((8, width), F32),
+        pltpu.VMEM((width, 3 * qw), BF16),
+        pltpu.VMEM((qw, width), BF16),
+        pltpu.VMEM((width, uw), BF16),
+        pltpu.VMEM((uw, width), BF16),
     ]
     readout, gtok, small, fin_in, fin_out, fin_up, fin_dn = pl.pallas_call(
         functools.partial(kernel, nn),
@@ -882,7 +1022,7 @@
         out_specs=[vm] * 7,
         scratch_shapes=scratch,
         compiler_params=pltpu.CompilerParams(
-            collective_id=0, has_side_effects=True, vmem_limit_bytes=60 * 1024 * 1024
+            collective_id=0, has_side_effects=True, vmem_limit_bytes=52 * 1024 * 1024
         ),
         name="layer",
     )(
@@ -922,7 +1062,15 @@
             line,
         ],
         in_specs=[vm] * 7,
-        out_specs=[vm] * 13,
+        out_specs=[hbm, hbm, vm, vm, hbm, hbm, hbm, hbm, vm, vm, hbm, hbm, vm],
+        scratch_shapes=[v(width, qw, dtype=F32)] * 3
+        + [
+            v(qw, width, dtype=F32),
+            v(width, uw, dtype=F32),
+            v(uw, width, dtype=F32),
+            pltpu.SemaphoreType.DMA((8,)),
+        ],
+        compiler_params=pltpu.CompilerParams(vmem_limit_bytes=16 * 1024 * 1024),
         name="results",
     )(readout, gtok, small, fin_in, fin_out, fin_up, fin_dn)
 

time: 102 us -> 86.7 us (0.85)
  Pallas kernels: 101 us -> 85.7 us
    pallas_call x1, Pallas kernels: 97.4 us -> 83.3 us  [shards(): pl.pallas_call(functools.partial(kernel, nn), out_shape=outs, in_specs=[h...]
where the time goes in v4:
time: 86.7 us; the launch traced here: 86.5 us
  Pallas kernels  85.7 us (99%)
    pallas_call x1, Pallas kernels, shards(): pl.pallas_call(functools.partial(kernel, nn), out_shape=outs, in_specs=[h...  83.3 us
    pallas_call x1, Pallas kernels, shards(): pl.pallas_call(results_kernel, out_shape=[jax.ShapeDtypeStruct((nodes, wi...  2.37 us

profile of v4, /device:TPU:0, one launch (start us, length us, event | category | flops | bytes accessed | tf_op | source)
XLA Modules:
  0.0 86.5 jit_solution(4215382494977123979)
XLA Ops:
  0.7 83.3 %layer.1 = (bf16[128,512]{1,0:T(8,128)(2,1)S(1)}, bf16[1024,512]{1,0:T(8,128)(2,1)S(1)}, f32[8,512]{1,0:T(8,128)S(1)}, bf16[512,384]{1,0:T(8,128)(2,1)S(1)}, bf1...) custom-call(bf16[1024,512]{1,0:T(8,128)(2,1)} %tok_hbm.1, s32[8,128]{1,0:T(8,128)} %bitcast.2, ...), custom_call_target="tpu_custom_call" | custom-call | tf_op jit(solution)/shard_map/layer/pallas_call | solution.py:1018
  84.0 2.4 %results.1 = (bf16[128,512]{1,0:T(8,128)(2,1)}, bf16[1024,512]{1,0:T(8,128)(2,1)}, f32[512]{0:T(512)}, f32[512]{0:T(512)}, f32[512,128]{1,0:T(8,128)}, /*index=5...) custom-call(bf16[128,512]{1,0:T(8,128)(2,1)S(1)} %get-tuple-element., ...), custom_call_target="tpu_custom_call" | custom-call | tf_op jit(solution)/shard_map/results/pallas_call | solution.py:1047

commit v5 on v4

--- a/solution.py
+++ b/solution.py
@@ -114,6 +114,13 @@
     fin_out_ref,
     fin_up_ref,
     fin_dn_ref,
+    mask_v,
+    gid_v,
+    g1_v,
+    s1_v,
+    g2_v,
+    s2_v,
+    hw_v,
     w_in,
     w_up,
     w_ot,
@@ -131,6 +138,9 @@
     lay,
     emask,
     pmask,
+    n1t,
+    n2t,
+    ctxt,
     vcol,
     mt,
     gexp,
@@ -221,6 +231,9 @@
         pltpu.make_async_copy(wu_hbm, w_up.at[:, 0 : wu_hbm.shape[1]], lsem.at[6]),
         pltpu.make_async_copy(cot_hbm, cot, lsem.at[7]),
     ]
+    tiny = ((mask_ref, mask_v), (gid_ref, gid_v), (g1_ref, g1_v), (s1_ref, s1_v), (g2_ref, g2_v), (s2_ref, s2_v))
+    for i, (src, dst) in enumerate(tiny + ((hw_ref, hw_v),)):
+        local.append(pltpu.make_async_copy(src, dst, lsem.at[8 + i]))
     for copy in local:
         copy.start()
 
@@ -288,7 +301,7 @@
 
     fetch_in = [None] + [Fetch(w_in, (d, d + 1), 8 * (d - 1)) for d in (1, 2, 3)]
     fetch_ot = Fetch(w_ot, (1, 4), 24)
-    fetch_up = Fetch(w_up, (1, 4), 32, halves=True)
+    fetch_up = Fetch(w_up, (1, 4), 32)
     fetch_dn = Fetch(w_dn, (1, 4), 40)
 
     for i in (0, 1, 2):
@@ -296,11 +309,13 @@
     for d in (1, 2, 3):
         fetch_in[d].start_z()
 
-    gain1 = tokens_of(g1_ref)
-    shift1 = tokens_of(s1_ref)
-    gain2 = tokens_of(g2_ref)
-    shift2 = tokens_of(s2_ref)
-    hopw = tokens_of(hw_ref)
+    for i in range(8, 15):
+        local[i].wait()
+    gain1 = tokens_of(g1_v)
+    shift1 = tokens_of(s1_v)
+    gain2 = tokens_of(g2_v)
+    shift2 = tokens_of(s2_v)
+    hopw = tokens_of(hw_v)
     hop16 = jnp.broadcast_to(hopw, (16, width)).astype(BF16)
 
     eye = iota((TILE, TILE), 0) == iota((TILE, TILE), 1)
@@ -317,7 +332,7 @@
     def rows_of(i, size):
         return pl.ds(pl.multiple_of(i * size, size), size)
 
-    mask_f = mask_ref[...].astype(F32)
+    mask_f = mask_v[...].astype(F32)
     for i in range(tiles):
         col = mm(jnp.where(eye, mask_f[i : i + 1, :], 0.0).astype(BF16), ones)
         vcol[i * TILE : (i + 1) * TILE, :] = col
@@ -326,9 +341,6 @@
         for r in range(TILE // HOPS):
             acc = jnp.where(block8 == r, col3[r], acc)
         mt[i] = acc
-    gcol = mm(jnp.where(eye, gid_ref[...].astype(F32), 0.0).astype(BF16), ones).astype(BF16)
-    for i in range(chunks):
-        gexp[i * CHUNK : (i + 1) * CHUNK, :] = mm(spread_c, gcol[i * nodes_chunk : (i + 1) * nodes_chunk])
 
     local[3].wait()
 
@@ -340,7 +352,7 @@
 
     lax.fori_loop(0, chunks, norm_one, 0)
 
-    def project(d):
+    def project(d, lo, hi):
         base = d * 3 * qw
 
         def step(i, carry):
@@ -350,7 +362,7 @@
             qkv[r, base + qw : base + 3 * qw] = out[:, qw:].astype(BF16)
             return carry
 
-        lax.fori_loop(0, chunks, step, 0)
+        lax.fori_loop(lo, hi, step, 0)
 
     def pair(x):
         return jnp.concatenate([x, x], axis=0) * pmask[...]
@@ -407,39 +419,44 @@
 
         lax.fori_loop(lo, hi, step, 0)
 
+    gcol = mm(jnp.where(eye, gid_v[...].astype(F32), 0.0).astype(BF16), ones).astype(BF16)
+    for i in range(chunks):
+        gexp[i * CHUNK : (i + 1) * CHUNK, :] = mm(spread_c, gcol[i * nodes_chunk : (i + 1) * nodes_chunk])
+    cmid = chunks // 2
     fetch_in[1].start_plane()
+    project(0, 0, cmid)
+    fetch_in[2].start_plane()
+    project(0, cmid, chunks)
+    fetch_in[3].start_plane()
     for i in (4, 5, 6, 7):
         local[i].wait()
     fetch_ot.start_z()
-    project(0)
-    fetch_in[2].start_plane()
+    fetch_up.start_z()
+    fetch_dn.start_z()
     attend(0, 0, mid)
-    fetch_in[3].start_plane()
-    fetch_up.start_z()
+    fetch_ot.start_plane()
+    fetch_in[1].start_core()
     attend(0, mid, steps)
-    fetch_in[1].start_core()
-    fetch_ot.start_plane()
     fetch_in[1].end()
-    project(1)
     fetch_in[2].start_core()
+    project(1, 0, cmid)
+    fetch_up.start_plane()
+    project(1, cmid, chunks)
     attend(1, 0, mid)
     fetch_in[3].start_core()
-    fetch_dn.start_z()
+    attend(1, mid, steps)
     fetch_in[2].end()
-    attend(1, mid, steps)
-    project(2)
+    project(2, 0, cmid)
+    fetch_dn.start_plane()
+    project(2, cmid, chunks)
+    attend(2, 0, mid)
     fetch_ot.start_core()
-    attend(2, 0, mid)
-    fetch_up.start_plane()
     attend(2, mid, steps)
     fetch_in[3].end()
-    project(3)
+    project(3, 0, chunks)
     attend(3, 0, mid)
-    fetch_dn.start_plane()
     attend(3, mid, steps)
     fetch_ot.end()
-    fetch_up.start_core()
-    fetch_up.end()
 
     def w_out():
         return w_ot[...].reshape(4 * qw, width)
@@ -452,19 +469,27 @@
     node3 = iota((nodes_chunk, HOPS, TILE), 0)
     lane_graph = (lane3 % GRAPHS).astype(F32)
 
-    def feed_up(i, carry):
+    def feed_norm(i, carry):
         r = rows_of(i, CHUNK)
-        attended = mm(ctx[r, :], w_out())
-        x = tok[r, :].astype(F32) + attended
+        x = tok[r, :].astype(F32) + mm(ctx[r, :], w_out())
         res[r, :] = x
         hat, _ = centred(x)
-        normed = (hat * gain2 + shift2).astype(BF16)
-        n2[r, :] = normed
-        value, slope = gelu_both(mm(normed, w_up[...]))
-        value = value.astype(BF16)
-        act[r, :] = value
-        gp[r, :] = slope.astype(BF16)
+        n2[r, :] = (hat * gain2 + shift2).astype(BF16)
         return carry
+
+    uw = wu_hbm.shape[1]
+
+    def feed_up(lo, hi):
+        cols = slice(lo * uw, hi * uw)
+
+        def step(i, carry):
+            r = rows_of(i, CHUNK)
+            value, slope = gelu_both(mm(n2[r, :], w_up[:, cols]))
+            act[r, cols] = value.astype(BF16)
+            gp[r, cols] = slope.astype(BF16)
+            return carry
+
+        return step
 
     def feed_down(i, acc):
         r = rows_of(i, CHUNK)
@@ -487,9 +512,13 @@
         both = jnp.where(lane3 < GRAPHS, jnp.where(hop3 == 0, 1.0, weight), -direct)
         return acc + jnp.sum(jnp.where(mine, both, 0.0), axis=0)
 
-    lax.fori_loop(0, chunks // 2, feed_up, 0)
+    lax.fori_loop(0, chunks, feed_norm, 0)
+    fetch_up.start_core()
+    lax.fori_loop(0, chunks, feed_up(0, 1), 0)
+    fetch_up.end()
+    lax.fori_loop(0, cmid, feed_up(1, 4), 0)
     fetch_dn.start_core()
-    lax.fori_loop(chunks // 2, chunks, feed_up, 0)
+    lax.fori_loop(cmid, chunks, feed_up(1, 4), 0)
     fetch_dn.end()
     sums = lax.fori_loop(0, chunks, feed_down, jnp.zeros((HOPS, TILE), F32))
 
@@ -534,6 +563,10 @@
             ab[i, nodes_chunk : 2 * nodes_chunk] = piece
             ab[i, 2 * nodes_chunk : 2 * nodes_chunk + 16] = hopdown
             ab[i, 2 * nodes_chunk + 16 :] = jnp.zeros((TILE - 2 * nodes_chunk - 16, ab.shape[2]), BF16)
+        for i in range(chunks):
+            at = slice(i * CHUNK, (i + 1) * CHUNK)
+            for src, dst in ((n2, n2t), (ctx, ctxt), (n1, n1t)):
+                dst[:, at] = src[at, :].T
 
     copies, total = reduce_all(sums, ar_one, ar_nodes, ar_tp, asend, arecv, small_products)
     for cp in copies:
@@ -544,7 +577,7 @@
     means = (sums / (counts + 1.0))[None]
 
     def back_one(i, carry):
-        gain_acc, shift_acc, hop_acc, zed_acc = carry
+        hop_acc, zed_acc = carry
         r = rows_of(i, CHUNK)
         shape = (nodes_chunk, HOPS, TILE)
         picked = jnp.where(gexp[r, :].reshape(shape) == lane_graph, means, 0.0)
@@ -567,10 +600,8 @@
         dr = cot[rows_of(i, nodes_chunk), :]
         rest = jnp.zeros((TILE - 2 * nodes_chunk - 16, width), BF16)
         dh = jnp.concatenate([dr, dr, hop16, rest], axis=0)
-        grad_layer = mm(mix, dh)
-        gl[r, :] = grad_layer
-        before_back = (mm(mix, ab[i]) * gp[r, :].astype(F32)).astype(BF16)
-        gbef[r, :] = before_back
+        gl[r, :] = mm(mix, dh)
+        gbef[r, :] = (mm(mix, ab[i]) * gp[r, :].astype(F32)).astype(BF16)
 
         seen = mm_lt(mix, lay[r, :].astype(BF16))
         readout_ref[rows_of(i, nodes_chunk), :] = (seen[0:nodes_chunk] + seen[nodes_chunk : 2 * nodes_chunk]).astype(
@@ -581,7 +612,12 @@
         zed[rows_of(i, nodes_chunk), :] = (fold[0:nodes_chunk] + fold[nodes_chunk : 2 * nodes_chunk]).astype(BF16)
         zed_acc = zed_acc + fold[2 * nodes_chunk : 2 * nodes_chunk + 8]
 
-        dy = mm_rt(before_back, w_up[...])
+        return hop_acc, zed_acc
+
+    def back_norm(i, carry):
+        gain_acc, shift_acc = carry
+        r = rows_of(i, CHUNK)
+        dy = mm_rt(gbef[r, :], w_up[...])
         hat, inv = centred(res[r, :])
         gain_acc = gain_acc + jnp.sum((dy * hat).reshape(nodes_chunk, HOPS, width), axis=0)
         shift_acc = shift_acc + jnp.sum(dy.reshape(nodes_chunk, HOPS, width), axis=0)
@@ -589,17 +625,15 @@
         back = inv * (
             g - jnp.mean(g, axis=-1, keepdims=True) - hat * jnp.mean(g * hat, axis=-1, keepdims=True)
         )
-        grad_res = grad_layer + back
+        grad_res = gl[r, :] + back
         gl[r, :] = grad_res
         att = grad_res.astype(BF16)
         datt[r, :] = att
         dctx[r, :] = mm_rt(att, w_out()).astype(BF16)
-        return gain_acc, shift_acc, hop_acc, zed_acc
+        return gain_acc, shift_acc
 
     zero8 = jnp.zeros((HOPS, width), F32)
-    gain_two, shift_two, hop_sum, zed_sum = lax.fori_loop(
-        0, chunks, back_one, (zero8, zero8, zero8, jnp.zeros((HOPS, zed.shape[1]), F32))
-    )
+    hop_sum, zed_sum = lax.fori_loop(0, chunks, back_one, (zero8, jnp.zeros((HOPS, zed.shape[1]), F32)))
 
     def group(at, array, wide, cols, rc, rp, rz, final, more):
         return Group(array, wide, cols, rc, rp, rz, final, more, gsend, grecv, at * (15 + len(extra)))
@@ -642,19 +676,27 @@
         for cp in plane_copies(g):
             cp.start()
 
-    def cut(g, rows, e):
-        w = (g.cols[1] - g.cols[0]) * g.width // 2
-        base = g.cols[0] * g.width + e * w
-        return g.array.at[rows, base : base + w]
+    def cut(g, p, e):
+        if g.wide:
+            w = g.piece_rows // 2
+            rows = pl.ds(pl.multiple_of(c * g.half_rows + p * g.piece_rows + e * w, 16), w)
+            return g.array.at[rows, g.cols[0] * g.width : g.cols[1] * g.width]
+        w = g.width // 2
+        return g.array.at[:, g.rows(c, p), e * w : (e + 1) * w]
+
+    def landing(g, m, e):
+        if g.wide:
+            w = g.piece_rows // 2
+            return g.recv_plane.at[m, e * w : (e + 1) * w]
+        w = g.width // 2
+        return g.recv_plane.at[m, :, :, e * w : (e + 1) * w]
 
     def fold_copies(g):
-        w = (g.cols[1] - g.cols[0]) * g.width // 2
         out = []
         for e in range(2):
-            away = plane_of(1 << e)
-            for m, far in enumerate((away, plane_of(3))):
-                dst = g.recv_plane.at[m, :, e * w : (e + 1) * w]
-                out.append(remote(cut(g, g.rows(c, far), e), dst, *g.sems(11 + 2 * e + m), node_peer(2 << e)))
+            for m, far in enumerate((plane_of(1 << e), plane_of(3))):
+                sems = g.sems(11 + 2 * e + m)
+                out.append(remote(cut(g, far, e), landing(g, m, e), *sems, node_peer(2 << e)))
         return out
 
     def go_fold(g):
@@ -663,23 +705,17 @@
             cp.start()
 
     def fold_last(g):
-        w = (g.cols[1] - g.cols[0]) * g.width // 2
-        out = []
-        for e in range(2):
-            dst = g.recv_plane.at[2, :, e * w : (e + 1) * w]
-            far = plane_of(2 >> e)
-            out.append(remote(cut(g, g.rows(c, far), e), dst, *g.sems(1 + e), node_peer(4 >> e)))
-        return out
+        return [
+            remote(cut(g, plane_of(2 >> e), e), landing(g, 2, e), *g.sems(1 + e), node_peer(4 >> e)) for e in range(2)
+        ]
 
     def go_fold_last(g):
         for cp in fold_copies(g):
             cp.wait()
-        w = (g.cols[1] - g.cols[0]) * g.width // 2
         for e in range(2):
             for m, keep in enumerate((plane, plane_of(2 >> e))):
-                mine = cut(g, g.rows(c, keep), e)
-                got = g.recv_plane[m, :, e * w : (e + 1) * w]
-                mine[...] = (mine[...].astype(F32) + got.astype(F32)).astype(BF16)
+                mine = cut(g, keep, e)
+                mine[...] = (mine[...].astype(F32) + landing(g, m, e)[...].astype(F32)).astype(BF16)
         for cp in fold_last(g):
             cp.start()
 
@@ -779,12 +815,14 @@
     drh = jnp.concatenate([cot[...], hop16], axis=0)
     g_dn[...] = mm_lt(zed[...], drh).astype(BF16).reshape(g_dn.shape)
     go_core(dn)
-    g_up[...] = mm_lt(n2[...], gbef[...]).astype(BF16)
+    g_up[...] = mm(n2t[...], gbef[...]).astype(BF16)
     go_core(up)
+    norm_sums = lax.fori_loop(0, cmid, back_norm, (zero8, zero8))
     go_z_first(dn)
-    g_out[...] = mm_lt(ctx[...], datt[...]).astype(BF16).reshape(g_out.shape)
+    gain_two, shift_two = lax.fori_loop(cmid, chunks, back_norm, norm_sums)
+    go_fold(up)
+    g_out[...] = mm(ctxt[...], datt[...]).astype(BF16).reshape(g_out.shape)
     go_core(ot)
-    go_fold(up)
 
     def attend_back(d):
         base = d * 3 * qw
@@ -815,7 +853,7 @@
             return carry
 
         lax.fori_loop(0, tiles // together, step, 0)
-        g_in[:, base : base + 3 * qw] = mm_lt(n1[...], dqkv[:, base : base + 3 * qw]).astype(BF16)
+        g_in[:, base : base + 3 * qw] = mm(n1t[...], dqkv[:, base : base + 3 * qw]).astype(BF16)
         go_core(qk[d])
 
     def back_two(i, carry):
@@ -833,28 +871,29 @@
         return gain_acc, shift_acc
 
     attend_back(3)
-    go_plane(ot)
+    go_fold(ot)
     attend_back(2)
+    go_fold(qk[3])
     go_fold_last(up)
-    go_plane(qk[3])
     attend_back(1)
-    go_plane(qk[2])
-    go_z_fold(up, every)
+    go_fold(qk[2])
+    go_fold_last(ot)
     attend_back(0)
     go_plane(qk[1])
-    go_z(ot, every)
-    go_own_plane(dn)
-    go_z(qk[3], (3,))
+    go_z_fold(up, every)
+    go_fold_last(qk[3])
     quarter = chunks // 4
     norm_sums = lax.fori_loop(0, quarter, back_two, (zero8, zero8))
     go_plane(qk[0])
-    go_z(qk[2], (2,))
+    go_z_fold(ot, every)
+    go_fold_last(qk[2])
     norm_sums = lax.fori_loop(quarter, 2 * quarter, back_two, norm_sums)
+    go_own_plane(dn)
+    go_z_fold(qk[3], (3,))
+    norm_sums = lax.fori_loop(2 * quarter, 3 * quarter, back_two, norm_sums)
     go_z(qk[1], (1,))
-    go_final(up, z_copies(up, every))
-    go_own_final(dn)
-    go_final(ot, z_copies(ot, every))
-    gain_one, shift_one = lax.fori_loop(2 * quarter, chunks, back_two, norm_sums)
+    go_z_fold(qk[2], (2,))
+    gain_one, shift_one = lax.fori_loop(3 * quarter, chunks, back_two, norm_sums)
 
     def fold8(x):
         return jnp.sum(x, axis=0, keepdims=True)
@@ -864,6 +903,9 @@
     )
 
     def rest_of():
+        go_final(up, z_copies(up, every))
+        go_final(ot, z_copies(ot, every))
+        go_own_final(dn)
         go_z(qk[0], ())
         go_final(qk[0], [z_copies(qk[d], (d,))[0] for d in every])
 
@@ -941,6 +983,13 @@
     half = width // 2
     more = max(2 * extra, 1)
     scratch = [
+        v(tiles, TILE, dtype=jnp.int32),
+        v(1, nodes, dtype=jnp.int32),
+        v(width),
+        v(width),
+        v(width),
+        v(width),
+        v(width),
         v(width, 12 * qw),
         v(width, 4 * uw),
         v(4, qw, width),
@@ -958,6 +1007,9 @@
         v(rows, width, dtype=F32),
         v(TILE, TILE),
         v(2 * TILE, TILE),
+        v(width, rows),
+        v(width, rows),
+        v(width, rows),
         v(rows, TILE, dtype=F32),
         v(tiles, HOPS, TILE, dtype=F32),
         v(rows, TILE, dtype=F32),
@@ -996,7 +1048,7 @@
         v(2 + extra, 8, width, dtype=F32),
         v(7 + extra, 8, width, dtype=F32),
         v(3, 8, width, dtype=F32),
-        pltpu.SemaphoreType.DMA((8,)),
+        pltpu.SemaphoreType.DMA((15,)),
         pltpu.SemaphoreType.DMA((48,)),
         pltpu.SemaphoreType.DMA((48,)),
         pltpu.SemaphoreType.DMA((7 * (15 + extra),)),
@@ -1018,11 +1070,11 @@
     readout, gtok, small, fin_in, fin_out, fin_up, fin_dn = pl.pallas_call(
         functools.partial(kernel, nn),
         out_shape=outs,
-        in_specs=[hbm, vm, vm, vm, vm, hbm, hbm, hbm, hbm, vm, vm, hbm, hbm, vm, hbm],
+        in_specs=[hbm] * 15,
         out_specs=[vm] * 7,
         scratch_shapes=scratch,
         compiler_params=pltpu.CompilerParams(
-            collective_id=0, has_side_effects=True, vmem_limit_bytes=52 * 1024 * 1024
+            collective_id=0, has_side_effects=True, vmem_limit_bytes=56 * 1024 * 1024
         ),
         name="layer",
     )(

time: 86.7 us -> 81.9 us (0.945)
  Pallas kernels: 85.7 us -> 80.9 us
    pallas_call x1, Pallas kernels: 83.3 us -> 78.5 us  [shards(): pl.pallas_call(functools.partial(kernel, nn), out_shape=outs, in_specs=[h...]
where the time goes in v5:
time: 81.9 us; the launch traced here: 81.7 us
  Pallas kernels  80.9 us (99%)
  between operations  0.82 us (1%)
    pallas_call x1, Pallas kernels, shards(): pl.pallas_call(functools.partial(kernel, nn), out_shape=outs, in_specs=[h...  78.5 us
    pallas_call x1, Pallas kernels, shards(): pl.pallas_call(results_kernel, out_shape=[jax.ShapeDtypeStruct((nodes, wi...  2.37 us

profile of v5, /device:TPU:0, one launch (start us, length us, event | category | flops | bytes accessed | tf_op | source)
XLA Modules:
  0.0 81.7 jit_solution(2740834243138278461)
XLA Ops:
  0.7 78.5 %layer.1 = (bf16[128,512]{1,0:T(8,128)(2,1)S(1)}, bf16[1024,512]{1,0:T(8,128)(2,1)S(1)}, f32[8,512]{1,0:T(8,128)S(1)}, bf16[512,384]{1,0:T(8,128)(2,1)S(1)}, bf1...) custom-call(bf16[1024,512]{1,0:T(8,128)(2,1)} %tok_hbm.1, s32[8,128]{1,0:T(8,128)} %bitcast.2, ...), custom_call_target="tpu_custom_call" | custom-call | tf_op jit(solution)/shard_map/layer/pallas_call | solution.py:1070
  79.2 2.4 %results.1 = (bf16[128,512]{1,0:T(8,128)(2,1)}, bf16[1024,512]{1,0:T(8,128)(2,1)}, f32[512]{0:T(512)}, f32[512]{0:T(512)}, f32[512,128]{1,0:T(8,128)}, /*index=5...) custom-call(bf16[128,512]{1,0:T(8,128)(2,1)S(1)} %get-tuple-element., ...), custom_call_target="tpu_custom_call" | custom-call | tf_op jit(solution)/shard_map/results/pallas_call | solution.py:1099

commit v6 on v5

--- a/solution.py
+++ b/solution.py
@@ -16,6 +16,7 @@
 F32 = jnp.float32
 BF16 = jnp.bfloat16
 CHUNK = 256
+WIDE = 512
 TILE = 128
 
 
@@ -42,15 +43,8 @@
 
 
 def gelu_both(x):
-    size = jnp.abs(x)
-    t = 1.0 / (1.0 + (0.3275911 * 0.7071067811865476) * size)
-    bell = jnp.exp(-0.5 * (x * x))
-    poly = 1.061405429 * t - 1.453152027
-    poly = poly * t + 1.421413741
-    poly = poly * t - 0.284496736
-    poly = poly * t + 0.254829592
-    tail = (0.5 * t) * poly * bell
-    phi = jnp.where(x >= 0, 1.0 - tail, tail)
+    phi = 0.5 + 0.5 * lax.erf(x * 0.7071067811865476)
+    bell = jnp.exp2((-0.5 * 1.4426950408889634) * (x * x))
     return x * phi, phi + x * (bell * 0.3989422804014327)
 
 
@@ -148,6 +142,7 @@
     dcol,
     ab,
     zed,
+    mixes,
     gbef,
     gl,
     datt,
@@ -192,6 +187,7 @@
     n, t = lax.axis_index("nodes"), lax.axis_index("tp")
     rows_here, width = tok.shape
     chunks = rows_here // CHUNK
+    wides = rows_here // WIDE
     tiles = rows_here // TILE
     c = n % 2
     plane = (n // 2) % 4
@@ -356,7 +352,7 @@
         base = d * 3 * qw
 
         def step(i, carry):
-            r = rows_of(i, CHUNK)
+            r = rows_of(i, WIDE)
             out = mm(n1[r, :], w_in[:, base : base + 3 * qw])
             qkv[r, base : base + qw] = (out[:, 0:qw] * (HEAD**-0.5)).astype(BF16)
             qkv[r, base + qw : base + 3 * qw] = out[:, qw:].astype(BF16)
@@ -383,7 +379,7 @@
         twice = jnp.concatenate([x, x], axis=0).astype(BF16)
         return jnp.concatenate([twice] * (TILE // 16), axis=0) * emask[...]
 
-    together = 4
+    together = 8
 
     steps = tiles // together
     mid = steps // 2
@@ -422,11 +418,10 @@
     gcol = mm(jnp.where(eye, gid_v[...].astype(F32), 0.0).astype(BF16), ones).astype(BF16)
     for i in range(chunks):
         gexp[i * CHUNK : (i + 1) * CHUNK, :] = mm(spread_c, gcol[i * nodes_chunk : (i + 1) * nodes_chunk])
-    cmid = chunks // 2
     fetch_in[1].start_plane()
-    project(0, 0, cmid)
+    project(0, 0, wides // 2)
     fetch_in[2].start_plane()
-    project(0, cmid, chunks)
+    project(0, wides // 2, wides)
     fetch_in[3].start_plane()
     for i in (4, 5, 6, 7):
         local[i].wait()
@@ -439,21 +434,21 @@
     attend(0, mid, steps)
     fetch_in[1].end()
     fetch_in[2].start_core()
-    project(1, 0, cmid)
+    project(1, 0, wides // 2)
     fetch_up.start_plane()
-    project(1, cmid, chunks)
+    project(1, wides // 2, wides)
     attend(1, 0, mid)
     fetch_in[3].start_core()
     attend(1, mid, steps)
     fetch_in[2].end()
-    project(2, 0, cmid)
+    project(2, 0, wides // 2)
     fetch_dn.start_plane()
-    project(2, cmid, chunks)
+    project(2, wides // 2, wides)
     attend(2, 0, mid)
     fetch_ot.start_core()
     attend(2, mid, steps)
     fetch_in[3].end()
-    project(3, 0, chunks)
+    project(3, 0, wides)
     attend(3, 0, mid)
     attend(3, mid, steps)
     fetch_ot.end()
@@ -470,7 +465,7 @@
     lane_graph = (lane3 % GRAPHS).astype(F32)
 
     def feed_norm(i, carry):
-        r = rows_of(i, CHUNK)
+        r = rows_of(i, WIDE)
         x = tok[r, :].astype(F32) + mm(ctx[r, :], w_out())
         res[r, :] = x
         hat, _ = centred(x)
@@ -483,7 +478,7 @@
         cols = slice(lo * uw, hi * uw)
 
         def step(i, carry):
-            r = rows_of(i, CHUNK)
+            r = rows_of(i, WIDE)
             value, slope = gelu_both(mm(n2[r, :], w_up[:, cols]))
             act[r, cols] = value.astype(BF16)
             gp[r, cols] = slope.astype(BF16)
@@ -492,9 +487,15 @@
         return step
 
     def feed_down(i, acc):
+        r = rows_of(i, WIDE)
+        lay[r, :] = res[r, :] + mm(act[r, :], w_down())
+        for m in range(WIDE // CHUNK):
+            acc = hops(i * (WIDE // CHUNK) + m, acc)
+        return acc
+
+    def hops(i, acc):
         r = rows_of(i, CHUNK)
-        out = res[r, :] + mm(act[r, :], w_down())
-        lay[r, :] = out
+        out = lay[r, :]
         dr = mm(spread_c, cot[rows_of(i, nodes_chunk), :])
         logit = jnp.sum(out * hopw, axis=-1, keepdims=True)
         gcoef = jnp.sum(out * dr, axis=-1, keepdims=True)
@@ -512,15 +513,15 @@
         both = jnp.where(lane3 < GRAPHS, jnp.where(hop3 == 0, 1.0, weight), -direct)
         return acc + jnp.sum(jnp.where(mine, both, 0.0), axis=0)
 
-    lax.fori_loop(0, chunks, feed_norm, 0)
+    lax.fori_loop(0, wides, feed_norm, 0)
     fetch_up.start_core()
-    lax.fori_loop(0, chunks, feed_up(0, 1), 0)
+    lax.fori_loop(0, wides, feed_up(0, 1), 0)
     fetch_up.end()
-    lax.fori_loop(0, cmid, feed_up(1, 4), 0)
+    lax.fori_loop(0, wides // 2, feed_up(1, 4), 0)
     fetch_dn.start_core()
-    lax.fori_loop(cmid, chunks, feed_up(1, 4), 0)
+    lax.fori_loop(wides // 2, wides, feed_up(1, 4), 0)
     fetch_dn.end()
-    sums = lax.fori_loop(0, chunks, feed_down, jnp.zeros((HOPS, TILE), F32))
+    sums = lax.fori_loop(0, wides, feed_down, jnp.zeros((HOPS, TILE), F32))
 
     def reduce_all(value, one, by_nodes, by_tp, ssem, rsem, overlap=None):
         one[0] = value
@@ -577,7 +578,7 @@
     means = (sums / (counts + 1.0))[None]
 
     def back_one(i, carry):
-        hop_acc, zed_acc = carry
+        zed_acc = carry
         r = rows_of(i, CHUNK)
         shape = (nodes_chunk, HOPS, TILE)
         picked = jnp.where(gexp[r, :].reshape(shape) == lane_graph, means, 0.0)
@@ -597,30 +598,23 @@
         mix = jnp.where(lane3 == 2 * nodes_chunk + 1, glog - glog_hi, mix)
         mix = mix.reshape(CHUNK, TILE).astype(BF16)
 
-        dr = cot[rows_of(i, nodes_chunk), :]
-        rest = jnp.zeros((TILE - 2 * nodes_chunk - 16, width), BF16)
-        dh = jnp.concatenate([dr, dr, hop16, rest], axis=0)
-        gl[r, :] = mm(mix, dh)
+        mixes[r, :] = mix
         gbef[r, :] = (mm(mix, ab[i]) * gp[r, :].astype(F32)).astype(BF16)
 
-        seen = mm_lt(mix, lay[r, :].astype(BF16))
-        readout_ref[rows_of(i, nodes_chunk), :] = (seen[0:nodes_chunk] + seen[nodes_chunk : 2 * nodes_chunk]).astype(
-            BF16
-        )
-        hop_acc = hop_acc + seen[2 * nodes_chunk : 2 * nodes_chunk + 8]
         fold = mm_lt(mix, act[r, :])
         zed[rows_of(i, nodes_chunk), :] = (fold[0:nodes_chunk] + fold[nodes_chunk : 2 * nodes_chunk]).astype(BF16)
         zed_acc = zed_acc + fold[2 * nodes_chunk : 2 * nodes_chunk + 8]
 
-        return hop_acc, zed_acc
+        return zed_acc
 
     def back_norm(i, carry):
-        gain_acc, shift_acc = carry
-        r = rows_of(i, CHUNK)
+        gain_acc, shift_acc, hop_acc = carry
+        r = rows_of(i, WIDE)
+        hop_acc = layer_grads(i, hop_acc)
         dy = mm_rt(gbef[r, :], w_up[...])
         hat, inv = centred(res[r, :])
-        gain_acc = gain_acc + jnp.sum((dy * hat).reshape(nodes_chunk, HOPS, width), axis=0)
-        shift_acc = shift_acc + jnp.sum(dy.reshape(nodes_chunk, HOPS, width), axis=0)
+        gain_acc = gain_acc + jnp.sum((dy * hat).reshape(WIDE // HOPS, HOPS, width), axis=0)
+        shift_acc = shift_acc + jnp.sum(dy.reshape(WIDE // HOPS, HOPS, width), axis=0)
         g = dy * gain2
         back = inv * (
             g - jnp.mean(g, axis=-1, keepdims=True) - hat * jnp.mean(g * hat, axis=-1, keepdims=True)
@@ -630,10 +624,24 @@
         att = grad_res.astype(BF16)
         datt[r, :] = att
         dctx[r, :] = mm_rt(att, w_out()).astype(BF16)
-        return gain_acc, shift_acc
+        return gain_acc, shift_acc, hop_acc
+
+    def layer_grads(wide, hop_acc):
+        for m in range(WIDE // CHUNK):
+            i = wide * (WIDE // CHUNK) + m
+            r = rows_of(i, CHUNK)
+            mix = mixes[r, :]
+            dr = cot[rows_of(i, nodes_chunk), :]
+            rest = jnp.zeros((TILE - 2 * nodes_chunk - 16, width), BF16)
+            gl[r, :] = mm(mix, jnp.concatenate([dr, dr, hop16, rest], axis=0))
+            seen = mm_lt(mix, lay[r, :].astype(BF16))
+            both = seen[0:nodes_chunk] + seen[nodes_chunk : 2 * nodes_chunk]
+            readout_ref[rows_of(i, nodes_chunk), :] = both.astype(BF16)
+            hop_acc = hop_acc + seen[2 * nodes_chunk : 2 * nodes_chunk + 8]
+        return hop_acc
 
     zero8 = jnp.zeros((HOPS, width), F32)
-    hop_sum, zed_sum = lax.fori_loop(0, chunks, back_one, (zero8, jnp.zeros((HOPS, zed.shape[1]), F32)))
+    zed_sum = lax.fori_loop(0, chunks, back_one, jnp.zeros((HOPS, zed.shape[1]), F32))
 
     def group(at, array, wide, cols, rc, rp, rz, final, more):
         return Group(array, wide, cols, rc, rp, rz, final, more, gsend, grecv, at * (15 + len(extra)))
@@ -817,9 +825,9 @@
     go_core(dn)
     g_up[...] = mm(n2t[...], gbef[...]).astype(BF16)
     go_core(up)
-    norm_sums = lax.fori_loop(0, cmid, back_norm, (zero8, zero8))
+    norm_sums = lax.fori_loop(0, wides // 2, back_norm, (zero8, zero8, zero8))
     go_z_first(dn)
-    gain_two, shift_two = lax.fori_loop(cmid, chunks, back_norm, norm_sums)
+    gain_two, shift_two, hop_sum = lax.fori_loop(wides // 2, wides, back_norm, norm_sums)
     go_fold(up)
     g_out[...] = mm(ctxt[...], datt[...]).astype(BF16).reshape(g_out.shape)
     go_core(ot)
@@ -858,11 +866,11 @@
 
     def back_two(i, carry):
         gain_acc, shift_acc = carry
-        r = rows_of(i, CHUNK)
+        r = rows_of(i, WIDE)
         dy = mm_rt(dqkv[r, :], w_in[...])
         hat, inv = centred(tok[r, :].astype(F32))
-        gain_acc = gain_acc + jnp.sum((dy * hat).reshape(nodes_chunk, HOPS, width), axis=0)
-        shift_acc = shift_acc + jnp.sum(dy.reshape(nodes_chunk, HOPS, width), axis=0)
+        gain_acc = gain_acc + jnp.sum((dy * hat).reshape(WIDE // HOPS, HOPS, width), axis=0)
+        shift_acc = shift_acc + jnp.sum(dy.reshape(WIDE // HOPS, HOPS, width), axis=0)
         g = dy * gain1
         back = inv * (
             g - jnp.mean(g, axis=-1, keepdims=True) - hat * jnp.mean(g * hat, axis=-1, keepdims=True)
@@ -882,18 +890,15 @@
     go_plane(qk[1])
     go_z_fold(up, every)
     go_fold_last(qk[3])
-    quarter = chunks // 4
-    norm_sums = lax.fori_loop(0, quarter, back_two, (zero8, zero8))
+    norm_sums = lax.fori_loop(0, wides // 2, back_two, (zero8, zero8))
     go_plane(qk[0])
     go_z_fold(ot, every)
     go_fold_last(qk[2])
-    norm_sums = lax.fori_loop(quarter, 2 * quarter, back_two, norm_sums)
     go_own_plane(dn)
     go_z_fold(qk[3], (3,))
-    norm_sums = lax.fori_loop(2 * quarter, 3 * quarter, back_two, norm_sums)
+    gain_one, shift_one = lax.fori_loop(wides // 2, wides, back_two, norm_sums)
     go_z(qk[1], (1,))
     go_z_fold(qk[2], (2,))
-    gain_one, shift_one = lax.fori_loop(3 * quarter, chunks, back_two, norm_sums)
 
     def fold8(x):
         return jnp.sum(x, axis=0, keepdims=True)
@@ -1017,6 +1022,7 @@
         v(rows, TILE, dtype=F32),
         v(chunks, TILE, 4 * uw),
         v(nodes + 16, 4 * uw),
+        v(rows, TILE),
         v(rows, 4 * uw),
         v(rows, width, dtype=F32),
         v(rows, width),

time: 81.9 us -> 78.1 us (0.954)
  Pallas kernels: 80.9 us -> 77.2 us
    pallas_call x1, Pallas kernels: 78.5 us -> 74.8 us  [shards(): pl.pallas_call(functools.partial(kernel, nn), out_shape=outs, in_specs=[h...]
where the time goes in v6:
time: 78.1 us; the launch traced here: 78 us
  Pallas kernels  77.2 us (99%)
  between operations  0.82 us (1%)
    pallas_call x1, Pallas kernels, shards(): pl.pallas_call(functools.partial(kernel, nn), out_shape=outs, in_specs=[h...  74.8 us
    pallas_call x1, Pallas kernels, shards(): pl.pallas_call(results_kernel, out_shape=[jax.ShapeDtypeStruct((nodes, wi...  2.37 us

profile of v6, /device:TPU:0, one launch (start us, length us, event | category | flops | bytes accessed | tf_op | source)
XLA Modules:
  0.0 78.0 jit_solution(13488710520803202853)
XLA Ops:
  0.7 74.8 %layer.1 = (bf16[128,512]{1,0:T(8,128)(2,1)S(1)}, bf16[1024,512]{1,0:T(8,128)(2,1)S(1)}, f32[8,512]{1,0:T(8,128)S(1)}, bf16[512,384]{1,0:T(8,128)(2,1)S(1)}, bf1...) custom-call(bf16[1024,512]{1,0:T(8,128)(2,1)} %tok_hbm.1, s32[8,128]{1,0:T(8,128)} %bitcast.2, ...), custom_call_target="tpu_custom_call" | custom-call | tf_op jit(solution)/shard_map/layer/pallas_call | solution.py:1076
  75.5 2.4 %results.1 = (bf16[128,512]{1,0:T(8,128)(2,1)}, bf16[1024,512]{1,0:T(8,128)(2,1)}, f32[512]{0:T(512)}, f32[512]{0:T(512)}, f32[512,128]{1,0:T(8,128)}, /*index=5...) custom-call(bf16[128,512]{1,0:T(8,128)(2,1)S(1)} %get-tuple-element., ...), custom_call_target="tpu_custom_call" | custom-call | tf_op jit(solution)/shard_map/results/pallas_call | solution.py:1105

commit v7 on v6

--- a/solution.py
+++ b/solution.py
@@ -105,6 +105,9 @@
     gtok_ref,
     small_ref,
     fin_in_ref,
+    wide_out_ref,
+    wide_up_ref,
+    wide_dn_ref,
     fin_out_ref,
     fin_up_ref,
     fin_dn_ref,
@@ -192,7 +195,6 @@
     c = n % 2
     plane = (n // 2) % 4
     eighth = 4 * c + plane
-    side = (plane % 2 + plane // 2) % 2
     extra = [b for b in range(3, 12) if (1 << b) < nn]
 
     def node_peer(k):
@@ -240,6 +242,13 @@
         pl.semaphore_signal(barrier, inc=1, device_id=peer, device_id_type=MESH)
     pl.semaphore_wait(barrier, len(greet))
 
+    def plane_of(e):
+        out = plane
+        for b in range(2):
+            if (e >> b) & 1:
+                out = out + (1 << b) * (1 - 2 * ((plane // (1 << b)) % 2))
+        return out
+
     def weight_block(ref, off, size, d0, d1):
         rows = pl.ds(pl.multiple_of(off, 16), size)
         if len(ref.shape) == 3:
@@ -248,7 +257,7 @@
         return ref.at[rows, d0 * w : d1 * w]
 
     class Fetch:
-        def __init__(self, ref, slots, base, halves=False):
+        def __init__(self, ref, slots, base, relay=False):
             total = ref.shape[1] if len(ref.shape) == 3 else ref.shape[0]
             d0, d1 = slots
             sems = iter(range(base, base + 8))
@@ -260,19 +269,21 @@
             def rows(off, size):
                 return weight_block(ref, off, size, d0, d1)
 
-            part = total // 4 if halves else total // 8
-            own = (2 * side + c if halves else eighth) * part
+            part = total // 8
+            own = eighth * part
             self.z = [
                 go(weight_block(ref, own, part, 0, 1), weight_block(ref, own, part, d, d + 1), tp_peer(d))
                 for d in range(d0, d1)
             ]
-            if halves:
-                some = [rows(own + e * (part // 2), part // 2) for e in range(2)]
-                self.plane = [go(x, x, node_peer(2 << e)) for e, x in enumerate(some)]
-                lots = [rows(own, part), rows((2 * (1 - side) + c) * part, part)]
+            self.more = []
+            lots = [rows(c * (total // 2), total // 2)]
+            if relay:
+                self.plane = [go(rows(own, part), rows(own, part), node_peer(2 << e)) for e in range(2)]
+                for e in range(2):
+                    got = rows((4 * c + plane_of(1 << e)) * part + e * (part // 2), part // 2)
+                    self.more.append(go(got, got, node_peer(4 >> e)))
             else:
                 self.plane = [go(rows(own, part), rows(own, part), node_peer(2 * e)) for e in (1, 2, 3)]
-                lots = [rows(c * (total // 2), total // 2)]
             self.core = [go(x, x, node_peer(1)) for x in lots]
 
         def start_z(self):
@@ -285,8 +296,14 @@
             for cp in self.plane:
                 cp.start()
 
+        def start_relay(self):
+            for cp in self.plane:
+                cp.wait()
+            for cp in self.more:
+                cp.start()
+
         def start_core(self):
-            for cp in self.plane:
+            for cp in self.more or self.plane:
                 cp.wait()
             for cp in self.core:
                 cp.start()
@@ -428,29 +445,23 @@
     fetch_ot.start_z()
     fetch_up.start_z()
     fetch_dn.start_z()
-    attend(0, 0, mid)
+    attend(0, 0, steps)
     fetch_ot.start_plane()
     fetch_in[1].start_core()
-    attend(0, mid, steps)
+    fetch_up.start_plane()
     fetch_in[1].end()
     fetch_in[2].start_core()
-    project(1, 0, wides // 2)
-    fetch_up.start_plane()
-    project(1, wides // 2, wides)
-    attend(1, 0, mid)
+    project(1, 0, wides)
     fetch_in[3].start_core()
-    attend(1, mid, steps)
+    attend(1, 0, steps)
+    fetch_dn.start_plane()
     fetch_in[2].end()
-    project(2, 0, wides // 2)
-    fetch_dn.start_plane()
-    project(2, wides // 2, wides)
-    attend(2, 0, mid)
+    project(2, 0, wides)
     fetch_ot.start_core()
-    attend(2, mid, steps)
+    attend(2, 0, steps)
     fetch_in[3].end()
     project(3, 0, wides)
-    attend(3, 0, mid)
-    attend(3, mid, steps)
+    attend(3, 0, steps)
     fetch_ot.end()
 
     def w_out():
@@ -654,13 +665,6 @@
     ]
     every = (1, 2, 3)
 
-    def plane_of(e):
-        out = plane
-        for b in range(2):
-            if (e >> b) & 1:
-                out = out + (1 << b) * (1 - 2 * ((plane // (1 << b)) % 2))
-        return out
-
     def core_copy(g):
         s, r = g.sems(0)
         return remote(g.block(g.rows(1 - c)), g.recv_core, s, r, node_peer(1))
@@ -671,7 +675,7 @@
     def add_core(g):
         core_copy(g).wait()
         mine = g.block(g.rows(c))
-        mine[...] = (mine[...].astype(F32) + g.recv_core[...].astype(F32)).astype(BF16)
+        mine[...] = mine[...] + g.recv_core[...]
 
     def plane_copies(g):
         return [
@@ -723,7 +727,7 @@
         for e in range(2):
             for m, keep in enumerate((plane, plane_of(2 >> e))):
                 mine = cut(g, keep, e)
-                mine[...] = (mine[...].astype(F32) + landing(g, m, e)[...].astype(F32)).astype(BF16)
+                mine[...] = mine[...] + landing(g, m, e)[...]
         for cp in fold_last(g):
             cp.start()
 
@@ -731,7 +735,7 @@
         for cp in fold_last(g):
             cp.wait()
         mine = g.block(g.rows(c, plane))
-        mine[...] = (mine[...].astype(F32) + g.recv_plane[2].astype(F32)).astype(BF16)
+        mine[...] = mine[...] + g.recv_plane[2]
         for cp in z_copies(g, slots):
             cp.start()
 
@@ -919,18 +923,18 @@
     go_last(dn)
     go_last(ot)
     go_last(qk[0])
+    for g, wide in ((dn, wide_dn_ref), (up, wide_up_ref), (ot, wide_out_ref)):
+        finish(g)
+        wide[...] = g.final[...].astype(F32)
     for cp in copies:
         cp.wait()
     small_ref[...] = total_small()
-    finish(dn)
-    finish(up)
-    finish(ot)
     finish(qk[0])
 
 
 def results_kernel(readout, gtok, small, fin_in, fin_out, fin_up, fin_dn, *rest):
     o_read, o_tok, o_g1, o_s1, o_q, o_k, o_v, o_out, o_g2, o_s2, o_up, o_dn, o_hop = rest[:13]
-    v_q, v_k, v_v, v_out, v_up, v_dn, sems = rest[13:]
+    v_q, v_k, v_v, *lines, sems = rest[13:]
     moves = []
 
     def send(src, dst):
@@ -939,19 +943,17 @@
 
     send(gtok, o_tok)
     send(readout, o_read)
-    v_up[...] = fin_up[...].astype(F32)
-    send(v_up, o_up)
-    v_dn[...] = fin_dn[...].astype(F32)
-    send(v_dn, o_dn)
+    send(fin_up, o_up)
+    send(fin_dn, o_dn)
+    send(fin_out, o_out)
     qw = o_q.shape[1]
     for i, (x, o) in enumerate(((v_q, o_q), (v_k, o_k), (v_v, o_v))):
         x[...] = fin_in[:, i * qw : (i + 1) * qw].astype(F32)
         send(x, o)
-    v_out[...] = fin_out[...].astype(F32)
-    send(v_out, o_out)
     width = small.shape[1]
-    for i, o in enumerate((o_g1, o_s1, o_g2, o_s2, o_hop)):
-        o[...] = small[i : i + 1, :].reshape(width)
+    for i, (x, o) in enumerate(zip(lines, (o_g1, o_s1, o_g2, o_s2, o_hop), strict=True)):
+        x[...] = small[i : i + 1, :].reshape(width)
+        send(x, o)
     for cp in moves:
         cp.wait()
 
@@ -988,6 +990,9 @@
     half = width // 2
     more = max(2 * extra, 1)
     scratch = [
+        v(qw, width),
+        v(width, uw),
+        v(uw, width),
         v(tiles, TILE, dtype=jnp.int32),
         v(1, nodes, dtype=jnp.int32),
         v(width),
@@ -1069,9 +1074,9 @@
         pltpu.VMEM((rows, width), BF16),
         pltpu.VMEM((8, width), F32),
         pltpu.VMEM((width, 3 * qw), BF16),
-        pltpu.VMEM((qw, width), BF16),
-        pltpu.VMEM((width, uw), BF16),
-        pltpu.VMEM((uw, width), BF16),
+        pltpu.VMEM((qw, width), F32),
+        pltpu.VMEM((width, uw), F32),
+        pltpu.VMEM((uw, width), F32),
     ]
     readout, gtok, small, fin_in, fin_out, fin_up, fin_dn = pl.pallas_call(
         functools.partial(kernel, nn),
@@ -1080,7 +1085,7 @@
         out_specs=[vm] * 7,
         scratch_shapes=scratch,
         compiler_params=pltpu.CompilerParams(
-            collective_id=0, has_side_effects=True, vmem_limit_bytes=56 * 1024 * 1024
+            collective_id=0, has_side_effects=True, vmem_limit_bytes=54 * 1024 * 1024
         ),
         name="layer",
     )(
@@ -1120,14 +1125,8 @@
             line,
         ],
         in_specs=[vm] * 7,
-        out_specs=[hbm, hbm, vm, vm, hbm, hbm, hbm, hbm, vm, vm, hbm, hbm, vm],
-        scratch_shapes=[v(width, qw, dtype=F32)] * 3
-        + [
-            v(qw, width, dtype=F32),
-            v(width, uw, dtype=F32),
-            v(uw, width, dtype=F32),
-            pltpu.SemaphoreType.DMA((8,)),
-        ],
+        out_specs=[hbm] * 13,
+        scratch_shapes=[v(width, qw, dtype=F32)] * 3 + [v(width, dtype=F32)] * 5 + [pltpu.SemaphoreType.DMA((13,))],
         compiler_params=pltpu.CompilerParams(vmem_limit_bytes=16 * 1024 * 1024),
         name="results",
     )(readout, gtok, small, fin_in, fin_out, fin_up, fin_dn)

time: 78.1 us -> 76.5 us (0.980)
  Pallas kernels: 77.2 us -> 75.5 us
    pallas_call x1, Pallas kernels: 74.8 us -> 73.7 us  [shards(): pl.pallas_call(functools.partial(kernel, nn), out_shape=outs, in_specs=[h...]
where the time goes in v7:
time: 76.5 us; the launch traced here: 76.4 us
  Pallas kernels  75.5 us (99%)
  between operations  0.82 us (1%)
    pallas_call x1, Pallas kernels, shards(): pl.pallas_call(functools.partial(kernel, nn), out_shape=outs, in_specs=[h...  73.7 us
    pallas_call x1, Pallas kernels, shards(): pl.pallas_call(results_kernel, out_shape=[jax.ShapeDtypeStruct((nodes, wi...  1.83 us

profile of v7, /device:TPU:0, one launch (start us, length us, event | category | flops | bytes accessed | tf_op | source)
XLA Modules:
  0.0 76.4 jit_solution(9491760327822572350)
XLA Ops:
  0.7 73.7 %layer.1 = (bf16[128,512]{1,0:T(8,128)(2,1)S(1)}, bf16[1024,512]{1,0:T(8,128)(2,1)S(1)}, f32[8,512]{1,0:T(8,128)S(1)}, bf16[512,384]{1,0:T(8,128)(2,1)S(1)}, f32...) custom-call(bf16[1024,512]{1,0:T(8,128)(2,1)} %tok_hbm.1, s32[8,128]{1,0:T(8,128)} %bitcast.2, ...), custom_call_target="tpu_custom_call" | custom-call | tf_op jit(solution)/shard_map/layer/pallas_call | solution.py:1081
  74.4 1.8 %results.1 = (bf16[128,512]{1,0:T(8,128)(2,1)}, bf16[1024,512]{1,0:T(8,128)(2,1)}, f32[512]{0:T(512)}, f32[512]{0:T(512)}, f32[512,128]{1,0:T(8,128)}, /*index=5...) custom-call(bf16[128,512]{1,0:T(8,128)(2,1)S(1)} %get-tuple-element., ...), custom_call_target="tpu_custom_call" | custom-call | tf_op jit(solution)/shard_map/results/pallas_call | solution.py:1110

commit v8 on v7

--- a/solution.py
+++ b/solution.py
@@ -524,7 +524,7 @@
         both = jnp.where(lane3 < GRAPHS, jnp.where(hop3 == 0, 1.0, weight), -direct)
         return acc + jnp.sum(jnp.where(mine, both, 0.0), axis=0)
 
-    lax.fori_loop(0, wides, feed_norm, 0)
+    lax.fori_loop(0, wides, feed_norm, 0, unroll=True)
     fetch_up.start_core()
     lax.fori_loop(0, wides, feed_up(0, 1), 0)
     fetch_up.end()
@@ -532,7 +532,7 @@
     fetch_dn.start_core()
     lax.fori_loop(wides // 2, wides, feed_up(1, 4), 0)
     fetch_dn.end()
-    sums = lax.fori_loop(0, wides, feed_down, jnp.zeros((HOPS, TILE), F32))
+    sums = lax.fori_loop(0, wides, feed_down, jnp.zeros((HOPS, TILE), F32), unroll=True)
 
     def reduce_all(value, one, by_nodes, by_tp, ssem, rsem, overlap=None):
         one[0] = value
@@ -619,9 +619,9 @@
         return zed_acc
 
     def back_norm(i, carry):
-        gain_acc, shift_acc, hop_acc = carry
+        gain_acc, shift_acc = carry
         r = rows_of(i, WIDE)
-        hop_acc = layer_grads(i, hop_acc)
+        layer_grads(i)
         dy = mm_rt(gbef[r, :], w_up[...])
         hat, inv = centred(res[r, :])
         gain_acc = gain_acc + jnp.sum((dy * hat).reshape(WIDE // HOPS, HOPS, width), axis=0)
@@ -635,9 +635,9 @@
         att = grad_res.astype(BF16)
         datt[r, :] = att
         dctx[r, :] = mm_rt(att, w_out()).astype(BF16)
-        return gain_acc, shift_acc, hop_acc
-
-    def layer_grads(wide, hop_acc):
+        return gain_acc, shift_acc
+
+    def layer_grads(wide):
         for m in range(WIDE // CHUNK):
             i = wide * (WIDE // CHUNK) + m
             r = rows_of(i, CHUNK)
@@ -645,14 +645,16 @@
             dr = cot[rows_of(i, nodes_chunk), :]
             rest = jnp.zeros((TILE - 2 * nodes_chunk - 16, width), BF16)
             gl[r, :] = mm(mix, jnp.concatenate([dr, dr, hop16, rest], axis=0))
-            seen = mm_lt(mix, lay[r, :].astype(BF16))
-            both = seen[0:nodes_chunk] + seen[nodes_chunk : 2 * nodes_chunk]
-            readout_ref[rows_of(i, nodes_chunk), :] = both.astype(BF16)
-            hop_acc = hop_acc + seen[2 * nodes_chunk : 2 * nodes_chunk + 8]
-        return hop_acc
+
+    def readouts(i, hop_acc):
+        r = rows_of(i, CHUNK)
+        seen = mm_lt(mixes[r, :], lay[r, :].astype(BF16))
+        both = seen[0:nodes_chunk] + seen[nodes_chunk : 2 * nodes_chunk]
+        readout_ref[rows_of(i, nodes_chunk), :] = both.astype(BF16)
+        return hop_acc + seen[2 * nodes_chunk : 2 * nodes_chunk + 8]
 
     zero8 = jnp.zeros((HOPS, width), F32)
-    zed_sum = lax.fori_loop(0, chunks, back_one, jnp.zeros((HOPS, zed.shape[1]), F32))
+    zed_sum = lax.fori_loop(0, chunks, back_one, jnp.zeros((HOPS, zed.shape[1]), F32), unroll=True)
 
     def group(at, array, wide, cols, rc, rp, rz, final, more):
         return Group(array, wide, cols, rc, rp, rz, final, more, gsend, grecv, at * (15 + len(extra)))
@@ -829,9 +831,9 @@
     go_core(dn)
     g_up[...] = mm(n2t[...], gbef[...]).astype(BF16)
     go_core(up)
-    norm_sums = lax.fori_loop(0, wides // 2, back_norm, (zero8, zero8, zero8))
+    norm_sums = lax.fori_loop(0, wides // 2, back_norm, (zero8, zero8))
     go_z_first(dn)
-    gain_two, shift_two, hop_sum = lax.fori_loop(wides // 2, wides, back_norm, norm_sums)
+    gain_two, shift_two = lax.fori_loop(wides // 2, wides, back_norm, norm_sums)
     go_fold(up)
     g_out[...] = mm(ctxt[...], datt[...]).astype(BF16).reshape(g_out.shape)
     go_core(ot)
@@ -894,6 +896,7 @@
     go_plane(qk[1])
     go_z_fold(up, every)
     go_fold_last(qk[3])
+    hop_sum = lax.fori_loop(0, chunks, readouts, zero8)
     norm_sums = lax.fori_loop(0, wides // 2, back_two, (zero8, zero8))
     go_plane(qk[0])
     go_z_fold(ot, every)

time: 76.5 us -> 75.9 us (level)
  no operation moved by 1% of the time
where the time goes in v8:
time: 75.9 us; the launch traced here: 75.8 us
  Pallas kernels  74.9 us (99%)
  between operations  0.84 us (1%)
    pallas_call x1, Pallas kernels, shards(): pl.pallas_call(functools.partial(kernel, nn), out_shape=outs, in_specs=[h...  73.1 us
    pallas_call x1, Pallas kernels, shards(): pl.pallas_call(results_kernel, out_shape=[jax.ShapeDtypeStruct((nodes, wi...  1.83 us

profile of v8, /device:TPU:0, one launch (start us, length us, event | category | flops | bytes accessed | tf_op | source)
XLA Modules:
  0.0 75.8 jit_solution(15377249458574163480)
XLA Ops:
  0.7 73.1 %layer.1 = (bf16[128,512]{1,0:T(8,128)(2,1)S(1)}, bf16[1024,512]{1,0:T(8,128)(2,1)S(1)}, f32[8,512]{1,0:T(8,128)S(1)}, bf16[512,384]{1,0:T(8,128)(2,1)S(1)}, f32...) custom-call(bf16[1024,512]{1,0:T(8,128)(2,1)} %tok_hbm.1, s32[8,128]{1,0:T(8,128)} %bitcast.2, ...), custom_call_target="tpu_custom_call" | custom-call | tf_op jit(solution)/shard_map/layer/pallas_call | solution.py:1084
  73.8 1.8 %results.1 = (bf16[128,512]{1,0:T(8,128)(2,1)}, bf16[1024,512]{1,0:T(8,128)(2,1)}, f32[512]{0:T(512)}, f32[512]{0:T(512)}, f32[512,128]{1,0:T(8,128)}, /*index=5...) custom-call(bf16[128,512]{1,0:T(8,128)(2,1)S(1)} %get-tuple-element., ...), custom_call_target="tpu_custom_call" | custom-call | tf_op jit(solution)/shard_map/results/pallas_call | solution.py:1113

commit v9 on v8

--- a/solution.py
+++ b/solution.py
@@ -833,8 +833,8 @@
     go_core(up)
     norm_sums = lax.fori_loop(0, wides // 2, back_norm, (zero8, zero8))
     go_z_first(dn)
+    go_fold(up)
     gain_two, shift_two = lax.fori_loop(wides // 2, wides, back_norm, norm_sums)
-    go_fold(up)
     g_out[...] = mm(ctxt[...], datt[...]).astype(BF16).reshape(g_out.shape)
     go_core(ot)
 

time: 75.9 us -> 75.4 us (level)
  no operation moved by 1% of the time
where the time goes in v9:
time: 75.4 us; the launch traced here: 75.2 us
  Pallas kernels  74.4 us (99%)
  between operations  0.84 us (1%)
    pallas_call x1, Pallas kernels, shards(): pl.pallas_call(functools.partial(kernel, nn), out_shape=outs, in_specs=[h...  72.6 us
    pallas_call x1, Pallas kernels, shards(): pl.pallas_call(results_kernel, out_shape=[jax.ShapeDtypeStruct((nodes, wi...  1.83 us

profile of v9, /device:TPU:0, one launch (start us, length us, event | category | flops | bytes accessed | tf_op | source)
XLA Modules:
  0.0 75.2 jit_solution(1076636130312448929)
XLA Ops:
  0.7 72.6 %layer.1 = (bf16[128,512]{1,0:T(8,128)(2,1)S(1)}, bf16[1024,512]{1,0:T(8,128)(2,1)S(1)}, f32[8,512]{1,0:T(8,128)S(1)}, bf16[512,384]{1,0:T(8,128)(2,1)S(1)}, f32...) custom-call(bf16[1024,512]{1,0:T(8,128)(2,1)} %tok_hbm.1, s32[8,128]{1,0:T(8,128)} %bitcast.2, ...), custom_call_target="tpu_custom_call" | custom-call | tf_op jit(solution)/shard_map/layer/pallas_call | solution.py:1084
  73.2 1.8 %results.1 = (bf16[128,512]{1,0:T(8,128)(2,1)}, bf16[1024,512]{1,0:T(8,128)(2,1)}, f32[512]{0:T(512)}, f32[512]{0:T(512)}, f32[512,128]{1,0:T(8,128)}, /*index=5...) custom-call(bf16[128,512]{1,0:T(8,128)(2,1)S(1)} %get-tuple-element., ...), custom_call_target="tpu_custom_call" | custom-call | tf_op jit(solution)/shard_map/results/pallas_call | solution.py:1113
